TPU v7x, 32 devices: a whole 2x2x4 slice. The times are simulated.
32 devices in a mesh: slab: 8 (over z, x), head: 4 (over y, core).
Axes of the slice: x: 2, y: 2, z: 4, core: 2. Of those that a mesh axis runs over, the one named last changes fastest.
Arguments:
- query_in: bfloat16 [3072, 3072], P(('slab', 'head')), may hold values from -6 to 6
- key_in: bfloat16 [3072, 3072], P(('slab', 'head')), may hold values from -6 to 6
- value_in: bfloat16 [3072, 3072], P(('slab', 'head')), may hold values from -6 to 6
- grad_out: bfloat16 [3072, 3072], P(('slab', 'head')), may hold values from -6 to 6
- neighbours: int32 [48, 16], P('slab'), may hold values from -1 to 47, as said below
Outputs:
- attended: bfloat16 [3072, 3072], P(('slab', 'head'))
- grad_query: bfloat16 [3072, 3072], P(('slab', 'head'))
- grad_key: bfloat16 [3072, 3072], P(('slab', 'head'))
- grad_value: bfloat16 [3072, 3072], P(('slab', 'head'))
Inputs may be any that keep to these rules, and one draw needn't show every extreme that they name: `neighbours`: slab s is tiles s * 6 to (s + 1) * 6 - 1. Row t names distinct key tiles, all in the slab of tile t or in the slabs directly before and after it; its first entry is t itself; -1 marks an unused slot, which names no tile.
All inputs are finite; a program needn't handle non-finite values.
Results may differ from a plain program's by a relative error of at most 0.018.
Values may be sent and summed in bfloat16 or wider, within the bound.
No kernel may reach another device: no remote copies, remote signals or barrier semaphores. Data moves between devices by JAX's collectives and lax.ppermute only.
A program may use at most 64 MiB of HBM per device.

v0:
```python
import math

import jax
import jax.numpy as jnp
from jax import lax
from jax.sharding import PartitionSpec as P

HD = 128
TILE = 64


def shifted(shard, axis, by):
    peers = lax.axis_size(axis)
    pairs = [(i, i + by) for i in range(peers) if 0 <= i + by < peers]
    return lax.ppermute(shard, axis, pairs)


def window_mask(id_rows, first_tile, key_count):
    tiles_key = key_count // TILE
    tile_ids = first_tile + jnp.arange(tiles_key, dtype=jnp.int32)
    listed = jnp.any(
        (id_rows[:, :, None] == tile_ids[None, None, :]) & (id_rows[:, :, None] >= 0), axis=1
    )
    tile_count = id_rows.shape[0]
    spread = jnp.broadcast_to(listed[:, None, :, None], (tile_count, TILE, tiles_key, TILE))
    return spread.reshape(tile_count * TILE, key_count)


def attend_tile(query_tile, grad_tile, id_row, key_win, val_win, first_tile):
    score_scale = 1.0 / math.sqrt(HD)
    head_count = query_tile.shape[1] // HD
    query_heads = query_tile.reshape(-1, head_count, HD)
    grad_heads = grad_tile.reshape(-1, head_count, HD)
    key_heads = key_win.reshape(-1, head_count, HD)
    val_heads = val_win.reshape(-1, head_count, HD)
    allowed = window_mask(id_row[None, :], first_tile, key_win.shape[0])[None]
    scores = (
        jnp.einsum("qhd,khd->hqk", query_heads, key_heads, preferred_element_type=jnp.float32)
        * score_scale
    )
    scores = jnp.where(allowed, scores, -1e30)
    row_peak = jnp.max(scores, axis=2, keepdims=True)
    log_total = row_peak + jnp.log(jnp.sum(jnp.exp(scores - row_peak), axis=2, keepdims=True))
    weights = jnp.where(allowed, jnp.exp(scores - log_total), 0.0)
    weights_low = weights.astype(jnp.bfloat16)
    out_heads = jnp.einsum(
        "hqk,khd->qhd", weights_low, val_heads, preferred_element_type=jnp.float32
    ).astype(jnp.bfloat16)
    out_dot = jnp.sum(grad_heads.astype(jnp.float32) * out_heads.astype(jnp.float32), axis=2)
    dweights = jnp.einsum("qhd,khd->hqk", grad_heads, val_heads, preferred_element_type=jnp.float32)
    dscores = (weights * (dweights - out_dot.T[:, :, None])).astype(jnp.bfloat16)
    dq_heads = (
        jnp.einsum("hqk,khd->qhd", dscores, key_heads, preferred_element_type=jnp.float32)
        * score_scale
    ).astype(jnp.bfloat16)
    return (
        out_heads.reshape(query_tile.shape),
        dq_heads.reshape(query_tile.shape),
        log_total[:, :, 0].T,
        out_dot,
        weights_low,
        dscores,
    )


def per_device(query_in, key_in, value_in, grad_out, neighbours):
    score_scale = 1.0 / math.sqrt(HD)
    local_query, local_key, local_value, local_grad = (
        lax.all_to_all(query_in, "head", split_axis=1, concat_axis=0, tiled=True),
        lax.all_to_all(key_in, "head", split_axis=1, concat_axis=0, tiled=True),
        lax.all_to_all(value_in, "head", split_axis=1, concat_axis=0, tiled=True),
        lax.all_to_all(grad_out, "head", split_axis=1, concat_axis=0, tiled=True),
    )
    slab_rows = local_query.shape[0]
    width_local = local_query.shape[1]
    head_count = width_local // HD
    slab_tiles = neighbours.shape[0]
    own_first = lax.axis_index("slab") * slab_tiles
    joined = jnp.concatenate([local_key, local_value], axis=1)
    beside = {}
    for offset in (1, -1):
        beside[offset] = shifted(joined, "slab", offset)
    window = jnp.concatenate([beside[1], joined, beside[-1]], axis=0)
    key_win = window[:, :width_local]
    val_win = window[:, width_local:]
    first_tile = own_first - slab_tiles
    query_tiles = local_query.reshape(slab_tiles, TILE, width_local)
    grad_tiles = local_grad.reshape(slab_tiles, TILE, width_local)

    def per_tile(pieces):
        return attend_tile(pieces[0], pieces[1], pieces[2], key_win, val_win, first_tile)

    out_tiles, dq_tiles, lse_tiles, dot_tiles, weight_tiles, dscore_tiles = lax.map(
        per_tile, (query_tiles, grad_tiles, neighbours)
    )
    attended = out_tiles.reshape(slab_rows, width_local)
    grad_query = dq_tiles.reshape(slab_rows, width_local)
    query_four = local_query.reshape(slab_tiles, TILE, head_count, HD)
    grad_four = local_grad.reshape(slab_tiles, TILE, head_count, HD)

    def window_grads(low_row, high_row):
        key_part = (
            jnp.einsum(
                "jhqk,jqhd->khd",
                dscore_tiles[..., low_row:high_row],
                query_four,
                preferred_element_type=jnp.float32,
            )
            * score_scale
        )
        value_part = jnp.einsum(
            "jhqk,jqhd->khd",
            weight_tiles[..., low_row:high_row],
            grad_four,
            preferred_element_type=jnp.float32,
        )
        return jnp.concatenate(
            [
                key_part.reshape(high_row - low_row, width_local),
                value_part.reshape(high_row - low_row, width_local),
            ],
            axis=1,
        )

    outgoing = {1: window_grads(2 * slab_rows, 3 * slab_rows), -1: window_grads(0, slab_rows)}
    arrived = {}
    for offset in (1, -1):
        arrived[offset] = shifted(outgoing[offset].astype(jnp.bfloat16), "slab", offset).astype(
            jnp.float32
        )
    own_part = window_grads(slab_rows, 2 * slab_rows)
    grad_sum = own_part + arrived[1] + arrived[-1]
    grad_key = grad_sum[:, :width_local].astype(jnp.bfloat16)
    grad_value = grad_sum[:, width_local:].astype(jnp.bfloat16)
    return (
        lax.all_to_all(attended, "head", split_axis=0, concat_axis=1, tiled=True),
        lax.all_to_all(grad_query, "head", split_axis=0, concat_axis=1, tiled=True),
        lax.all_to_all(grad_key, "head", split_axis=0, concat_axis=1, tiled=True),
        lax.all_to_all(grad_value, "head", split_axis=0, concat_axis=1, tiled=True),
    )


def solution(mesh):
    in_specs = (
        P(("slab", "head"), None),
        P(("slab", "head"), None),
        P(("slab", "head"), None),
        P(("slab", "head"), None),
        P("slab", None),
    )
    out_specs = (
        P(("slab", "head"), None),
        P(("slab", "head"), None),
        P(("slab", "head"), None),
        P(("slab", "head"), None),
    )
    return jax.shard_map(
        per_device, mesh=mesh, in_specs=in_specs, out_specs=out_specs, check_vma=False
    )
```

profile of v0, /device:TPU:0, one launch (start us, length us, event | category | flops | bytes accessed | tf_op | source)
XLA Modules:
  0.0 316.7 jit_solution(93680851770151180)
XLA Ops:
  2.6 4.2 %all-to-all-start.1 = ((bf16[96,4,768]{2,0,1:T(8,128)(2,1)}), bf16[96,4,768]{2,0,1:T(8,128)(2,1)S(1)}, u32[]{:S(2)}, u32[]{:S(2)}) async-start(bf16[96,4,768]{2,0,1:T(8,128)(2,1)} %bitcast.115), calls=%async_computation.1 | async-start | bytes 1179648 | tf_op jit(solution)/shard_map/all_to_all | solution.py:70
  6.9 9.5 %all-to-all-done.1 = bf16[96,4,768]{2,0,1:T(8,128)(2,1)S(1)} async-done(((bf16[96,4,768]{2,0,1:T(8,128)(2,1)}), bf16[96,4,768]{2,0,1:T(8,128)(2,1)S(1)}, u32[]{:S(2)}, u32[]{:S(2)}) %all-to-all-start.1) | async-done | bytes 589856 | tf_op jit(solution)/shard_map/all_to_all | solution.py:70
  16.4 12.1 %all_to_all.146 = bf16[96,4,768]{2,0,1:T(8,128)(2,1)S(1)} all-to-all(bf16[96,4,768]{2,0,1:T(8,128)(2,1)S(1)} %bitcast.155), channel_id=1, replica_groups=mesh['slab'=8,'head'=4] {'head'}, dimensions={1} | all-to-all | bytes 1179648 | tf_op jit(solution)/shard_map/all_to_all | solution.py:71
  29.6 4.1 %collective-permute-start = (bf16[384,1536]{1,0:T(8,128)(2,1)}, bf16[384,1536]{1,0:T(8,128)(2,1)S(1)}, u32[]{:S(2)}, u32[]{:S(2)}) collective-permute-start(bf16[384,1536]{1,0:T(8,128)(2,1)} %pad_maximum_fusion.1), channel_id=1, source_target_pairs={{0,4},{4,8},{8,12},{12,16},{16,20},{20,24},{24,28},{1,5},{5,9},{9,... | collective-permute-start | bytes 3538952 | tf_op jit(solution)/shard_map/ppermute | solution.py:15
  35.9 3.5 %all-to-all-start = ((bf16[96,4,768]{2,0,1:T(8,128)(2,1)}), bf16[96,4,768]{2,0,1:T(8,128)(2,1)S(1)}, u32[]{:S(2)}, u32[]{:S(2)}) async-start(bf16[96,4,768]{2,0,1:T(8,128)(2,1)} %bitcast.116), calls=%async_computation | async-start | bytes 1179648 | tf_op jit(solution)/shard_map/all_to_all | solution.py:69
  41.3 7.6 %all-to-all-done = bf16[96,4,768]{2,0,1:T(8,128)(2,1)S(1)} async-done(((bf16[96,4,768]{2,0,1:T(8,128)(2,1)}), bf16[96,4,768]{2,0,1:T(8,128)(2,1)S(1)}, u32[]{:S(2)}, u32[]{:S(2)}) %all-to-all-start) | async-done | bytes 589856 | tf_op jit(solution)/shard_map/all_to_all | solution.py:69
  48.9 3.5 %all-to-all-start.3 = ((bf16[96,4,768]{2,0,1:T(8,128)(2,1)}), bf16[96,4,768]{2,0,1:T(8,128)(2,1)S(1)}, u32[]{:S(2)}, u32[]{:S(2)}) async-start(bf16[96,4,768]{2,0,1:T(8,128)(2,1)} %bitcast.113), calls=%async_computation.3 | async-start | bytes 1179648 | tf_op jit(solution)/shard_map/all_to_all | solution.py:72
  53.9 7.9 %all-to-all-done.3 = bf16[96,4,768]{2,0,1:T(8,128)(2,1)S(1)} async-done(((bf16[96,4,768]{2,0,1:T(8,128)(2,1)}), bf16[96,4,768]{2,0,1:T(8,128)(2,1)S(1)}, u32[]{:S(2)}, u32[]{:S(2)}) %all-to-all-start.3) | async-done | bytes 589856 | tf_op jit(solution)/shard_map/all_to_all | solution.py:72
  63.4 20.9 %collective-permute-done = bf16[384,1536]{1,0:T(8,128)(2,1)S(1)} collective-permute-done((bf16[384,1536]{1,0:T(8,128)(2,1)}, bf16[384,1536]{1,0:T(8,128)(2,1)S(1)}, u32[]{:S(2)}, u32[]{:S(2)}) %collective-permute-start) | collective-permute-done | bytes 1179680 | tf_op jit(solution)/shard_map/ppermute | solution.py:15
  92.8 130.1 %while.16 = (s32[]{:T(128)}, bf16[6,64,768]{2,1,0:T(8,128)(2,1)}, bf16[6,64,768]{2,1,0:T(8,128)(2,1)}, bf16[6,6,64,1152]{3,2,0,1:T(8,128)(2,1)}, bf16[6,6,64,115...) while((s32[]{:T(128)}, bf16[6,64,768]{2,1,0:T(8,128)(2,1)}, ...), condition=%wide.region_5.6_spmd, body=%wide.region_0.5_spmd.sunk | while | flops 460406912 | bytes 29419984 | solution.py:93
  100.5 3.1 multiply_reduce_fusion.2
  122.2 3.1 multiply_reduce_fusion.2
  143.9 3.1 multiply_reduce_fusion.2
  165.6 3.1 multiply_reduce_fusion.2
  187.2 3.1 multiply_reduce_fusion.2
  208.9 3.1 multiply_reduce_fusion.2
  233.9 5.3 %collective-permute-start.2 = (bf16[384,1536]{1,0:T(8,128)(2,1)}, bf16[384,1536]{1,0:T(8,128)(2,1)}, u32[]{:S(2)}, u32[]{:S(2)}) collective-permute-start(bf16[384,1536]{1,0:T(8,128)(2,1)} %pad_maximum_fusion.2), channel_id=1, source_target_pairs={{0,4},{4,8},{8,12},{12,16},{16,20},{20,24},{24,28},{1,5},{5,9},{9,... | collective-permute-start | bytes 3538952 | tf_op jit(solution)/shard_map/ppermute | solution.py:15
  244.2 4.4 %all-to-all-start.4 = ((bf16[4,96,768]{2,1,0:T(8,128)(2,1)}), bf16[4,96,768]{2,1,0:T(8,128)(2,1)}, u32[]{:S(2)}, u32[]{:S(2)}) async-start(bf16[4,96,768]{2,1,0:T(8,128)(2,1)} %bitcast.162), calls=%async_computation.4 | async-start | bytes 1179648 | tf_op jit(solution)/shard_map/all_to_all | solution.py:136
  253.5 4.5 %all-to-all-done.4 = bf16[4,96,768]{2,1,0:T(8,128)(2,1)} async-done(((bf16[4,96,768]{2,1,0:T(8,128)(2,1)}), bf16[4,96,768]{2,1,0:T(8,128)(2,1)}, u32[]{:S(2)}, u32[]{:S(2)}) %all-to-all-start.4) | async-done | bytes 589856 | tf_op jit(solution)/shard_map/all_to_all | solution.py:136
  258.0 3.5 %all-to-all-start.5 = ((bf16[4,96,768]{2,1,0:T(8,128)(2,1)}), bf16[4,96,768]{2,1,0:T(8,128)(2,1)S(1)}, u32[]{:S(2)}, u32[]{:S(2)}) async-start(bf16[4,96,768]{2,1,0:T(8,128)(2,1)} %bitcast.163), calls=%async_computation.5 | async-start | bytes 1179648 | tf_op jit(solution)/shard_map/all_to_all | solution.py:137
  261.5 26.5 %collective-permute-done.2 = bf16[384,1536]{1,0:T(8,128)(2,1)} collective-permute-done((bf16[384,1536]{1,0:T(8,128)(2,1)}, bf16[384,1536]{1,0:T(8,128)(2,1)}, u32[]{:S(2)}, u32[]{:S(2)}) %collective-permute-start.2) | collective-permute-done | bytes 1179680 | tf_op jit(solution)/shard_map/ppermute | solution.py:15
  290.9 11.9 %all_to_all.147 = bf16[4,96,768]{2,1,0:T(8,128)(2,1)S(1)} all-to-all(bf16[4,96,768]{2,1,0:T(8,128)(2,1)S(1)} %bitcast.156), channel_id=1, replica_groups=mesh['slab'=8,'head'=4] {'head'}, dimensions={0} | all-to-all | bytes 1179648 | tf_op jit(solution)/shard_map/all_to_all | solution.py:138
  302.9 3.5 %all-to-all-start.7 = ((bf16[4,96,768]{2,1,0:T(8,128)(2,1)}), bf16[4,96,768]{2,1,0:T(8,128)(2,1)S(1)}, u32[]{:S(2)}, u32[]{:S(2)}) async-start(bf16[4,96,768]{2,1,0:T(8,128)(2,1)} %bitcast.46), calls=%async_computation.7 | async-start | bytes 1179648 | tf_op jit(solution)/shard_map/all_to_all | solution.py:139
  310.0 5.8 %all-to-all-done.7 = bf16[4,96,768]{2,1,0:T(8,128)(2,1)S(1)} async-done(((bf16[4,96,768]{2,1,0:T(8,128)(2,1)}), bf16[4,96,768]{2,1,0:T(8,128)(2,1)S(1)}, u32[]{:S(2)}, u32[]{:S(2)}) %all-to-all-start.7) | async-done | bytes 589856 | tf_op jit(solution)/shard_map/all_to_all | solution.py:139
  (198 shorter events, 158.5 us)
Async XLA Ops:
  0.6 6.2 %copy-start.7 = (bf16[96,3072]{1,0:T(8,128)(2,1)S(1)}, bf16[96,3072]{1,0:T(8,128)(2,1)}, u32[]{:S(2)}) copy-start(bf16[96,3072]{1,0:T(8,128)(2,1)} %param.9) | copy-start | bytes 1769476
  2.6 13.8 %all-to-all-start.1 = ((bf16[96,4,768]{2,0,1:T(8,128)(2,1)}), bf16[96,4,768]{2,0,1:T(8,128)(2,1)S(1)}, u32[]{:S(2)}, u32[]{:S(2)}) async-start(bf16[96,4,768]{2,0,1:T(8,128)(2,1)} %bitcast.115), calls=%async_computation.1 | async-start | bytes 1179648 | tf_op jit(solution)/shard_map/all_to_all | solution.py:70
  16.4 18.6 %copy-start.8 = (bf16[96,3072]{1,0:T(8,128)(2,1)S(1)}, bf16[96,3072]{1,0:T(8,128)(2,1)}, u32[]{:S(2)}) copy-start(bf16[96,3072]{1,0:T(8,128)(2,1)} %param.7) | copy-start | bytes 1769476
  29.6 54.8 %collective-permute-start = (bf16[384,1536]{1,0:T(8,128)(2,1)}, bf16[384,1536]{1,0:T(8,128)(2,1)S(1)}, u32[]{:S(2)}, u32[]{:S(2)}) collective-permute-start(bf16[384,1536]{1,0:T(8,128)(2,1)} %pad_maximum_fusion.1), channel_id=1, source_target_pairs={{0,4},{4,8},{8,12},{12,16},{16,20},{20,24},{24,28},{1,5},{5,9},{9,... | collective-permute-start | bytes 3538952 | tf_op jit(solution)/shard_map/ppermute | solution.py:15
  33.7 50.7 %collective-permute-start.1 = (bf16[384,1536]{1,0:T(8,128)(2,1)}, bf16[384,1536]{1,0:T(8,128)(2,1)}, u32[]{:S(2)}, u32[]{:S(2)}) collective-permute-start(bf16[384,1536]{1,0:T(8,128)(2,1)} %pad_maximum_fusion.1), channel_id=1, source_target_pairs={{4,0},{8,4},{12,8},{16,12},{20,16},{24,20},{28,24},{5,1},{9,5},{13... | collective-permute-start | bytes 3538952 | tf_op jit(solution)/shard_map/ppermute | solution.py:15
  35.9 13.0 %all-to-all-start = ((bf16[96,4,768]{2,0,1:T(8,128)(2,1)}), bf16[96,4,768]{2,0,1:T(8,128)(2,1)S(1)}, u32[]{:S(2)}, u32[]{:S(2)}) async-start(bf16[96,4,768]{2,0,1:T(8,128)(2,1)} %bitcast.116), calls=%async_computation | async-start | bytes 1179648 | tf_op jit(solution)/shard_map/all_to_all | solution.py:69
  48.9 14.6 %copy-start.2 = (bf16[96,4,768]{2,0,1:T(8,128)(2,1)}, bf16[96,4,768]{2,0,1:T(8,128)(2,1)S(1)}, u32[]{:S(2)}) copy-start(bf16[96,4,768]{2,0,1:T(8,128)(2,1)S(1)} %all-to-all-done) | copy-start | bytes 1769476
  48.9 13.0 %all-to-all-start.3 = ((bf16[96,4,768]{2,0,1:T(8,128)(2,1)}), bf16[96,4,768]{2,0,1:T(8,128)(2,1)S(1)}, u32[]{:S(2)}, u32[]{:S(2)}) async-start(bf16[96,4,768]{2,0,1:T(8,128)(2,1)} %bitcast.113), calls=%async_computation.3 | async-start | bytes 1179648 | tf_op jit(solution)/shard_map/all_to_all | solution.py:72
  61.9 22.5 %copy-start.3 = (bf16[96,4,768]{2,0,1:T(8,128)(2,1)}, bf16[96,4,768]{2,0,1:T(8,128)(2,1)S(1)}, u32[]{:S(2)}) copy-start(bf16[96,4,768]{2,0,1:T(8,128)(2,1)S(1)} %all-to-all-done.3) | copy-start | bytes 1769476
  100.5 3.1 copy-start.1
  122.2 3.1 copy-start
  122.2 3.1 copy-start.1
  165.6 3.1 copy-start
  165.6 3.1 copy-start.1
  187.2 3.1 copy-start
  187.2 3.1 copy-start.1
  208.9 3.1 copy-start
  208.9 3.1 copy-start.1
  222.9 5.5 %copy-start.6 = (bf16[6,6,64,1152]{3,2,0,1:T(8,128)(2,1)S(1)}, bf16[6,6,64,1152]{3,2,0,1:T(8,128)(2,1)}, u32[]{:S(2)}) copy-start(bf16[6,6,64,1152]{3,2,0,1:T(8,128)(2,1)} %get-tuple-element.67) | copy-start | bytes 15925252
  233.9 54.1 %collective-permute-start.2 = (bf16[384,1536]{1,0:T(8,128)(2,1)}, bf16[384,1536]{1,0:T(8,128)(2,1)}, u32[]{:S(2)}, u32[]{:S(2)}) collective-permute-start(bf16[384,1536]{1,0:T(8,128)(2,1)} %pad_maximum_fusion.2), channel_id=1, source_target_pairs={{0,4},{4,8},{8,12},{12,16},{16,20},{20,24},{24,28},{1,5},{5,9},{9,... | collective-permute-start | bytes 3538952 | tf_op jit(solution)/shard_map/ppermute | solution.py:15
  242.9 45.1 %collective-permute-start.3 = (bf16[384,1536]{1,0:T(8,128)(2,1)}, bf16[384,1536]{1,0:T(8,128)(2,1)}, u32[]{:S(2)}, u32[]{:S(2)}) collective-permute-start(bf16[384,1536]{1,0:T(8,128)(2,1)} %pad_maximum_fusion.3), channel_id=1, source_target_pairs={{4,0},{8,4},{12,8},{16,12},{20,16},{24,20},{28,24},{5,1},{9,5},{13... | collective-permute-start | bytes 3538952 | tf_op jit(solution)/shard_map/ppermute | solution.py:15
  244.2 13.8 %all-to-all-start.4 = ((bf16[4,96,768]{2,1,0:T(8,128)(2,1)}), bf16[4,96,768]{2,1,0:T(8,128)(2,1)}, u32[]{:S(2)}, u32[]{:S(2)}) async-start(bf16[4,96,768]{2,1,0:T(8,128)(2,1)} %bitcast.162), calls=%async_computation.4 | async-start | bytes 1179648 | tf_op jit(solution)/shard_map/all_to_all | solution.py:136
  258.0 32.9 %all-to-all-start.5 = ((bf16[4,96,768]{2,1,0:T(8,128)(2,1)}), bf16[4,96,768]{2,1,0:T(8,128)(2,1)S(1)}, u32[]{:S(2)}, u32[]{:S(2)}) async-start(bf16[4,96,768]{2,1,0:T(8,128)(2,1)} %bitcast.163), calls=%async_computation.5 | async-start | bytes 1179648 | tf_op jit(solution)/shard_map/all_to_all | solution.py:137
  302.9 13.0 %all-to-all-start.7 = ((bf16[4,96,768]{2,1,0:T(8,128)(2,1)}), bf16[4,96,768]{2,1,0:T(8,128)(2,1)S(1)}, u32[]{:S(2)}, u32[]{:S(2)}) async-start(bf16[4,96,768]{2,1,0:T(8,128)(2,1)} %bitcast.46), calls=%async_computation.7 | async-start | bytes 1179648 | tf_op jit(solution)/shard_map/all_to_all | solution.py:139
  (5 other events, 14.7 us)
where the time goes:
time: 322 us; the launch traced here: 317 us
  local copies, waits for them, and re-layouts  98.8 us (31%)
  waiting for transfers between devices  82.8 us (26%)
  matrix products  53.6 us (17%)
  starting transfers between devices  34.5 us (11%)
  blocking collectives  24 us (7%)
  other arithmetic  22 us (7%)
    ppermute x4, waiting for transfers between devices, shifted(): return lax.ppermute(shard, axis, pairs)  47.5 us
    broadcast_in_dim x12, local copies, waits for them, and re-layouts, per_device(): lax.map(per_tile, (query_tiles, grad_tiles, neighbours))  20 us
    dot_general x6, matrix products, attend_tile(): jnp.einsum('hqk,khd->qhd', weights_low, val_heads, preferred_element_type...  18.4 us
    dynamic_slice x12, local copies, waits for them, and re-layouts, per_device(): lax.map(per_tile, (query_tiles, grad_tiles, neighbours))  14.6 us
    all_to_all x1, blocking collectives, per_device(): lax.all_to_all(value_in, 'head', split_axis=1, concat_axis=0, tiled=True)  12.1 us
    ppermute x4, starting transfers between devices, shifted(): return lax.ppermute(shard, axis, pairs)  12 us
    all_to_all x1, blocking collectives, per_device(): lax.all_to_all(grad_key, 'head', split_axis=0, concat_axis=1, tiled=True)  11.9 us
    reshape x6, local copies, waits for them, and re-layouts, attend_tile(): grad_heads = grad_tile.reshape(-1, head_count, HD)  10 us
  transfers between devices with their start and end apart: 10, of which 7 were waited for; matrix products, arithmetic and copies ran while one was open for 7% of the time, Pallas kernels for 0%

commit v1 on v0

v1 whole, which is shorter than its diff:
```python
import functools
import math

import jax
import jax.numpy as jnp
from jax import lax
from jax.experimental import pallas as pl
from jax.experimental.pallas import tpu as pltpu
from jax.sharding import Mesh
from jax.sharding import PartitionSpec as P

HD = 128
TILE = 64
PAIR = 2
MASKED = -1e30


def window_bias(id_rows, first_tile, key_tiles):
    tile_ids = first_tile + jnp.arange(key_tiles, dtype=jnp.int32)
    listed = jnp.any(
        (id_rows[:, :, None] == tile_ids[None, None, :]) & (id_rows[:, :, None] >= 0), axis=1
    )
    bias = jnp.where(listed, 0.0, MASKED).astype(jnp.float32)
    return jnp.repeat(bias, TILE, axis=1)


def attend_kernel(bias_ref, qg_ref, kv_ref, before_ref, after_ref, oq_ref, own_ref, back_ref, ahead_ref):
    scale = 1.0 / math.sqrt(HD)
    log2_scale = scale * math.log2(math.e)
    blocks, _, rows, _ = qg_ref.shape
    half = blocks // 2
    slab = half * rows
    tiles = slab // TILE

    def flat(ref, low, high, which):
        return ref[low:high, which].reshape((high - low) * rows, HD)

    keys = [flat(before_ref, 0, half, 0), flat(kv_ref, 0, half, 0), flat(kv_ref, half, blocks, 0), flat(after_ref, 0, half, 0)]
    vals = [flat(before_ref, 0, half, 1), flat(kv_ref, 0, half, 1), flat(kv_ref, half, blocks, 1), flat(after_ref, 0, half, 1)]
    key_grads = [None] * 4
    val_grads = [None] * 4
    nt = (((1,), (1,)), ((), ()))
    nn = (((1,), (0,)), ((), ()))
    tn = (((0,), (0,)), ((), ()))
    dot = functools.partial(lax.dot_general, preferred_element_type=jnp.float32)
    for part in range(2):
        query = flat(qg_ref, part * half, (part + 1) * half, 0)
        grad = flat(qg_ref, part * half, (part + 1) * half, 1)
        key_win = jnp.concatenate(keys[part : part + 3], axis=0)
        val_win = jnp.concatenate(vals[part : part + 3], axis=0)
        bias = bias_ref[part * tiles : (part + 1) * tiles]
        bias = jnp.broadcast_to(bias[:, None, :], (tiles, TILE, bias.shape[1])).reshape(slab, bias.shape[1])
        scores = dot(query, key_win, nt) + bias
        peak = jnp.max(scores, axis=1, keepdims=True)
        weights = jnp.exp2((scores - peak) * log2_scale)
        weights = weights * (1.0 / jnp.sum(weights, axis=1, keepdims=True))
        weights_low = weights.astype(jnp.bfloat16)
        out = dot(weights_low, val_win, nn).astype(jnp.bfloat16)
        out_dot = jnp.sum(grad.astype(jnp.float32) * out.astype(jnp.float32), axis=1, keepdims=True)
        dweights = dot(grad, val_win, nt)
        dscores = (weights * (dweights - out_dot)).astype(jnp.bfloat16)
        dquery = (dot(dscores, key_win, nn) * scale).astype(jnp.bfloat16)
        oq_ref[part * half : (part + 1) * half, 0] = out.reshape(half, rows, HD)
        oq_ref[part * half : (part + 1) * half, 1] = dquery.reshape(half, rows, HD)
        dkey = dot(dscores, query, tn) * scale
        dval = dot(weights_low, grad, tn)
        for third in range(3):
            at = part + third
            dk = dkey[third * slab : (third + 1) * slab]
            dv = dval[third * slab : (third + 1) * slab]
            key_grads[at] = dk if key_grads[at] is None else key_grads[at] + dk
            val_grads[at] = dv if val_grads[at] is None else val_grads[at] + dv
    for which, grads in enumerate((key_grads, val_grads)):
        back_ref[:, which] = grads[0].reshape(half, rows, HD).astype(jnp.bfloat16)
        own_ref[:half, which] = grads[1].reshape(half, rows, HD)
        own_ref[half:, which] = grads[2].reshape(half, rows, HD)
        ahead_ref[:, which] = grads[3].reshape(half, rows, HD).astype(jnp.bfloat16)


def attend(bias, qg, kv, before, after):
    blocks, _, rows, width = qg.shape
    half = blocks // 2

    def spec(count):
        return pl.BlockSpec((count, 2, rows, HD), lambda h: (0, 0, 0, h))

    def shape(count, dtype):
        return jax.ShapeDtypeStruct((count, 2, rows, width), dtype)

    pairs = bias.shape[0] * TILE * bias.shape[1] * (width // HD)
    return pl.pallas_call(
        attend_kernel,
        grid=(width // HD,),
        in_specs=[pl.BlockSpec(bias.shape, lambda h: (0, 0)), spec(blocks), spec(blocks), spec(half), spec(half)],
        out_specs=[spec(blocks), spec(blocks), spec(half), spec(half)],
        out_shape=[shape(blocks, jnp.bfloat16), shape(blocks, jnp.float32), shape(half, jnp.bfloat16), shape(half, jnp.bfloat16)],
        compiler_params=pltpu.CompilerParams(vmem_limit_bytes=48 * 1024 * 1024),
        cost_estimate=pl.CostEstimate(flops=12 * pairs * HD, bytes_accessed=16 * 2**20, transcendentals=pairs),
    )(bias, qg, kv, before, after)


def per_device(query_in, key_in, value_in, grad_out, neighbours):
    plane = ("pair", "head")
    peers = lax.axis_size(plane)
    groups = lax.axis_size("group")
    rows, full_width = query_in.shape
    slab_tiles = neighbours.shape[0]
    half = peers // PAIR

    def outgoing(first, second):
        joined = jnp.stack([first.reshape(rows, peers, -1), second.reshape(rows, peers, -1)], axis=0)
        return jnp.transpose(joined, (2, 0, 1, 3))

    def incoming(joined):
        first, second = joined[:, 0], joined[:, 1]
        return (
            jnp.transpose(first, (1, 0, 2)).reshape(rows, full_width),
            jnp.transpose(second, (1, 0, 2)).reshape(rows, full_width),
        )

    up = [(i, i + 1) for i in range(groups - 1)]
    down = [(i + 1, i) for i in range(groups - 1)]
    slab = lax.axis_index("group") * PAIR + lax.axis_index("pair")
    bias = window_bias(neighbours, (slab - 1) * slab_tiles, 3 * slab_tiles)
    other = lax.ppermute(bias, "pair", [(0, 1), (1, 0)])
    first = lax.axis_index("pair") == 0
    bias = jnp.concatenate([jnp.where(first, bias, other), jnp.where(first, other, bias)], axis=0)
    kv = lax.all_to_all(outgoing(key_in, value_in), plane, 0, 0, tiled=True)
    before = lax.ppermute(kv[half:], "group", up)
    after = lax.ppermute(kv[:half], "group", down)
    qg = lax.all_to_all(outgoing(query_in, grad_out), plane, 0, 0, tiled=True)
    oq, own, back, ahead = attend(bias, qg, kv, before, after)
    from_before = lax.ppermute(ahead, "group", up)
    from_after = lax.ppermute(back, "group", down)
    attended, grad_query = incoming(lax.all_to_all(oq, plane, 0, 0, tiled=True))
    arrived = jnp.concatenate([from_before, from_after], axis=0).astype(jnp.float32)
    grads = (own + arrived).astype(jnp.bfloat16)
    grad_key, grad_value = incoming(lax.all_to_all(grads, plane, 0, 0, tiled=True))
    return attended, grad_query, grad_key, grad_value


def solution(mesh):
    slabs, heads = mesh.devices.shape
    paired = Mesh(mesh.devices.reshape(slabs // PAIR, PAIR, heads), ("group", "pair", "head"))
    tokens = P(("group", "pair", "head"), None)
    return jax.shard_map(
        per_device,
        mesh=paired,
        in_specs=(tokens, tokens, tokens, tokens, P(("group", "pair"), None)),
        out_specs=(tokens, tokens, tokens, tokens),
        check_vma=False,
    )
```

time: 322 us -> 117 us (0.36); the launches traced: 317 us -> 116 us
  local copies, waits for them, and re-layouts: 98.8 us -> 9.9 us
  matrix products: 53.6 us -> 0 us
  waiting for transfers between devices: 82.8 us -> 54.5 us
  blocking collectives: 24 us -> 0 us
  other arithmetic: 22 us -> 5.53 us
  Pallas kernels: 0 us -> 14.7 us
  starting transfers between devices: 34.5 us -> 30.8 us
    dot_general x30 -> x0, matrix products: 53.6 us -> none  [the longest x6 18.4 us: attend_tile(): jnp.einsum('hqk,khd->qhd', weights_low, val_heads, preferred_element_type...]
    all_to_all x2 -> x0, blocking collectives: 24 us -> none  [the longest x1 12.1 us: per_device(): lax.all_to_all(value_in, 'head', split_axis=1, concat_axis=0, tiled=True)]
    broadcast_in_dim x24 -> x1, local copies, waits for them, and re-layouts: 21 us -> 0.07 us  [window_bias(): return jnp.repeat(bias, TILE, axis=1)]
    ppermute x4 -> x5, waiting for transfers between devices: 47.5 us -> 27.7 us  [the longest x1 11.7 us: per_device(): from_before = lax.ppermute(ahead, 'group', up)]
    reshape x20 -> x5, local copies, waits for them, and re-layouts: 22.6 us -> 3.67 us  [the longest x2 1.79 us: incoming(): jnp.transpose(second, (1, 0, 2)).reshape(rows, full_width)]
    pallas_call x0 -> x1, Pallas kernels: none -> 14.7 us  [attend(): pl.pallas_call(attend_kernel, grid=(width // HD,), in_specs=[pl.BlockSpec...]
    dynamic_slice x12 -> x0, local copies, waits for them, and re-layouts: 14.6 us -> none  [per_device(): lax.map(per_tile, (query_tiles, grad_tiles, neighbours))]
    convert_element_type x12 -> x0, local copies, waits for them, and re-layouts: 14 us -> none  [the longest x6 9.64 us: attend_tile(): out_heads = jnp.einsum('hqk,khd->qhd', weights_low, val_heads, preferred_...]
  transfers between devices with their start and end apart: 10 -> 9, of which waited for: 7 -> 7; matrix products, arithmetic and copies ran while one was open for 7% -> 7% of each run, Pallas kernels for 0% -> 0%
where the time goes in v1:
time: 117 us; the launch traced here: 116 us
  waiting for transfers between devices  54.5 us (47%)
  starting transfers between devices  30.8 us (26%)
  Pallas kernels  14.7 us (13%)
  local copies, waits for them, and re-layouts  9.9 us (8%)
  other arithmetic  5.53 us (5%)
    pallas_call x1, Pallas kernels, attend(): pl.pallas_call(attend_kernel, grid=(width // HD,), in_specs=[pl.BlockSpec...  14.7 us
    all_to_all x1, waiting for transfers between devices, per_device(): lax.all_to_all(grads, plane, 0, 0, tiled=True)  13.9 us
    all_to_all x1, waiting for transfers between devices, per_device(): kv = lax.all_to_all(outgoing(key_in, value_in), plane, 0, 0, tiled=True)  12.8 us
    ppermute x1, waiting for transfers between devices, per_device(): from_before = lax.ppermute(ahead, 'group', up)  11.7 us
    ppermute x1, waiting for transfers between devices, per_device(): other = lax.ppermute(bias, 'pair', [(0, 1), (1, 0)])  6.66 us
    ppermute x1, starting transfers between devices, per_device(): before = lax.ppermute(kv[half:], 'group', up)  5.37 us
    all_to_all x1, starting transfers between devices, per_device(): kv = lax.all_to_all(outgoing(key_in, value_in), plane, 0, 0, tiled=True)  5.3 us
    unnamed x22, local copies, waits for them, and re-layouts  4.73 us
  transfers between devices with their start and end apart: 9, of which 7 were waited for; matrix products, arithmetic and copies ran while one was open for 7% of the time, Pallas kernels for 0%

profile of v1, /device:TPU:0, one launch (start us, length us, event | category | flops | bytes accessed | tf_op | source)
XLA Modules:
  0.0 116.2 jit_solution(7747800476549927021)
XLA Ops:
  0.6 1.2 %copy.31 = bf16[12,8,8,384]{3,2,1,0:T(8,128)(2,1)S(1)} copy(bf16[12,8,8,384]{3,1,2,0:T(8,128)(2,1)} %bitcast.44) | data formatting | bytes 1179648
  2.1 1.2 maximum_bitcast_fusion.1
  3.3 5.3 %all-to-all-start.1 = ((bf16[8,2,96,384]{3,2,1,0:T(8,128)(2,1)}), bf16[8,2,96,384]{3,2,1,0:T(8,128)(2,1)S(1)}, u32[]{:S(2)}, u32[]{:S(2)}) async-start(bf16[8,2,96,384]{3,2,1,0:T(8,128)(2,1)} %maximum_bitcast_fusion.1), calls=%async_computation.1 | async-start | bytes 2359296 | tf_op jit(solution)/shard_map/all_to_all | solution.py:128
  10.5 1.2 %maximum_bitcast_fusion = bf16[8,2,96,384]{3,2,1,0:T(8,128)(2,1)} fusion(bf16[1,96,8,384]{3,1,0,2:T(8,128)(2,1)S(1)} %copy.18, bf16[1,96,8,384]{3,1,0,2:T(8,128)(2,1)S(1)} %copy.17), kind=kLoop, calls=%fused_computation.1 | loop fusion | flops 589824 | bytes 2359296 | tf_op jit(solution)/shard_map/transpose | solution.py:112
  11.6 12.8 %all-to-all-done.1.kv_ref = bf16[8,2,96,384]{3,2,1,0:T(8,128)(2,1)S(1)} async-done(((bf16[8,2,96,384]{3,2,1,0:T(8,128)(2,1)}), bf16[8,2,96,384]{3,2,1,0:T(8,128)(2,1)S(1)}, u32[]{:S(2)}, u32[]{:S(2)}) %all-to-all-start.1) | async-done | bytes 1179680 | tf_op jit(solution)/shard_map/all_to_all | solution.py:128
  24.5 3.6 %all-to-all-start = ((bf16[8,2,96,384]{3,2,1,0:T(8,128)(2,1)}), bf16[8,2,96,384]{3,2,1,0:T(8,128)(2,1)S(1)}, u32[]{:S(2)}, u32[]{:S(2)}) async-start(bf16[8,2,96,384]{3,2,1,0:T(8,128)(2,1)} %maximum_bitcast_fusion), calls=%async_computation | async-start | bytes 2359296 | tf_op jit(solution)/shard_map/all_to_all | solution.py:131
  28.2 2.0 %collective-permute-start = (f32[6,1152]{1,0:T(8,128)S(1)}, f32[6,1152]{1,0:T(8,128)S(1)}, u32[]{:S(2)}, u32[]{:S(2)}) collective-permute-start(f32[6,1152]{1,0:T(8,128)S(1)} %reshape.30), channel_id=1, source_target_pairs={{0,4},{4,0},{1,5},{5,1},{2,6},{6,2},{3,7},{7,3},{8,12},{12,8},{9,1... | collective-permute-start | bytes 82952 | tf_op jit(solution)/shard_map/ppermute | solution.py:125
  30.2 1.1 fusion
  31.3 1.3 %collective-permute-start.2 = (bf16[4,2,96,384]{3,2,1,0:T(8,128)(2,1)}, bf16[4,2,96,384]{3,2,1,0:T(8,128)(2,1)S(1)}, u32[]{:S(2)}, u32[]{:S(2)}) collective-permute-start(bf16[4,2,96,384]{3,2,1,0:T(8,128)(2,1)} %get-tuple-element.16), channel_id=1, source_target_pairs={{8,0},{16,8},{24,16},{9,1},{17,9},{25,17},{10,2},{18,10},{26,18},{... | collective-permute-start | bytes 1769480 | tf_op jit(solution)/shard_map/ppermute | solution.py:130
  32.6 5.4 %collective-permute-start.1 = (bf16[4,2,96,384]{3,2,1,0:T(8,128)(2,1)}, bf16[4,2,96,384]{3,2,1,0:T(8,128)(2,1)}, u32[]{:S(2)}, u32[]{:S(2)}) collective-permute-start(bf16[4,2,96,384]{3,2,1,0:T(8,128)(2,1)} %get-tuple-element.17), channel_id=1, source_target_pairs={{0,8},{8,16},{16,24},{1,9},{9,17},{17,25},{2,10},{10,18},{18,26},{... | collective-permute-start | bytes 1769480 | tf_op jit(solution)/shard_map/ppermute | solution.py:129
  37.9 6.7 %collective-permute-done = f32[6,1152]{1,0:T(8,128)S(1)} collective-permute-done((f32[6,1152]{1,0:T(8,128)S(1)}, f32[6,1152]{1,0:T(8,128)S(1)}, u32[]{:S(2)}, u32[]{:S(2)}) %collective-permute-start) | collective-permute-done | bytes 27680 | tf_op jit(solution)/shard_map/ppermute | solution.py:125
  44.6 3.8 %collective-permute-done.2.after_ref = bf16[4,2,96,384]{3,2,1,0:T(8,128)(2,1)S(1)} collective-permute-done((bf16[4,2,96,384]{3,2,1,0:T(8,128)(2,1)}, bf16[4,2,96,384]{3,2,1,0:T(8,128)(2,1)S(1)}, u32[]{:S(2)}, u32[]{:S(2)}) %collective-permute-start.2) | collective-permute-done | bytes 589856 | tf_op jit(solution)/shard_map/ppermute | solution.py:130
  48.5 1.3 %collective-permute-done.1.before_ref = bf16[4,2,96,384]{3,2,1,0:T(8,128)(2,1)} collective-permute-done((bf16[4,2,96,384]{3,2,1,0:T(8,128)(2,1)}, bf16[4,2,96,384]{3,2,1,0:T(8,128)(2,1)}, u32[]{:S(2)}, u32[]{:S(2)}) %collective-permute-start.1) | collective-permute-done | bytes 589856 | tf_op jit(solution)/shard_map/ppermute | solution.py:129
  49.8 14.7 %shard_map.84 = (bf16[8,2,96,384]{3,2,1,0:T(8,128)(2,1)}, f32[8,2,96,384]{3,2,1,0:T(8,128)}, bf16[4,2,96,384]{3,2,1,0:T(8,128)(2,1)S(1)}, bf16[4,2,96,384]{3,2,1,0:T(8,128)(2,1)S(1)}) custom-call(f32[12,1152]{1,0:T(8,128)S(1)} %pad_maximum_fusion.bias_ref, bf16[8,2,96,384]{3,2,1,0:T(8,128)(2,1)S(1)} %all-to-all-done.qg_ref, ...), custom_call_target="tpu_custom_call" | custom-call | flops 4076863488 | bytes 16777216 | tf_op jit(solution)/shard_map/pallas_call | solution.py:91
  66.1 3.7 %all-to-all-start.2 = ((bf16[8,2,96,384]{3,2,1,0:T(8,128)(2,1)}), bf16[8,2,96,384]{3,2,1,0:T(8,128)(2,1)S(1)}, u32[]{:S(2)}, u32[]{:S(2)}) async-start(bf16[8,2,96,384]{3,2,1,0:T(8,128)(2,1)} %get-tuple-element.8), calls=%async_computation.2 | async-start | bytes 2359296 | tf_op jit(solution)/shard_map/all_to_all | solution.py:135
  69.8 4.4 %collective-permute-start.3 = (bf16[4,2,96,384]{3,2,1,0:T(8,128)(2,1)S(1)}, bf16[4,2,96,384]{3,2,1,0:T(8,128)(2,1)S(1)}, u32[]{:S(2)}, u32[]{:S(2)}) collective-permute-start(bf16[4,2,96,384]{3,2,1,0:T(8,128)(2,1)S(1)} %copy-done.3), channel_id=1, source_target_pairs={{0,8},{8,16},{16,24},{1,9},{9,17},{17,25},{2,10},{10,18},{18,26},{... | collective-permute-start | bytes 1769480 | tf_op jit(solution)/shard_map/ppermute | solution.py:133
  74.2 1.3 %collective-permute-start.4 = (bf16[4,2,96,384]{3,2,1,0:T(8,128)(2,1)S(1)}, bf16[4,2,96,384]{3,2,1,0:T(8,128)(2,1)S(1)}, u32[]{:S(2)}, u32[]{:S(2)}) collective-permute-start(bf16[4,2,96,384]{3,2,1,0:T(8,128)(2,1)S(1)} %copy-done.1), channel_id=1, source_target_pairs={{8,0},{16,8},{24,16},{9,1},{17,9},{25,17},{10,2},{18,10},{26,18},{... | collective-permute-start | bytes 1769480 | tf_op jit(solution)/shard_map/ppermute | solution.py:134
  75.5 11.7 %collective-permute-done.3 = bf16[4,2,96,384]{3,2,1,0:T(8,128)(2,1)S(1)} collective-permute-done((bf16[4,2,96,384]{3,2,1,0:T(8,128)(2,1)S(1)}, bf16[4,2,96,384]{3,2,1,0:T(8,128)(2,1)S(1)}, u32[]{:S(2)}, u32[]{:S(2)}) %collective-permute-start.3) | collective-permute-done | bytes 589856 | tf_op jit(solution)/shard_map/ppermute | solution.py:133
  87.3 4.2 %collective-permute-done.4 = bf16[4,2,96,384]{3,2,1,0:T(8,128)(2,1)S(1)} collective-permute-done((bf16[4,2,96,384]{3,2,1,0:T(8,128)(2,1)S(1)}, bf16[4,2,96,384]{3,2,1,0:T(8,128)(2,1)S(1)}, u32[]{:S(2)}, u32[]{:S(2)}) %collective-permute-start.4) | collective-permute-done | bytes 589856 | tf_op jit(solution)/shard_map/ppermute | solution.py:134
  91.5 3.1 %add_convert_fusion = bf16[8,2,96,384]{3,2,1,0:T(8,128)(2,1)} fusion(f32[8,2,96,384]{3,2,1,0:T(8,128)} %get-tuple-element.9, bf16[4,2,96,384]{3,2,1,0:T(8,128)(2,1)S(1)} %collective-permute-done.4, bf16[4,2,96,384]{3,2,1,0:T(8,128)(2,1)S(1)} %collective-permute-done.3), kind=kLoop, calls=%fused_computation | loop fusion | flops 2359296 | bytes 4718592 | tf_op jit(solution)/shard_map/convert_element_type | solution.py:137
  94.5 3.9 %all-to-all-start.3 = ((bf16[8,2,96,384]{3,2,1,0:T(8,128)(2,1)}), bf16[8,2,96,384]{3,2,1,0:T(8,128)(2,1)S(1)}, u32[]{:S(2)}, u32[]{:S(2)}) async-start(bf16[8,2,96,384]{3,2,1,0:T(8,128)(2,1)} %add_convert_fusion), calls=%async_computation.3 | async-start | bytes 2359296 | tf_op jit(solution)/shard_map/all_to_all | solution.py:138
  98.5 0.9 copy.26
  100.3 13.9 %all-to-all-done.3 = bf16[8,2,96,384]{3,2,1,0:T(8,128)(2,1)S(1)} async-done(((bf16[8,2,96,384]{3,2,1,0:T(8,128)(2,1)}), bf16[8,2,96,384]{3,2,1,0:T(8,128)(2,1)S(1)}, u32[]{:S(2)}, u32[]{:S(2)}) %all-to-all-start.3) | async-done | bytes 1179680 | tf_op jit(solution)/shard_map/all_to_all | solution.py:138
  114.4 0.9 copy.28
  (37 shorter events, 5.9 us)
Async XLA Ops:
  0.6 1.3 %copy-start.4 = (bf16[96,3072]{1,0:T(8,128)(2,1)S(1)}, bf16[96,3072]{1,0:T(8,128)(2,1)}, u32[]{:S(2)}) copy-start(bf16[96,3072]{1,0:T(8,128)(2,1)} %param.7) | copy-start | bytes 1769476
  3.3 5.3 %copy-start.5 = (bf16[96,3072]{1,0:T(8,128)(2,1)S(1)}, bf16[96,3072]{1,0:T(8,128)(2,1)}, u32[]{:S(2)}) copy-start(bf16[96,3072]{1,0:T(8,128)(2,1)} %param.5) | copy-start | bytes 1769476
  3.3 21.2 %all-to-all-start.1 = ((bf16[8,2,96,384]{3,2,1,0:T(8,128)(2,1)}), bf16[8,2,96,384]{3,2,1,0:T(8,128)(2,1)S(1)}, u32[]{:S(2)}, u32[]{:S(2)}) async-start(bf16[8,2,96,384]{3,2,1,0:T(8,128)(2,1)} %maximum_bitcast_fusion.1), calls=%async_computation.1 | async-start | bytes 2359296 | tf_op jit(solution)/shard_map/all_to_all | solution.py:128
  8.6 1.1 copy-start.6
  9.7 0.7 copy-start.7
  24.5 20.2 %all-to-all-start = ((bf16[8,2,96,384]{3,2,1,0:T(8,128)(2,1)}), bf16[8,2,96,384]{3,2,1,0:T(8,128)(2,1)S(1)}, u32[]{:S(2)}, u32[]{:S(2)}) async-start(bf16[8,2,96,384]{3,2,1,0:T(8,128)(2,1)} %maximum_bitcast_fusion), calls=%async_computation | async-start | bytes 2359296 | tf_op jit(solution)/shard_map/all_to_all | solution.py:131
  28.2 16.4 %collective-permute-start = (f32[6,1152]{1,0:T(8,128)S(1)}, f32[6,1152]{1,0:T(8,128)S(1)}, u32[]{:S(2)}, u32[]{:S(2)}) collective-permute-start(f32[6,1152]{1,0:T(8,128)S(1)} %reshape.30), channel_id=1, source_target_pairs={{0,4},{4,0},{1,5},{5,1},{2,6},{6,2},{3,7},{7,3},{8,12},{12,8},{9,1... | collective-permute-start | bytes 82952 | tf_op jit(solution)/shard_map/ppermute | solution.py:125
  31.3 17.2 %collective-permute-start.2 = (bf16[4,2,96,384]{3,2,1,0:T(8,128)(2,1)}, bf16[4,2,96,384]{3,2,1,0:T(8,128)(2,1)S(1)}, u32[]{:S(2)}, u32[]{:S(2)}) collective-permute-start(bf16[4,2,96,384]{3,2,1,0:T(8,128)(2,1)} %get-tuple-element.16), channel_id=1, source_target_pairs={{8,0},{16,8},{24,16},{9,1},{17,9},{25,17},{10,2},{18,10},{26,18},{... | collective-permute-start | bytes 1769480 | tf_op jit(solution)/shard_map/ppermute | solution.py:130
  32.6 17.2 %collective-permute-start.1 = (bf16[4,2,96,384]{3,2,1,0:T(8,128)(2,1)}, bf16[4,2,96,384]{3,2,1,0:T(8,128)(2,1)}, u32[]{:S(2)}, u32[]{:S(2)}) collective-permute-start(bf16[4,2,96,384]{3,2,1,0:T(8,128)(2,1)} %get-tuple-element.17), channel_id=1, source_target_pairs={{0,8},{8,16},{16,24},{1,9},{9,17},{17,25},{2,10},{10,18},{18,26},{... | collective-permute-start | bytes 1769480 | tf_op jit(solution)/shard_map/ppermute | solution.py:129
  64.4 0.8 copy-start
  65.3 0.8 copy-start.2
  66.1 3.7 %copy-start.3 = (bf16[4,2,96,384]{3,2,1,0:T(8,128)(2,1)S(1)}, bf16[4,2,96,384]{3,2,1,0:T(8,128)(2,1)}, u32[]{:S(2)}) copy-start(bf16[4,2,96,384]{3,2,1,0:T(8,128)(2,1)} %copy-done.2) | copy-start | bytes 1769476
  66.1 8.2 %copy-start.1 = (bf16[4,2,96,384]{3,2,1,0:T(8,128)(2,1)S(1)}, bf16[4,2,96,384]{3,2,1,0:T(8,128)(2,1)}, u32[]{:S(2)}) copy-start(bf16[4,2,96,384]{3,2,1,0:T(8,128)(2,1)} %copy-done) | copy-start | bytes 1769476
  66.1 28.5 %all-to-all-start.2 = ((bf16[8,2,96,384]{3,2,1,0:T(8,128)(2,1)}), bf16[8,2,96,384]{3,2,1,0:T(8,128)(2,1)S(1)}, u32[]{:S(2)}, u32[]{:S(2)}) async-start(bf16[8,2,96,384]{3,2,1,0:T(8,128)(2,1)} %get-tuple-element.8), calls=%async_computation.2 | async-start | bytes 2359296 | tf_op jit(solution)/shard_map/all_to_all | solution.py:135
  69.8 17.5 %collective-permute-start.3 = (bf16[4,2,96,384]{3,2,1,0:T(8,128)(2,1)S(1)}, bf16[4,2,96,384]{3,2,1,0:T(8,128)(2,1)S(1)}, u32[]{:S(2)}, u32[]{:S(2)}) collective-permute-start(bf16[4,2,96,384]{3,2,1,0:T(8,128)(2,1)S(1)} %copy-done.3), channel_id=1, source_target_pairs={{0,8},{8,16},{16,24},{1,9},{9,17},{17,25},{2,10},{10,18},{18,26},{... | collective-permute-start | bytes 1769480 | tf_op jit(solution)/shard_map/ppermute | solution.py:133
  74.2 17.2 %collective-permute-start.4 = (bf16[4,2,96,384]{3,2,1,0:T(8,128)(2,1)S(1)}, bf16[4,2,96,384]{3,2,1,0:T(8,128)(2,1)S(1)}, u32[]{:S(2)}, u32[]{:S(2)}) collective-permute-start(bf16[4,2,96,384]{3,2,1,0:T(8,128)(2,1)S(1)} %copy-done.1), channel_id=1, source_target_pairs={{8,0},{16,8},{24,16},{9,1},{17,9},{25,17},{10,2},{18,10},{26,18},{... | collective-permute-start | bytes 1769480 | tf_op jit(solution)/shard_map/ppermute | solution.py:134
  94.5 19.7 %all-to-all-start.3 = ((bf16[8,2,96,384]{3,2,1,0:T(8,128)(2,1)}), bf16[8,2,96,384]{3,2,1,0:T(8,128)(2,1)S(1)}, u32[]{:S(2)}, u32[]{:S(2)}) async-start(bf16[8,2,96,384]{3,2,1,0:T(8,128)(2,1)} %add_convert_fusion), calls=%async_computation.3 | async-start | bytes 2359296 | tf_op jit(solution)/shard_map/all_to_all | solution.py:138

commit v2 on v1

v2 whole, which is shorter than its diff:
```python
import functools
import math

import jax
import jax.numpy as jnp
from jax import lax
from jax.experimental import pallas as pl
from jax.experimental.pallas import tpu as pltpu
from jax.sharding import Mesh
from jax.sharding import PartitionSpec as P

HD = 128
TILE = 64
MASKED = -1e30
AXES = ("group", "pair", "row", "core")
PLANE = ("pair", "row", "core")
SHIFTS = ((1, 1), (0, 0), (0, 1), (1, 0))
CHUNKS = 3
ANY = pl.BlockSpec(memory_space=pl.ANY)
BF16 = jnp.bfloat16


def head_group(shift):
    a, b = shift
    rows = lax.axis_size("row")
    return (lax.axis_index("core") ^ a) * rows + lax.rem(lax.axis_index("row") + b, rows)


def run_copies(copies):
    for copy in copies:
        copy.start()
    for copy in copies:
        copy.wait()


def pack_kernel(offset, width, group_width, *refs):
    arrays, messages, sem = refs[:4], refs[4:8], refs[8]
    copies = []
    for i, shift in enumerate(SHIFTS):
        column = pl.multiple_of(head_group(shift) * group_width + offset, HD)
        for j, array in enumerate(arrays):
            copies.append(
                pltpu.make_async_copy(array.at[:, pl.ds(column, width)], messages[i].at[j], sem.at[i, j])
            )
    run_copies(copies)


def pack(arrays, offset, width, group_width):
    rows = arrays[0].shape[0]
    return pl.pallas_call(
        functools.partial(pack_kernel, offset, width, group_width),
        in_specs=[ANY] * 4,
        out_specs=[ANY] * 4,
        out_shape=[jax.ShapeDtypeStruct((4, rows, width), BF16)] * 4,
        scratch_shapes=[pltpu.SemaphoreType.DMA((4, 4))],
        cost_estimate=pl.CostEstimate(flops=0, bytes_accessed=32 * rows * width * 2, transcendentals=0),
    )(*arrays)


def unpack_kernel(offset, width, group_width, *refs):
    messages, sem = refs[:4], refs[-1]
    arrays = refs[-3:-1]
    copies = []
    for i, shift in enumerate(SHIFTS):
        column = pl.multiple_of(head_group(shift) * group_width + offset, HD)
        for j, array in enumerate(arrays):
            copies.append(
                pltpu.make_async_copy(messages[i].at[j], array.at[:, pl.ds(column, width)], sem.at[i, j])
            )
    run_copies(copies)


def unpack(messages, arrays, offset, group_width, full_width):
    _, rows, width = messages[0].shape
    held = [] if arrays is None else list(arrays)
    return pl.pallas_call(
        functools.partial(unpack_kernel, offset, width, group_width),
        in_specs=[ANY] * (4 + len(held)),
        out_specs=[ANY] * 2,
        out_shape=[jax.ShapeDtypeStruct((rows, full_width), BF16)] * 2,
        input_output_aliases={4 + i: i for i in range(len(held))},
        scratch_shapes=[pltpu.SemaphoreType.DMA((4, 2))],
        cost_estimate=pl.CostEstimate(flops=0, bytes_accessed=16 * rows * width * 2, transcendentals=0),
    )(*messages, *held)


def join_kernel(*refs):
    messages, joined, sem = refs[:4], refs[4], refs[5]
    run_copies([pltpu.make_async_copy(m.at[:2], joined.at[i], sem.at[i]) for i, m in enumerate(messages)])


def join(messages):
    _, rows, width = messages[0].shape
    return pl.pallas_call(
        join_kernel,
        in_specs=[ANY] * 4,
        out_specs=ANY,
        out_shape=jax.ShapeDtypeStruct((4, 2, rows, width), BF16),
        scratch_shapes=[pltpu.SemaphoreType.DMA((4,))],
        cost_estimate=pl.CostEstimate(flops=0, bytes_accessed=16 * rows * width * 2, transcendentals=0),
    )(*messages)


def attend_kernel(bias_ref, *refs):
    messages, other_ref, halo_ref = refs[:4], refs[4], refs[5]
    oq_refs, own_out, other_out, halo_out = refs[6:10], refs[10], refs[11], refs[12]
    scale = 1.0 / math.sqrt(HD)
    log2_scale = scale * math.log2(math.e)
    rows = other_ref.shape[2]
    slab = 4 * rows

    def window(which):
        return jnp.concatenate(
            [m[which] for m in messages]
            + [other_ref[:, which].reshape(slab, HD), halo_ref[:, which].reshape(slab, HD)],
            axis=0,
        )

    nt = (((1,), (1,)), ((), ()))
    nn = (((1,), (0,)), ((), ()))
    tn = (((0,), (0,)), ((), ()))
    dot = functools.partial(lax.dot_general, preferred_element_type=jnp.float32)
    key_win, val_win = window(0), window(1)
    query = jnp.concatenate([m[2] for m in messages], axis=0)
    grad = jnp.concatenate([m[3] for m in messages], axis=0)
    scores = dot(query, key_win, nt) + bias_ref[...]
    peak = jnp.max(scores, axis=1, keepdims=True)
    weights = jnp.exp2((scores - peak) * log2_scale)
    weights = weights * (1.0 / jnp.sum(weights, axis=1, keepdims=True))
    weights_low = weights.astype(BF16)
    out = dot(weights_low, val_win, nn).astype(BF16)
    out_dot = jnp.sum(grad.astype(jnp.float32) * out.astype(jnp.float32), axis=1, keepdims=True)
    dweights = dot(grad, val_win, nt)
    dscores = (weights * (dweights - out_dot)).astype(BF16)
    dquery = (dot(dscores, key_win, nn) * scale).astype(BF16)
    for i, ref in enumerate(oq_refs):
        ref[0] = out[i * rows : (i + 1) * rows]
        ref[1] = dquery[i * rows : (i + 1) * rows]
    grads = (dot(dscores, query, tn) * scale, dot(weights_low, grad, tn))
    for which, value in enumerate(grads):
        for third, ref in enumerate((own_out, other_out, halo_out)):
            piece = value[third * slab : (third + 1) * slab]
            ref[:, which] = piece.reshape(4, rows, HD).astype(ref.dtype)


def attend(bias, messages, other, halo):
    _, rows, width = messages[0].shape
    heads = width // HD
    four = pl.BlockSpec((4, rows, HD), lambda h: (0, 0, h))
    two = pl.BlockSpec((2, rows, HD), lambda h: (0, 0, h))
    joined = pl.BlockSpec((4, 2, rows, HD), lambda h: (0, 0, 0, h))
    pairs = bias.shape[0] * bias.shape[1] * heads
    shapes = [jax.ShapeDtypeStruct((2, rows, width), BF16)] * 4
    shapes += [jax.ShapeDtypeStruct((4, 2, rows, width), t) for t in (jnp.float32, BF16, BF16)]
    outs = pl.pallas_call(
        attend_kernel,
        grid=(heads,),
        in_specs=[pl.BlockSpec(bias.shape, lambda h: (0, 0))] + [four] * 4 + [joined] * 2,
        out_specs=[two] * 4 + [joined] * 3,
        out_shape=shapes,
        compiler_params=pltpu.CompilerParams(vmem_limit_bytes=40 * 1024 * 1024),
        cost_estimate=pl.CostEstimate(flops=12 * pairs * HD, bytes_accessed=6 * 2**20, transcendentals=pairs),
    )(bias, *messages, other, halo)
    return outs[:4], outs[4], outs[5], outs[6]


def total_kernel(own_ref, other_ref, halo_ref, *outs):
    for i, ref in enumerate(outs):
        total = own_ref[i] + other_ref[i].astype(jnp.float32) + halo_ref[i].astype(jnp.float32)
        ref[...] = total.astype(BF16)


def total(own, other, halo):
    _, _, rows, width = own.shape
    joined = pl.BlockSpec((4, 1, rows, width), lambda k: (0, k, 0, 0))
    return pl.pallas_call(
        total_kernel,
        grid=(2,),
        in_specs=[joined] * 3,
        out_specs=[pl.BlockSpec((1, rows, width), lambda k: (k, 0, 0))] * 4,
        out_shape=[jax.ShapeDtypeStruct((2, rows, width), BF16)] * 4,
        cost_estimate=pl.CostEstimate(flops=own.size * 2, bytes_accessed=own.size * 10, transcendentals=0),
    )(own, other, halo)


def window_bias(neighbours, rows):
    tiles = neighbours.shape[0]
    slab_rows = tiles * TILE
    core = lax.axis_index("core")
    swap = []
    sizes = [lax.axis_size(a) for a in PLANE]
    index = lambda p, r, c: (p * sizes[1] + r) * 2 + c
    for p in range(2):
        for r in range(sizes[1]):
            for c in range(2):
                swap.append((index(p, r, c), index(c, r, p)))
    ids = lax.ppermute(neighbours, PLANE, swap)
    slab = lax.axis_index("group") * 2 + core
    window_ids = (slab - 1) * tiles + jnp.arange(3 * tiles, dtype=jnp.int32)
    listed = jnp.any((ids[:, :, None] == window_ids[None, None, :]) & (ids[:, :, None] >= 0), axis=1)
    blocks = []
    for a, b in SHIFTS:
        source_row = lax.rem(lax.axis_index("row") - b + sizes[1], sizes[1])
        blocks.append(source_row * 2 + (lax.axis_index("pair") ^ a))
    token = (jnp.stack(blocks)[:, None] * rows + jnp.arange(rows, dtype=jnp.int32)[None, :]).reshape(slab_rows)
    tile = token // TILE
    other = jnp.where(core == 0, 2 * tiles, 0)
    columns = jnp.concatenate([tile + tiles, tile + other, tile + 2 * tiles - other])
    pick_rows = (tile[:, None] == jnp.arange(tiles)[None, :]).astype(BF16)
    pick_columns = (jnp.arange(3 * tiles)[:, None] == columns[None, :]).astype(BF16)
    spread = jnp.dot(listed.astype(BF16), pick_columns)
    allowed = jnp.dot(pick_rows, spread, preferred_element_type=jnp.float32)
    return jnp.where(allowed > 0.5, 0.0, MASKED).astype(jnp.float32)


def per_device(query_in, key_in, value_in, grad_out, neighbours):
    groups, rings = lax.axis_size("group"), lax.axis_size("row")
    rows, full_width = query_in.shape
    group_width = full_width // (2 * rings)
    width = group_width // CHUNKS

    def place(g, p, r, c):
        return ((g * 2 + p) * rings + r) * 2 + c

    everyone = [(g, p, r, c) for g in range(groups) for p in range(2) for r in range(rings) for c in range(2)]

    def spread_pairs(shift):
        a, b = shift
        return [(place(g, p, r, c), place(g, c ^ a, (r + b) % rings, p)) for g, p, r, c in everyone]

    beside = []
    for g, p, r, c in everyone:
        to = g + 1 if c == 1 else g - 1
        if 0 <= to < groups:
            beside.append((place(g, p, r, c), place(to, p, r, 1 - c)))

    def send(messages):
        return [lax.ppermute(m, AXES, spread_pairs(s)) for m, s in zip(messages, SHIFTS)]

    def send_back(messages):
        return [
            lax.ppermute(m, AXES, [(d, s) for s, d in spread_pairs(shift)]) for m, shift in zip(messages, SHIFTS)
        ]

    def across(x):
        return lax.ppermute(x, "core", [(0, 1), (1, 0)])

    def halo(x):
        return lax.ppermute(x, AXES, beside)

    bias = window_bias(neighbours, rows)
    arrays = (key_in, value_in, query_in, grad_out)
    offsets = [k * width for k in range(CHUNKS)]
    received = [send(pack(arrays, offset, width, group_width)) for offset in offsets]
    forward = backward = None
    for k, offset in enumerate(offsets):
        messages = received[k]
        joined = join(messages)
        oq, own, other, far = attend(bias, messages, across(joined), halo(joined))
        grads = total(own, across(other), halo(far))
        forward = unpack(send_back(oq), forward, offset, group_width, full_width)
        backward = unpack(send_back(grads), backward, offset, group_width, full_width)
    return forward[0], forward[1], backward[0], backward[1]


def solution(mesh):
    slabs, heads = mesh.devices.shape
    paired = Mesh(mesh.devices.reshape(slabs // 2, 2, heads // 2, 2), AXES)
    tokens = P(AXES, None)
    return jax.shard_map(
        per_device,
        mesh=paired,
        in_specs=(tokens, tokens, tokens, tokens, P(("group", "pair"), None)),
        out_specs=(tokens, tokens, tokens, tokens),
        check_vma=False,
    )
```

time: 117 us -> 304 us (2.60)
  Pallas kernels: 14.7 us -> 216 us
  waiting for transfers between devices: 54.5 us -> 2.35 us
  starting transfers between devices: 30.8 us -> 72.6 us
  other arithmetic: 5.53 us -> 0.29 us
    pallas_call x1 -> x18, Pallas kernels: 14.7 us -> 216 us  [the longest x6 78.6 us: unpack(): pl.pallas_call(functools.partial(unpack_kernel, offset, width, group_widt...]
    ppermute x5 -> x49, starting transfers between devices: 14.3 us -> 72.6 us  [the longest x24 33 us: send_back(): lax.ppermute(m, AXES, [(d, s) for s, d in spread_pairs(shift)])]
    all_to_all x4 -> x0, waiting for transfers between devices: 26.8 us -> none  [the longest x1 13.9 us: per_device(): lax.all_to_all(grads, plane, 0, 0, tiled=True)]
    ppermute x5 -> x49, waiting for transfers between devices: 27.7 us -> 2.35 us  [the longest x24 2.28 us: send_back(): lax.ppermute(m, AXES, [(d, s) for s, d in spread_pairs(shift)])]
    all_to_all x4 -> x0, starting transfers between devices: 16.4 us -> none  [the longest x1 5.3 us: per_device(): kv = lax.all_to_all(outgoing(key_in, value_in), plane, 0, 0, tiled=True)]
    unnamed x22 -> x130, local copies, waits for them, and re-layouts: 4.73 us -> 10 us
    reshape x5 -> x0, local copies, waits for them, and re-layouts: 3.67 us -> none  [the longest x2 1.79 us: incoming(): jnp.transpose(second, (1, 0, 2)).reshape(rows, full_width)]
    convert_element_type x1 -> x0, other arithmetic: 3.07 us -> none  [per_device(): grads = (own + arrived).astype(jnp.bfloat16)]
  transfers between devices with their start and end apart: 9 -> 49, of which waited for: 7 -> 1; matrix products, arithmetic and copies ran while one was open for 7% -> 0% of each run, Pallas kernels for 0% -> 67%
where the time goes in v2:
time: 304 us; the launch traced here: 303 us
  Pallas kernels  216 us (71%)
  starting transfers between devices  72.6 us (24%)
  local copies, waits for them, and re-layouts  10.1 us (3%)
    pallas_call x6, Pallas kernels, unpack(): pl.pallas_call(functools.partial(unpack_kernel, offset, width, group_widt...  78.6 us
    pallas_call x3, Pallas kernels, pack(): pl.pallas_call(functools.partial(pack_kernel, offset, width, group_width)...  75.2 us
    pallas_call x3, Pallas kernels, join(): pl.pallas_call(join_kernel, in_specs=[ANY] * 4, out_specs=ANY, out_shape=...  39.1 us
    ppermute x24, starting transfers between devices, send_back(): lax.ppermute(m, AXES, [(d, s) for s, d in spread_pairs(shift)])  33 us
    ppermute x12, starting transfers between devices, send(): lax.ppermute(m, AXES, spread_pairs(s))  19.6 us
    pallas_call x3, Pallas kernels, attend(): pl.pallas_call(attend_kernel, grid=(heads,), in_specs=[pl.BlockSpec(bias....  16.6 us
    ppermute x6, starting transfers between devices, across(): return lax.ppermute(x, 'core', [(0, 1), (1, 0)])  13.1 us
    unnamed x130, local copies, waits for them, and re-layouts  10 us
  transfers between devices with their start and end apart: 49, of which 1 were waited for; matrix products, arithmetic and copies ran while one was open for 0% of the time, Pallas kernels for 67%

profile of v2, /device:TPU:0, one launch (start us, length us, event | category | flops | bytes accessed | tf_op | source)
XLA Modules:
  0.0 303.2 jit_solution(17542152930825622302)
XLA Ops:
  2.0 25.1 %shard_map.90 = (bf16[4,96,256]{2,1,0:T(8,128)(2,1)}, bf16[4,96,256]{2,1,0:T(8,128)(2,1)}, bf16[4,96,256]{2,1,0:T(8,128)(2,1)}, bf16[4,96,256]{2,1,0:T(8,128)(2,1)}) custom-call(bf16[96,3072]{1,0:T(8,128)(2,1)} %refs_0_.5, bf16[96,3072]{1,0:T(8,128)(2,1)} %refs_1_.5, bf16[96,3072]{1,0:T(8,128)(2,1)} %refs_2_.5, bf16[96,3072]{1,0:T(8,128)(2,1)} %refs_3_.5), custom_call_target="tpu_custom_call" | custom-call | bytes 1572864 | tf_op jit(solution)/shard_map/pallas_call | solution.py:50
  27.0 4.6 %collective-permute-start.21 = (bf16[4,96,256]{2,1,0:T(8,128)(2,1)}, bf16[4,96,256]{2,1,0:T(8,128)(2,1)S(1)}, u32[]{:S(2)}, u32[]{:S(2)}) collective-permute-start(bf16[4,96,256]{2,1,0:T(8,128)(2,1)} %get-tuple-element.77), channel_id=1, source_target_pairs={{0,6},{1,2},{2,4},{3,0},{4,7},{5,3},{6,5},{7,1},{8,14},{9,10},{10,... | collective-permute-start | bytes 589832 | tf_op jit(solution)/shard_map/ppermute | solution.py:238
  35.6 25.1 %shard_map.87 = (bf16[4,96,256]{2,1,0:T(8,128)(2,1)}, bf16[4,96,256]{2,1,0:T(8,128)(2,1)}, bf16[4,96,256]{2,1,0:T(8,128)(2,1)}, bf16[4,96,256]{2,1,0:T(8,128)(2,1)}) custom-call(bf16[96,3072]{1,0:T(8,128)(2,1)} %refs_0_.5, bf16[96,3072]{1,0:T(8,128)(2,1)} %refs_1_.5, bf16[96,3072]{1,0:T(8,128)(2,1)} %refs_2_.5, bf16[96,3072]{1,0:T(8,128)(2,1)} %refs_3_.5), custom_call_target="tpu_custom_call" | custom-call | bytes 1572864 | tf_op jit(solution)/shard_map/pallas_call | solution.py:50
  61.7 25.1 %shard_map.84 = (bf16[4,96,256]{2,1,0:T(8,128)(2,1)}, bf16[4,96,256]{2,1,0:T(8,128)(2,1)}, bf16[4,96,256]{2,1,0:T(8,128)(2,1)}, bf16[4,96,256]{2,1,0:T(8,128)(2,1)}) custom-call(bf16[96,3072]{1,0:T(8,128)(2,1)} %refs_0_.5, bf16[96,3072]{1,0:T(8,128)(2,1)} %refs_1_.5, bf16[96,3072]{1,0:T(8,128)(2,1)} %refs_2_.5, bf16[96,3072]{1,0:T(8,128)(2,1)} %refs_3_.5), custom_call_target="tpu_custom_call" | custom-call | bytes 1572864 | tf_op jit(solution)/shard_map/pallas_call | solution.py:50
  88.2 4.4 %collective-permute-start.14 = (bf16[4,96,256]{2,1,0:T(8,128)(2,1)S(1)}, bf16[4,96,256]{2,1,0:T(8,128)(2,1)S(1)}, u32[]{:S(2)}, u32[]{:S(2)}) collective-permute-start(bf16[4,96,256]{2,1,0:T(8,128)(2,1)S(1)} %copy-done.62), channel_id=1, source_target_pairs={{0,4},{1,0},{2,6},{3,2},{4,5},{5,1},{6,7},{7,3},{8,12},{9,8},{10,1... | collective-permute-start | bytes 589832 | tf_op jit(solution)/shard_map/ppermute | solution.py:238
  93.3 13.0 %shard_map.91 = bf16[4,2,96,256]{3,2,1,0:T(8,128)(2,1)} custom-call(bf16[4,96,256]{2,1,0:T(8,128)(2,1)} %copy-done.3, bf16[4,96,256]{2,1,0:T(8,128)(2,1)} %copy-done.5, bf16[4,96,256]{2,1,0:T(8,128)(2,1)} %copy-done.7, bf16[4,96,256]{2,1,0:T(8,128)(2,1)} %copy-done.9), custom_call_target="tpu_custom_call" | custom-call | bytes 786432 | tf_op jit(solution)/shard_map/pallas_call | solution.py:94
  112.7 13.1 %shard_map.88 = bf16[4,2,96,256]{3,2,1,0:T(8,128)(2,1)} custom-call(bf16[4,96,256]{2,1,0:T(8,128)(2,1)} %copy-done.11, bf16[4,96,256]{2,1,0:T(8,128)(2,1)} %copy-done.15, bf16[4,96,256]{2,1,0:T(8,128)(2,1)} %copy-done.19, bf16[4,96,256]{2,1,0:T(8,128)(2,1)} %copy-done.23), custom_call_target="tpu_custom_call" | custom-call | bytes 786432 | tf_op jit(solution)/shard_map/pallas_call | solution.py:94
  130.1 13.0 %shard_map.85 = bf16[4,2,96,256]{3,2,1,0:T(8,128)(2,1)} custom-call(bf16[4,96,256]{2,1,0:T(8,128)(2,1)} %copy-done.13, bf16[4,96,256]{2,1,0:T(8,128)(2,1)} %copy-done.17, bf16[4,96,256]{2,1,0:T(8,128)(2,1)} %copy-done.21, bf16[4,96,256]{2,1,0:T(8,128)(2,1)} %copy-done.25), custom_call_target="tpu_custom_call" | custom-call | bytes 786432 | tf_op jit(solution)/shard_map/pallas_call | solution.py:94
  143.2 2.3 collective-permute-start.5
  148.6 5.7 %shard_map.92 = (bf16[2,96,256]{2,1,0:T(8,128)(2,1)S(1)}, bf16[2,96,256]{2,1,0:T(8,128)(2,1)S(1)}, bf16[2,96,256]{2,1,0:T(8,128)(2,1)S(1)}, bf16[2,96,256]{2,1,0...) custom-call(f32[384,1152]{1,0:T(8,128)S(1)} %fusion.bias_ref, ...), custom_call_target="tpu_custom_call" | custom-call | flops 1358954496 | bytes 6291456 | tf_op jit(solution)/shard_map/pallas_call | solution.py:155
  155.3 2.9 collective-permute-start.43
  160.6 2.7 collective-permute-start.30
  163.3 5.8 %shard_map.89 = (bf16[2,96,256]{2,1,0:T(8,128)(2,1)S(1)}, bf16[2,96,256]{2,1,0:T(8,128)(2,1)S(1)}, bf16[2,96,256]{2,1,0:T(8,128)(2,1)S(1)}, bf16[2,96,256]{2,1,0...) custom-call(f32[384,1152]{1,0:T(8,128)S(1)} %fusion.bias_ref, ...), custom_call_target="tpu_custom_call" | custom-call | flops 1358954496 | bytes 6291456 | tf_op jit(solution)/shard_map/pallas_call | solution.py:155
  173.4 3.8 %collective-permute-start.20 = (bf16[2,96,256]{2,1,0:T(8,128)(2,1)S(1)}, bf16[2,96,256]{2,1,0:T(8,128)(2,1)S(1)}, u32[]{:S(2)}, u32[]{:S(2)}) collective-permute-start(bf16[2,96,256]{2,1,0:T(8,128)(2,1)S(1)} %get-tuple-element.76), channel_id=1, source_target_pairs={{4,0},{0,1},{6,2},{2,3},{5,4},{1,5},{7,6},{3,7},{12,8},{8,9},{14,1... | collective-permute-start | bytes 294920 | tf_op jit(solution)/shard_map/ppermute | solution.py:242
  179.2 5.0 %shard_map.86 = (bf16[2,96,256]{2,1,0:T(8,128)(2,1)S(1)}, bf16[2,96,256]{2,1,0:T(8,128)(2,1)S(1)}, bf16[2,96,256]{2,1,0:T(8,128)(2,1)S(1)}, bf16[2,96,256]{2,1,0...) custom-call(f32[384,1152]{1,0:T(8,128)S(1)} %fusion.bias_ref, ...), custom_call_target="tpu_custom_call" | custom-call | flops 1358954496 | bytes 6291456 | tf_op jit(solution)/shard_map/pallas_call | solution.py:155
  192.2 3.9 %collective-permute-start.31 = (bf16[4,2,96,256]{3,2,1,0:T(8,128)(2,1)S(1)}, bf16[4,2,96,256]{3,2,1,0:T(8,128)(2,1)S(1)}, u32[]{:S(2)}, u32[]{:S(2)}) collective-permute-start(bf16[4,2,96,256]{3,2,1,0:T(8,128)(2,1)S(1)} %get-tuple-element.92), channel_id=1, source_target_pairs={{0,1},{1,0},{2,3},{3,2},{4,5},{5,4},{6,7},{7,6},{8,9},{9,8},{10,11... | collective-permute-start | bytes 1179656 | tf_op jit(solution)/shard_map/ppermute | solution.py:246
  206.8 2.6 collective-permute-start.48
  219.9 3.2 %collective-permute-start.36 = (bf16[2,96,256]{2,1,0:T(8,128)(2,1)}, bf16[2,96,256]{2,1,0:T(8,128)(2,1)S(1)}, u32[]{:S(2)}, u32[]{:S(2)}) collective-permute-start(bf16[2,96,256]{2,1,0:T(8,128)(2,1)} %get-tuple-element.97), channel_id=1, source_target_pairs={{4,0},{0,1},{6,2},{2,3},{5,4},{1,5},{7,6},{3,7},{12,8},{8,9},{14,1... | collective-permute-start | bytes 294920 | tf_op jit(solution)/shard_map/ppermute | solution.py:242
  223.1 13.1 %shard_map.93 = (bf16[96,3072]{1,0:T(8,128)(2,1)}, bf16[96,3072]{1,0:T(8,128)(2,1)}) custom-call(bf16[2,96,256]{2,1,0:T(8,128)(2,1)} %copy-done.54, bf16[2,96,256]{2,1,0:T(8,128)(2,1)} %copy-done.55, bf16[2,96,256]{2,1,0:T(8,128)(2,1)} %copy-done.56, bf16[2,96,256]{2,1,0:T(8,128)(2,1)} %copy-done.57), custom_call_target="tpu_custom_call" | custom-call | bytes 786432 | tf_op jit(solution)/shard_map/pallas_call | solution.py:76
  236.2 13.1 %shard_map.94 = (bf16[96,3072]{1,0:T(8,128)(2,1)}, bf16[96,3072]{1,0:T(8,128)(2,1)}) custom-call(bf16[2,96,256]{2,1,0:T(8,128)(2,1)} %copy-done.39, bf16[2,96,256]{2,1,0:T(8,128)(2,1)} %copy-done.40, bf16[2,96,256]{2,1,0:T(8,128)(2,1)} %copy-done.41, bf16[2,96,256]{2,1,0:T(8,128)(2,1)} %copy-done.42, ...), custom_call_target="tpu_custom_call", output_to_operand_aliasing={{0}: (4, {}), {1}: (5, {})} | custom-call | bytes 786432 | tf_op jit(solution)/shard_map/pallas_call | solution.py:76
  249.3 13.1 %shard_map.95 = (bf16[96,3072]{1,0:T(8,128)(2,1)}, bf16[96,3072]{1,0:T(8,128)(2,1)}) custom-call(bf16[2,96,256]{2,1,0:T(8,128)(2,1)} %copy-done.44, bf16[2,96,256]{2,1,0:T(8,128)(2,1)} %copy-done.45, bf16[2,96,256]{2,1,0:T(8,128)(2,1)} %collective-permute-done.9.refs_2_, ...), custom_call_target="tpu_custom_call", output_to_operand_aliasing={{0}: (4, {}), {1}: (5, {})} | custom-call | bytes 786432 | tf_op jit(solution)/shard_map/pallas_call | solution.py:76
  262.5 13.1 %shard_map.99 = (bf16[96,3072]{1,0:T(8,128)(2,1)}, bf16[96,3072]{1,0:T(8,128)(2,1)}) custom-call(bf16[2,96,256]{2,1,0:T(8,128)(2,1)} %copy-done.58, bf16[2,96,256]{2,1,0:T(8,128)(2,1)} %copy-done.59, bf16[2,96,256]{2,1,0:T(8,128)(2,1)} %copy-done.60, bf16[2,96,256]{2,1,0:T(8,128)(2,1)} %copy-done.61), custom_call_target="tpu_custom_call" | custom-call | bytes 786432 | tf_op jit(solution)/shard_map/pallas_call | solution.py:76
  276.3 13.1 %shard_map.100 = (bf16[96,3072]{1,0:T(8,128)(2,1)}, bf16[96,3072]{1,0:T(8,128)(2,1)}) custom-call(bf16[2,96,256]{2,1,0:T(8,128)(2,1)} %copy-done.46, bf16[2,96,256]{2,1,0:T(8,128)(2,1)} %copy-done.47, bf16[2,96,256]{2,1,0:T(8,128)(2,1)} %copy-done.48, bf16[2,96,256]{2,1,0:T(8,128)(2,1)} %copy-done.52, ...), custom_call_target="tpu_custom_call", output_to_operand_aliasing={{0}: (4, {}), {1}: (5, {})} | custom-call | bytes 786432 | tf_op jit(solution)/shard_map/pallas_call | solution.py:76
  290.1 13.1 %shard_map.101 = (bf16[96,3072]{1,0:T(8,128)(2,1)}, bf16[96,3072]{1,0:T(8,128)(2,1)}) custom-call(bf16[2,96,256]{2,1,0:T(8,128)(2,1)} %copy-done.49, bf16[2,96,256]{2,1,0:T(8,128)(2,1)} %copy-done.50, bf16[2,96,256]{2,1,0:T(8,128)(2,1)} %copy-done.51, bf16[2,96,256]{2,1,0:T(8,128)(2,1)} %copy-done.53, ...), custom_call_target="tpu_custom_call", output_to_operand_aliasing={{0}: (4, {}), {1}: (5, {})} | custom-call | bytes 786432 | tf_op jit(solution)/shard_map/pallas_call | solution.py:76
  (232 shorter events, 61.8 us)
Async XLA Ops:
  0.6 60.1 %collective-permute-start = (s32[6,16]{1,0:T(8,128)}, s32[6,16]{1,0:T(8,128)S(1)}, u32[]{:S(2)}, u32[]{:S(2)}) collective-permute-start(s32[6,16]{1,0:T(8,128)} %param.9), channel_id=1, source_target_pairs={{0,0},{1,4},{2,2},{3,6},{4,1},{5,5},{6,3},{7,7},{8,8},{9,12},{10,1... | collective-permute-start | bytes 1160 | tf_op jit(solution)/shard_map/ppermute | solution.py:197
  27.0 59.7 %collective-permute-start.21 = (bf16[4,96,256]{2,1,0:T(8,128)(2,1)}, bf16[4,96,256]{2,1,0:T(8,128)(2,1)S(1)}, u32[]{:S(2)}, u32[]{:S(2)}) collective-permute-start(bf16[4,96,256]{2,1,0:T(8,128)(2,1)} %get-tuple-element.77), channel_id=1, source_target_pairs={{0,6},{1,2},{2,4},{3,0},{4,7},{5,3},{6,5},{7,1},{8,14},{9,10},{10,... | collective-permute-start | bytes 589832 | tf_op jit(solution)/shard_map/ppermute | solution.py:238
  31.6 55.9 %collective-permute-start.22 = (bf16[4,96,256]{2,1,0:T(8,128)(2,1)}, bf16[4,96,256]{2,1,0:T(8,128)(2,1)S(1)}, u32[]{:S(2)}, u32[]{:S(2)}) collective-permute-start(bf16[4,96,256]{2,1,0:T(8,128)(2,1)} %get-tuple-element.78), channel_id=1, source_target_pairs={{0,0},{1,4},{2,2},{3,6},{4,1},{5,5},{6,3},{7,7},{8,8},{9,12},{10,1... | collective-permute-start | bytes 589832 | tf_op jit(solution)/shard_map/ppermute | solution.py:238
  33.2 55.0 %collective-permute-start.23 = (bf16[4,96,256]{2,1,0:T(8,128)(2,1)}, bf16[4,96,256]{2,1,0:T(8,128)(2,1)S(1)}, u32[]{:S(2)}, u32[]{:S(2)}) collective-permute-start(bf16[4,96,256]{2,1,0:T(8,128)(2,1)} %get-tuple-element.79), channel_id=1, source_target_pairs={{0,2},{1,6},{2,0},{3,4},{4,3},{5,7},{6,1},{7,5},{8,10},{9,14},{10,... | collective-permute-start | bytes 589832 | tf_op jit(solution)/shard_map/ppermute | solution.py:238
  33.7 58.9 %collective-permute-start.24 = (bf16[4,96,256]{2,1,0:T(8,128)(2,1)}, bf16[4,96,256]{2,1,0:T(8,128)(2,1)S(1)}, u32[]{:S(2)}, u32[]{:S(2)}) collective-permute-start(bf16[4,96,256]{2,1,0:T(8,128)(2,1)} %get-tuple-element.80), channel_id=1, source_target_pairs={{0,4},{1,0},{2,6},{3,2},{4,5},{5,1},{6,7},{7,3},{8,12},{9,8},{10,1... | collective-permute-start | bytes 589832 | tf_op jit(solution)/shard_map/ppermute | solution.py:238
  60.7 45.6 %collective-permute-start.11 = (bf16[4,96,256]{2,1,0:T(8,128)(2,1)}, bf16[4,96,256]{2,1,0:T(8,128)(2,1)S(1)}, u32[]{:S(2)}, u32[]{:S(2)}) collective-permute-start(bf16[4,96,256]{2,1,0:T(8,128)(2,1)} %get-tuple-element.69), channel_id=1, source_target_pairs={{0,6},{1,2},{2,4},{3,0},{4,7},{5,3},{6,5},{7,1},{8,14},{9,10},{10,... | collective-permute-start | bytes 589832 | tf_op jit(solution)/shard_map/ppermute | solution.py:238
  86.8 19.7 %collective-permute-start.12 = (bf16[4,96,256]{2,1,0:T(8,128)(2,1)S(1)}, bf16[4,96,256]{2,1,0:T(8,128)(2,1)S(1)}, u32[]{:S(2)}, u32[]{:S(2)}) collective-permute-start(bf16[4,96,256]{2,1,0:T(8,128)(2,1)S(1)} %copy-done.64), channel_id=1, source_target_pairs={{0,0},{1,4},{2,2},{3,6},{4,1},{5,5},{6,3},{7,7},{8,8},{9,12},{10,1... | collective-permute-start | bytes 589832 | tf_op jit(solution)/shard_map/ppermute | solution.py:238
  87.5 20.6 %collective-permute-start.13 = (bf16[4,96,256]{2,1,0:T(8,128)(2,1)S(1)}, bf16[4,96,256]{2,1,0:T(8,128)(2,1)S(1)}, u32[]{:S(2)}, u32[]{:S(2)}) collective-permute-start(bf16[4,96,256]{2,1,0:T(8,128)(2,1)S(1)} %copy-done.63), channel_id=1, source_target_pairs={{0,2},{1,6},{2,0},{3,4},{4,3},{5,7},{6,1},{7,5},{8,10},{9,14},{10,... | collective-permute-start | bytes 589832 | tf_op jit(solution)/shard_map/ppermute | solution.py:238
  88.2 21.4 %collective-permute-start.14 = (bf16[4,96,256]{2,1,0:T(8,128)(2,1)S(1)}, bf16[4,96,256]{2,1,0:T(8,128)(2,1)S(1)}, u32[]{:S(2)}, u32[]{:S(2)}) collective-permute-start(bf16[4,96,256]{2,1,0:T(8,128)(2,1)S(1)} %copy-done.62), channel_id=1, source_target_pairs={{0,4},{1,0},{2,6},{3,2},{4,5},{5,1},{6,7},{7,3},{8,12},{9,8},{10,1... | collective-permute-start | bytes 589832 | tf_op jit(solution)/shard_map/ppermute | solution.py:238
  92.6 18.5 %collective-permute-start.1 = (bf16[4,96,256]{2,1,0:T(8,128)(2,1)}, bf16[4,96,256]{2,1,0:T(8,128)(2,1)S(1)}, u32[]{:S(2)}, u32[]{:S(2)}) collective-permute-start(bf16[4,96,256]{2,1,0:T(8,128)(2,1)} %get-tuple-element.61), channel_id=1, source_target_pairs={{0,6},{1,2},{2,4},{3,0},{4,7},{5,3},{6,5},{7,1},{8,14},{9,10},{10,... | collective-permute-start | bytes 589832 | tf_op jit(solution)/shard_map/ppermute | solution.py:238
  106.4 39.1 %collective-permute-start.25 = (bf16[4,2,96,256]{3,2,1,0:T(8,128)(2,1)}, bf16[4,2,96,256]{3,2,1,0:T(8,128)(2,1)S(1)}, u32[]{:S(2)}, u32[]{:S(2)}) collective-permute-start(bf16[4,2,96,256]{3,2,1,0:T(8,128)(2,1)} %shard_map.91), channel_id=1, source_target_pairs={{0,1},{1,0},{2,3},{3,2},{4,5},{5,4},{6,7},{7,6},{8,9},{9,8},{10,11... | collective-permute-start | bytes 1179656 | tf_op jit(solution)/shard_map/ppermute | solution.py:246
  106.5 19.3 %collective-permute-start.2 = (bf16[4,96,256]{2,1,0:T(8,128)(2,1)}, bf16[4,96,256]{2,1,0:T(8,128)(2,1)S(1)}, u32[]{:S(2)}, u32[]{:S(2)}) collective-permute-start(bf16[4,96,256]{2,1,0:T(8,128)(2,1)} %get-tuple-element.62), channel_id=1, source_target_pairs={{0,0},{1,4},{2,2},{3,6},{4,1},{5,5},{6,3},{7,7},{8,8},{9,12},{10,1... | collective-permute-start | bytes 589832 | tf_op jit(solution)/shard_map/ppermute | solution.py:238
  108.1 20.0 %collective-permute-start.3 = (bf16[4,96,256]{2,1,0:T(8,128)(2,1)}, bf16[4,96,256]{2,1,0:T(8,128)(2,1)S(1)}, u32[]{:S(2)}, u32[]{:S(2)}) collective-permute-start(bf16[4,96,256]{2,1,0:T(8,128)(2,1)} %get-tuple-element.63), channel_id=1, source_target_pairs={{0,2},{1,6},{2,0},{3,4},{4,3},{5,7},{6,1},{7,5},{8,10},{9,14},{10,... | collective-permute-start | bytes 589832 | tf_op jit(solution)/shard_map/ppermute | solution.py:238
  109.6 19.9 %collective-permute-start.4 = (bf16[4,96,256]{2,1,0:T(8,128)(2,1)}, bf16[4,96,256]{2,1,0:T(8,128)(2,1)S(1)}, u32[]{:S(2)}, u32[]{:S(2)}) collective-permute-start(bf16[4,96,256]{2,1,0:T(8,128)(2,1)} %get-tuple-element.64), channel_id=1, source_target_pairs={{0,4},{1,0},{2,6},{3,2},{4,5},{5,1},{6,7},{7,3},{8,12},{9,8},{10,1... | collective-permute-start | bytes 589832 | tf_op jit(solution)/shard_map/ppermute | solution.py:238
  111.1 36.4 %collective-permute-start.26 = (bf16[4,2,96,256]{3,2,1,0:T(8,128)(2,1)}, bf16[4,2,96,256]{3,2,1,0:T(8,128)(2,1)}, u32[]{:S(2)}, u32[]{:S(2)}) collective-permute-start(bf16[4,2,96,256]{3,2,1,0:T(8,128)(2,1)} %shard_map.91), channel_id=1, source_target_pairs={{1,8},{3,10},{5,12},{7,14},{8,1},{9,16},{10,3},{11,18},{12,5},{13,... | collective-permute-start | bytes 1179656 | tf_op jit(solution)/shard_map/ppermute | solution.py:249
  125.8 32.4 %collective-permute-start.15 = (bf16[4,2,96,256]{3,2,1,0:T(8,128)(2,1)}, bf16[4,2,96,256]{3,2,1,0:T(8,128)(2,1)}, u32[]{:S(2)}, u32[]{:S(2)}) collective-permute-start(bf16[4,2,96,256]{3,2,1,0:T(8,128)(2,1)} %shard_map.88), channel_id=1, source_target_pairs={{0,1},{1,0},{2,3},{3,2},{4,5},{5,4},{6,7},{7,6},{8,9},{9,8},{10,11... | collective-permute-start | bytes 1179656 | tf_op jit(solution)/shard_map/ppermute | solution.py:246
  128.0 30.8 %collective-permute-start.16 = (bf16[4,2,96,256]{3,2,1,0:T(8,128)(2,1)}, bf16[4,2,96,256]{3,2,1,0:T(8,128)(2,1)}, u32[]{:S(2)}, u32[]{:S(2)}) collective-permute-start(bf16[4,2,96,256]{3,2,1,0:T(8,128)(2,1)} %shard_map.88), channel_id=1, source_target_pairs={{1,8},{3,10},{5,12},{7,14},{8,1},{9,16},{10,3},{11,18},{12,5},{13,... | collective-permute-start | bytes 1179656 | tf_op jit(solution)/shard_map/ppermute | solution.py:249
  143.2 16.3 %collective-permute-start.5 = (bf16[4,2,96,256]{3,2,1,0:T(8,128)(2,1)}, bf16[4,2,96,256]{3,2,1,0:T(8,128)(2,1)S(1)}, u32[]{:S(2)}, u32[]{:S(2)}) collective-permute-start(bf16[4,2,96,256]{3,2,1,0:T(8,128)(2,1)} %shard_map.85), channel_id=1, source_target_pairs={{0,1},{1,0},{2,3},{3,2},{4,5},{5,4},{6,7},{7,6},{8,9},{9,8},{10,11... | collective-permute-start | bytes 1179656 | tf_op jit(solution)/shard_map/ppermute | solution.py:246
  155.3 40.8 %collective-permute-start.43 = (bf16[4,2,96,256]{3,2,1,0:T(8,128)(2,1)S(1)}, bf16[4,2,96,256]{3,2,1,0:T(8,128)(2,1)S(1)}, u32[]{:S(2)}, u32[]{:S(2)}) collective-permute-start(bf16[4,2,96,256]{3,2,1,0:T(8,128)(2,1)S(1)} %get-tuple-element.106), channel_id=1, source_target_pairs={{0,1},{1,0},{2,3},{3,2},{4,5},{5,4},{6,7},{7,6},{8,9},{9,8},{10,11... | collective-permute-start | bytes 1179656 | tf_op jit(solution)/shard_map/ppermute | solution.py:246
  214.8 60.8 %collective-permute-start.42 = (bf16[2,96,256]{2,1,0:T(8,128)(2,1)}, bf16[2,96,256]{2,1,0:T(8,128)(2,1)S(1)}, u32[]{:S(2)}, u32[]{:S(2)}) collective-permute-start(bf16[2,96,256]{2,1,0:T(8,128)(2,1)} %get-tuple-element.104), channel_id=1, source_target_pairs={{4,0},{0,1},{6,2},{2,3},{5,4},{1,5},{7,6},{3,7},{12,8},{8,9},{14,1... | collective-permute-start | bytes 294920 | tf_op jit(solution)/shard_map/ppermute | solution.py:242
  216.6 72.8 %collective-permute-start.33 = (bf16[2,96,256]{2,1,0:T(8,128)(2,1)}, bf16[2,96,256]{2,1,0:T(8,128)(2,1)S(1)}, u32[]{:S(2)}, u32[]{:S(2)}) collective-permute-start(bf16[2,96,256]{2,1,0:T(8,128)(2,1)} %get-tuple-element.94), channel_id=1, source_target_pairs={{6,0},{2,1},{4,2},{0,3},{7,4},{3,5},{5,6},{1,7},{14,8},{10,9},{12,... | collective-permute-start | bytes 294920 | tf_op jit(solution)/shard_map/ppermute | solution.py:242
  217.3 72.1 %collective-permute-start.34 = (bf16[2,96,256]{2,1,0:T(8,128)(2,1)}, bf16[2,96,256]{2,1,0:T(8,128)(2,1)S(1)}, u32[]{:S(2)}, u32[]{:S(2)}) collective-permute-start(bf16[2,96,256]{2,1,0:T(8,128)(2,1)} %get-tuple-element.95), channel_id=1, source_target_pairs={{0,0},{4,1},{2,2},{6,3},{1,4},{5,5},{3,6},{7,7},{8,8},{12,9},{10,1... | collective-permute-start | bytes 294920 | tf_op jit(solution)/shard_map/ppermute | solution.py:242
  218.8 70.6 %collective-permute-start.35 = (bf16[2,96,256]{2,1,0:T(8,128)(2,1)}, bf16[2,96,256]{2,1,0:T(8,128)(2,1)S(1)}, u32[]{:S(2)}, u32[]{:S(2)}) collective-permute-start(bf16[2,96,256]{2,1,0:T(8,128)(2,1)} %get-tuple-element.96), channel_id=1, source_target_pairs={{2,0},{6,1},{0,2},{4,3},{3,4},{7,5},{1,6},{5,7},{10,8},{14,9},{8,1... | collective-permute-start | bytes 294920 | tf_op jit(solution)/shard_map/ppermute | solution.py:242
  219.9 69.6 %collective-permute-start.36 = (bf16[2,96,256]{2,1,0:T(8,128)(2,1)}, bf16[2,96,256]{2,1,0:T(8,128)(2,1)S(1)}, u32[]{:S(2)}, u32[]{:S(2)}) collective-permute-start(bf16[2,96,256]{2,1,0:T(8,128)(2,1)} %get-tuple-element.97), channel_id=1, source_target_pairs={{4,0},{0,1},{6,2},{2,3},{5,4},{1,5},{7,6},{3,7},{12,8},{8,9},{14,1... | collective-permute-start | bytes 294920 | tf_op jit(solution)/shard_map/ppermute | solution.py:242
  (90 other events, 1200.1 us)

commit v3 on v2

v3 whole, which is shorter than its diff:
```python
import functools
import math

import jax
import jax.numpy as jnp
from jax import lax
from jax.experimental import pallas as pl
from jax.experimental.pallas import tpu as pltpu
from jax.sharding import Mesh
from jax.sharding import PartitionSpec as P

HD = 128
TILE = 64
MASKED = -1e30
AXES = ("group", "pair", "row", "core")
PLANE = ("pair", "row", "core")
SHIFTS = ((1, 1), (0, 0), (0, 1), (1, 0))
BF16 = jnp.bfloat16
ANY = pl.BlockSpec(memory_space=pl.ANY)


def head_group(shift):
    a, b = shift
    rows = lax.axis_size("row")
    return (lax.axis_index("core") ^ a) * rows + lax.rem(lax.axis_index("row") + b, rows)


MIB = 1024 * 1024


def limit(mib):
    return pltpu.CompilerParams(vmem_limit_bytes=mib * MIB)


def pack_kernel(first, second, *refs):
    messages, held, loads, stores = refs[:4], refs[4], refs[5], refs[6]
    width = held.shape[3]
    ins, outs = [], []
    for i, message in enumerate(messages):
        columns = pl.ds(pl.multiple_of(head_group(SHIFTS[i]) * width, HD), width)
        ins.append([pltpu.make_async_copy(a.at[:, columns], held.at[i, j], loads.at[i, j]) for j, a in enumerate((first, second))])
        outs.append(pltpu.make_async_copy(held.at[i], message, stores.at[i]))
    for pair in ins:
        for copy in pair:
            copy.start()
    for pair, out in zip(ins, outs):
        for copy in pair:
            copy.wait()
        out.start()
    for out in outs:
        out.wait()


def pack(first, second, group_width):
    rows = first.shape[0]
    return pl.pallas_call(
        pack_kernel,
        in_specs=[ANY, ANY],
        out_specs=[ANY] * 4,
        out_shape=[jax.ShapeDtypeStruct((2, rows, group_width), BF16)] * 4,
        scratch_shapes=[
            pltpu.VMEM((4, 2, rows, group_width), BF16),
            pltpu.SemaphoreType.DMA((4, 2)),
            pltpu.SemaphoreType.DMA((4,)),
        ],
        compiler_params=limit(60),
        cost_estimate=pl.CostEstimate(flops=0, bytes_accessed=32 * rows * group_width, transcendentals=0),
    )(first, second)


def unpack_kernel(*refs):
    messages, arrays, held, loads, stores = refs[:4], refs[4:6], refs[6], refs[7], refs[8]
    width = held.shape[3]
    ins, outs = [], []
    for i, message in enumerate(messages):
        columns = pl.ds(pl.multiple_of(head_group(SHIFTS[i]) * width, HD), width)
        ins.append(pltpu.make_async_copy(message, held.at[i], loads.at[i]))
        outs.append([pltpu.make_async_copy(held.at[i, j], a.at[:, columns], stores.at[i, j]) for j, a in enumerate(arrays)])
    for copy in ins:
        copy.start()
    for copy, pair in zip(ins, outs):
        copy.wait()
        for out in pair:
            out.start()
    for pair in outs:
        for out in pair:
            out.wait()


def unpack(messages, full_width):
    _, rows, width = messages[0].shape
    return pl.pallas_call(
        unpack_kernel,
        in_specs=[ANY] * 4,
        out_specs=[ANY] * 2,
        out_shape=[jax.ShapeDtypeStruct((rows, full_width), BF16)] * 2,
        scratch_shapes=[
            pltpu.VMEM((4, 2, rows, width), BF16),
            pltpu.SemaphoreType.DMA((4,)),
            pltpu.SemaphoreType.DMA((4, 2)),
        ],
        compiler_params=limit(4),
        cost_estimate=pl.CostEstimate(flops=0, bytes_accessed=8 * rows * full_width, transcendentals=0),
    )(*messages)


def join_kernel(*refs):
    messages, joined, held, loads, stores = refs[:4], refs[4], refs[5], refs[6], refs[7]
    ins = [pltpu.make_async_copy(m, held.at[i], loads.at[i]) for i, m in enumerate(messages)]
    outs = [pltpu.make_async_copy(held.at[i], joined.at[i], stores.at[i]) for i in range(4)]
    for copy in ins:
        copy.start()
    for copy, out in zip(ins, outs):
        copy.wait()
        out.start()
    for out in outs:
        out.wait()


def join(messages):
    _, rows, width = messages[0].shape
    return pl.pallas_call(
        join_kernel,
        in_specs=[ANY] * 4,
        out_specs=ANY,
        out_shape=jax.ShapeDtypeStruct((4, 2, rows, width), BF16),
        scratch_shapes=[
            pltpu.VMEM((4, 2, rows, width), BF16),
            pltpu.SemaphoreType.DMA((4,)),
            pltpu.SemaphoreType.DMA((4,)),
        ],
        compiler_params=limit(4),
        cost_estimate=pl.CostEstimate(flops=0, bytes_accessed=32 * rows * width, transcendentals=0),
    )(*messages)


def attend_kernel(bias_ref, *refs):
    queries, own_ref, other_ref, halo_ref = refs[:4], refs[4], refs[5], refs[6]
    oq_refs, own_out, other_out, halo_out = refs[7:11], refs[11], refs[12], refs[13]
    scale = 1.0 / math.sqrt(HD)
    log2_scale = scale * math.log2(math.e)
    rows = other_ref.shape[2]
    slab = 4 * rows

    def window(which):
        return jnp.concatenate([ref[:, which].reshape(slab, HD) for ref in (own_ref, other_ref, halo_ref)], axis=0)

    nt = (((1,), (1,)), ((), ()))
    nn = (((1,), (0,)), ((), ()))
    tn = (((0,), (0,)), ((), ()))
    dot = functools.partial(lax.dot_general, preferred_element_type=jnp.float32)
    key_win, val_win = window(0), window(1)
    query = jnp.concatenate([m[0] for m in queries], axis=0)
    grad = jnp.concatenate([m[1] for m in queries], axis=0)
    scores = dot(query, key_win, nt) + bias_ref[...]
    peak = jnp.max(scores, axis=1, keepdims=True)
    weights = jnp.exp2((scores - peak) * log2_scale)
    weights = weights * (1.0 / jnp.sum(weights, axis=1, keepdims=True))
    weights_low = weights.astype(BF16)
    out = dot(weights_low, val_win, nn).astype(BF16)
    out_dot = jnp.sum(grad.astype(jnp.float32) * out.astype(jnp.float32), axis=1, keepdims=True)
    dweights = dot(grad, val_win, nt)
    dscores = (weights * (dweights - out_dot)).astype(BF16)
    dquery = (dot(dscores, key_win, nn) * scale).astype(BF16)
    for i, ref in enumerate(oq_refs):
        ref[0] = out[i * rows : (i + 1) * rows]
        ref[1] = dquery[i * rows : (i + 1) * rows]
    grads = (dot(dscores, query, tn) * scale, dot(weights_low, grad, tn))
    for which, value in enumerate(grads):
        for third, ref in enumerate((own_out, other_out, halo_out)):
            piece = value[third * slab : (third + 1) * slab]
            ref[:, which] = piece.reshape(4, rows, HD).astype(ref.dtype)


def attend(bias, queries, own, other, halo):
    _, rows, width = queries[0].shape
    heads = width // HD
    two = pl.BlockSpec((2, rows, HD), lambda h: (0, 0, h))
    joined = pl.BlockSpec((4, 2, rows, HD), lambda h: (0, 0, 0, h))
    pairs = bias.shape[0] * bias.shape[1] * heads
    shapes = [jax.ShapeDtypeStruct((2, rows, width), BF16)] * 4
    shapes += [jax.ShapeDtypeStruct((4, 2, rows, width), t) for t in (BF16, BF16, BF16)]
    outs = pl.pallas_call(
        attend_kernel,
        grid=(heads,),
        in_specs=[pl.BlockSpec(bias.shape, lambda h: (0, 0))] + [two] * 4 + [joined] * 3,
        out_specs=[two] * 4 + [joined] * 3,
        out_shape=shapes,
        compiler_params=limit(20),
        cost_estimate=pl.CostEstimate(flops=12 * pairs * HD, bytes_accessed=16 * 2**20, transcendentals=pairs),
    )(bias, *queries, own, other, halo)
    return list(outs[:4]), outs[4], outs[5], outs[6]


def total_kernel(own_ref, other_ref, halo_ref, *outs):
    for i, ref in enumerate(outs):
        total = own_ref[i].astype(jnp.float32) + other_ref[i].astype(jnp.float32) + halo_ref[i].astype(jnp.float32)
        ref[...] = total.astype(BF16)


def total(own, other, halo):
    _, _, rows, width = own.shape
    piece = HD * 2
    joined = pl.BlockSpec((4, 2, rows, piece), lambda k: (0, 0, 0, k))
    return pl.pallas_call(
        total_kernel,
        grid=(width // piece,),
        in_specs=[joined] * 3,
        out_specs=[pl.BlockSpec((2, rows, piece), lambda k: (0, 0, k))] * 4,
        out_shape=[jax.ShapeDtypeStruct((2, rows, width), BF16)] * 4,
        compiler_params=limit(8),
        cost_estimate=pl.CostEstimate(flops=own.size * 2, bytes_accessed=own.size * 10, transcendentals=0),
    )(own, other, halo)


def window_bias(neighbours, rows):
    tiles = neighbours.shape[0]
    slab_rows = tiles * TILE
    core = lax.axis_index("core")
    rings = lax.axis_size("row")
    swap = []
    for p in range(2):
        for r in range(rings):
            for c in range(2):
                swap.append(((p * rings + r) * 2 + c, (c * rings + r) * 2 + p))
    ids = lax.ppermute(neighbours, PLANE, swap)
    slab = lax.axis_index("group") * 2 + core
    window_ids = (slab - 1) * tiles + jnp.arange(3 * tiles, dtype=jnp.int32)
    listed = jnp.any((ids[:, :, None] == window_ids[None, None, :]) & (ids[:, :, None] >= 0), axis=1)
    blocks = []
    for a, b in SHIFTS:
        source_row = lax.rem(lax.axis_index("row") - b + rings, rings)
        blocks.append(source_row * 2 + (lax.axis_index("pair") ^ a))
    token = (jnp.stack(blocks)[:, None] * rows + jnp.arange(rows, dtype=jnp.int32)[None, :]).reshape(slab_rows)
    tile = token // TILE
    other = jnp.where(core == 0, 2 * tiles, 0)
    columns = jnp.concatenate([tile + tiles, tile + other, tile + 2 * tiles - other])
    pick_rows = (tile[:, None] == jnp.arange(tiles)[None, :]).astype(BF16)
    pick_columns = (jnp.arange(3 * tiles)[:, None] == columns[None, :]).astype(BF16)
    spread = jnp.dot(listed.astype(BF16), pick_columns)
    allowed = jnp.dot(pick_rows, spread, preferred_element_type=jnp.float32)
    return jnp.where(allowed > 0.5, 0.0, MASKED).astype(jnp.float32)


def per_device(query_in, key_in, value_in, grad_out, neighbours):
    groups, rings = lax.axis_size("group"), lax.axis_size("row")
    rows, full_width = query_in.shape
    group_width = full_width // (2 * rings)

    def place(g, p, r, c):
        return ((g * 2 + p) * rings + r) * 2 + c

    everyone = [(g, p, r, c) for g in range(groups) for p in range(2) for r in range(rings) for c in range(2)]

    def spread_pairs(shift):
        a, b = shift
        return [(place(g, p, r, c), place(g, c ^ a, (r + b) % rings, p)) for g, p, r, c in everyone]

    beside = []
    for g, p, r, c in everyone:
        to = g + 1 if c == 1 else g - 1
        if 0 <= to < groups:
            beside.append((place(g, p, r, c), place(to, p, r, 1 - c)))

    def send(messages):
        return [lax.ppermute(m, AXES, spread_pairs(s)) for m, s in zip(messages, SHIFTS)]

    def send_back(messages):
        return [
            lax.ppermute(m, AXES, [(d, s) for s, d in spread_pairs(shift)]) for m, shift in zip(messages, SHIFTS)
        ]

    def across(x):
        return lax.ppermute(x, "core", [(0, 1), (1, 0)])

    def halo(x):
        return lax.ppermute(x, AXES, beside)

    key_out = pack(key_in, value_in, group_width)
    key_out, query_in, neighbours = lax.optimization_barrier((key_out, query_in, neighbours))
    query_out = pack(query_in, grad_out, group_width)
    bias = window_bias(neighbours, rows)
    own = join(send(key_out))
    query_out, own = lax.optimization_barrier((query_out, own))
    query_out = list(query_out)
    other = across(own)
    other, query_out[3] = lax.optimization_barrier((other, query_out[3]))
    far = halo(own)
    queries = send(query_out)
    oq, own_part, other_part, far_part = attend(bias, queries, own, other, far)
    other_part = across(other_part)
    other_part, oq[3] = lax.optimization_barrier((other_part, oq[3]))
    grads = total(own_part, other_part, halo(far_part))
    forward = unpack(send_back(oq), full_width)
    return *forward, *unpack(send_back(grads), full_width)


def solution(mesh):
    slabs, heads = mesh.devices.shape
    paired = Mesh(mesh.devices.reshape(slabs // 2, 2, heads // 2, 2), AXES)
    tokens = P(AXES, None)
    return jax.shard_map(
        per_device,
        mesh=paired,
        in_specs=(tokens, tokens, tokens, tokens, P(("group", "pair"), None)),
        out_specs=(tokens, tokens, tokens, tokens),
        check_vma=False,
    )
```

time: 304 us -> 96.4 us (0.32)
  Pallas kernels: 216 us -> 24 us
  starting transfers between devices: 72.6 us -> 45.4 us
  waiting for transfers between devices: 2.35 us -> 22.6 us
  local copies, waits for them, and re-layouts: 10.1 us -> 2.38 us
    pallas_call x12 -> x5, Pallas kernels: 160 us -> 7.88 us  [the longest x2 4.38 us: pack(): pl.pallas_call(pack_kernel, in_specs=[ANY, ANY], out_specs=[ANY] * 4, out...]
    pallas_call x3 -> x1, Pallas kernels: 39.1 us -> 0.56 us  [join(): pl.pallas_call(join_kernel, in_specs=[ANY] * 4, out_specs=ANY, out_shape=...]
    ppermute x12 -> x8, waiting for transfers between devices: 0.03 us -> 13 us  [send(): lax.ppermute(m, AXES, spread_pairs(s))]
    ppermute x6 -> x2, starting transfers between devices: 13.1 us -> 2.88 us  [across(): return lax.ppermute(x, 'core', [(0, 1), (1, 0)])]
    ppermute x24 -> x8, starting transfers between devices: 33 us -> 22.8 us  [send_back(): lax.ppermute(m, AXES, [(d, s) for s, d in spread_pairs(shift)])]
    unnamed x130 -> x6, local copies, waits for them, and re-layouts: 10 us -> 2.29 us
    ppermute x24 -> x8, waiting for transfers between devices: 2.28 us -> 9.57 us  [send_back(): lax.ppermute(m, AXES, [(d, s) for s, d in spread_pairs(shift)])]
    ppermute x6 -> x2, starting transfers between devices: 5.52 us -> 2.41 us  [halo(): return lax.ppermute(x, AXES, beside)]
  transfers between devices with their start and end apart: 49 -> 21, of which waited for: 1 -> 9; matrix products, arithmetic and copies ran while one was open for 0% -> 1% of each run, Pallas kernels for 67% -> 5%
where the time goes in v3:
time: 96.4 us; the launch traced here: 96 us
  starting transfers between devices  45.4 us (47%)
  Pallas kernels  24 us (25%)
  waiting for transfers between devices  22.6 us (23%)
  local copies, waits for them, and re-layouts  2.38 us (2%)
    ppermute x8, starting transfers between devices, send_back(): lax.ppermute(m, AXES, [(d, s) for s, d in spread_pairs(shift)])  22.8 us
    ppermute x8, starting transfers between devices, send(): lax.ppermute(m, AXES, spread_pairs(s))  16.7 us
    pallas_call x1, Pallas kernels, attend(): pl.pallas_call(attend_kernel, grid=(heads,), in_specs=[pl.BlockSpec(bias....  15.5 us
    ppermute x8, waiting for transfers between devices, send(): lax.ppermute(m, AXES, spread_pairs(s))  13 us
    ppermute x8, waiting for transfers between devices, send_back(): lax.ppermute(m, AXES, [(d, s) for s, d in spread_pairs(shift)])  9.57 us
    pallas_call x2, Pallas kernels, pack(): pl.pallas_call(pack_kernel, in_specs=[ANY, ANY], out_specs=[ANY] * 4, out...  4.38 us
    ppermute x2, starting transfers between devices, across(): return lax.ppermute(x, 'core', [(0, 1), (1, 0)])  2.88 us
    pallas_call x2, Pallas kernels, unpack(): pl.pallas_call(unpack_kernel, in_specs=[ANY] * 4, out_specs=[ANY] * 2, ou...  2.69 us
  transfers between devices with their start and end apart: 21, of which 9 were waited for; matrix products, arithmetic and copies ran while one was open for 1% of the time, Pallas kernels for 5%

profile of v3, /device:TPU:0, one launch (start us, length us, event | category | flops | bytes accessed | tf_op | source)
XLA Modules:
  0.0 96.0 jit_solution(18024987299221261395)
XLA Ops:
  0.6 2.2 %shard_map.84 = (bf16[2,96,768]{2,1,0:T(8,128)(2,1)}, bf16[2,96,768]{2,1,0:T(8,128)(2,1)}, bf16[2,96,768]{2,1,0:T(8,128)(2,1)}, bf16[2,96,768]{2,1,0:T(8,128)(2,1)}) custom-call(bf16[96,3072]{1,0:T(8,128)(2,1)} %first.1, bf16[96,3072]{1,0:T(8,128)(2,1)} %second.2), custom_call_target="tpu_custom_call" | custom-call | bytes 2359296 | tf_op jit(solution)/shard_map/pallas_call | solution.py:56
  2.8 4.0 %collective-permute-start.1 = (bf16[2,96,768]{2,1,0:T(8,128)(2,1)}, bf16[2,96,768]{2,1,0:T(8,128)(2,1)S(1)}, u32[]{:S(2)}, u32[]{:S(2)}) collective-permute-start(bf16[2,96,768]{2,1,0:T(8,128)(2,1)} %get-tuple-element.52), channel_id=1, source_target_pairs={{0,6},{1,2},{2,4},{3,0},{4,7},{5,3},{6,5},{7,1},{8,14},{9,10},{10,... | collective-permute-start | bytes 884744 | tf_op jit(solution)/shard_map/ppermute | solution.py:266
  6.8 1.6 %collective-permute-start.2 = (bf16[2,96,768]{2,1,0:T(8,128)(2,1)}, bf16[2,96,768]{2,1,0:T(8,128)(2,1)S(1)}, u32[]{:S(2)}, u32[]{:S(2)}) collective-permute-start(bf16[2,96,768]{2,1,0:T(8,128)(2,1)} %get-tuple-element.53), channel_id=1, source_target_pairs={{0,0},{1,4},{2,2},{3,6},{4,1},{5,5},{6,3},{7,7},{8,8},{9,12},{10,1... | collective-permute-start | bytes 884744 | tf_op jit(solution)/shard_map/ppermute | solution.py:266
  8.9 1.6 %collective-permute-start.4 = (bf16[2,96,768]{2,1,0:T(8,128)(2,1)}, bf16[2,96,768]{2,1,0:T(8,128)(2,1)S(1)}, u32[]{:S(2)}, u32[]{:S(2)}) collective-permute-start(bf16[2,96,768]{2,1,0:T(8,128)(2,1)} %get-tuple-element.55), channel_id=1, source_target_pairs={{0,4},{1,0},{2,6},{3,2},{4,5},{5,1},{6,7},{7,3},{8,12},{9,8},{10,1... | collective-permute-start | bytes 884744 | tf_op jit(solution)/shard_map/ppermute | solution.py:266
  11.2 2.2 %shard_map.85 = (bf16[2,96,768]{2,1,0:T(8,128)(2,1)}, bf16[2,96,768]{2,1,0:T(8,128)(2,1)}, bf16[2,96,768]{2,1,0:T(8,128)(2,1)}, bf16[2,96,768]{2,1,0:T(8,128)(2,1)}) custom-call(bf16[96,3072]{1,0:T(8,128)(2,1)} %first.2, bf16[96,3072]{1,0:T(8,128)(2,1)} %second.3), custom_call_target="tpu_custom_call" | custom-call | bytes 2359296 | tf_op jit(solution)/shard_map/pallas_call | solution.py:56
  13.9 3.9 %collective-permute-done.3.refs_2_ = bf16[2,96,768]{2,1,0:T(8,128)(2,1)S(1)} collective-permute-done((bf16[2,96,768]{2,1,0:T(8,128)(2,1)}, bf16[2,96,768]{2,1,0:T(8,128)(2,1)S(1)}, u32[]{:S(2)}, u32[]{:S(2)}) %collective-permute-start.3) | collective-permute-done | bytes 294944 | tf_op jit(solution)/shard_map/ppermute | solution.py:266
  17.8 1.7 %collective-permute-done.4.refs_3_ = bf16[2,96,768]{2,1,0:T(8,128)(2,1)S(1)} collective-permute-done((bf16[2,96,768]{2,1,0:T(8,128)(2,1)}, bf16[2,96,768]{2,1,0:T(8,128)(2,1)S(1)}, u32[]{:S(2)}, u32[]{:S(2)}) %collective-permute-start.4) | collective-permute-done | bytes 294944 | tf_op jit(solution)/shard_map/ppermute | solution.py:266
  20.2 1.5 %collective-permute-start.8 = (bf16[4,2,96,768]{3,2,1,0:T(8,128)(2,1)S(1)}, bf16[4,2,96,768]{3,2,1,0:T(8,128)(2,1)S(1)}, u32[]{:S(2)}, u32[]{:S(2)}) collective-permute-start(bf16[4,2,96,768]{3,2,1,0:T(8,128)(2,1)S(1)} %shard_map.86.refs_4_), channel_id=1, source_target_pairs={{0,1},{1,0},{2,3},{3,2},{4,5},{5,4},{6,7},{7,6},{8,9},{9,8},{10,11... | collective-permute-start | bytes 3538952 | tf_op jit(solution)/shard_map/ppermute | solution.py:274
  21.9 1.7 %collective-permute-start.10 = (bf16[4,2,96,768]{3,2,1,0:T(8,128)(2,1)S(1)}, bf16[4,2,96,768]{3,2,1,0:T(8,128)(2,1)}, u32[]{:S(2)}, u32[]{:S(2)}) collective-permute-start(bf16[4,2,96,768]{3,2,1,0:T(8,128)(2,1)S(1)} %shard_map.86.refs_4_), channel_id=1, source_target_pairs={{1,8},{3,10},{5,12},{7,14},{8,1},{9,16},{10,3},{11,18},{12,5},{13,... | collective-permute-start | bytes 3538952 | tf_op jit(solution)/shard_map/ppermute | solution.py:277
  23.6 3.2 %collective-permute-start.5 = (bf16[2,96,768]{2,1,0:T(8,128)(2,1)}, bf16[2,96,768]{2,1,0:T(8,128)(2,1)S(1)}, u32[]{:S(2)}, u32[]{:S(2)}) collective-permute-start(bf16[2,96,768]{2,1,0:T(8,128)(2,1)} %get-tuple-element.56), channel_id=1, source_target_pairs={{0,6},{1,2},{2,4},{3,0},{4,7},{5,3},{6,5},{7,1},{8,14},{9,10},{10,... | collective-permute-start | bytes 884744 | tf_op jit(solution)/shard_map/ppermute | solution.py:266
  26.9 1.6 %collective-permute-start.6 = (bf16[2,96,768]{2,1,0:T(8,128)(2,1)}, bf16[2,96,768]{2,1,0:T(8,128)(2,1)S(1)}, u32[]{:S(2)}, u32[]{:S(2)}) collective-permute-start(bf16[2,96,768]{2,1,0:T(8,128)(2,1)} %get-tuple-element.57), channel_id=1, source_target_pairs={{0,0},{1,4},{2,2},{3,6},{4,1},{5,5},{6,3},{7,7},{8,8},{9,12},{10,1... | collective-permute-start | bytes 884744 | tf_op jit(solution)/shard_map/ppermute | solution.py:266
  30.0 3.6 %collective-permute-start.9 = (bf16[2,96,768]{2,1,0:T(8,128)(2,1)}, bf16[2,96,768]{2,1,0:T(8,128)(2,1)}, u32[]{:S(2)}, u32[]{:S(2)}) collective-permute-start(bf16[2,96,768]{2,1,0:T(8,128)(2,1)} %get-tuple-element.61), channel_id=1, source_target_pairs={{0,4},{1,0},{2,6},{3,2},{4,5},{5,1},{6,7},{7,3},{8,12},{9,8},{10,1... | collective-permute-start | bytes 884744 | tf_op jit(solution)/shard_map/ppermute | solution.py:266
  34.8 3.0 %collective-permute-done.7.refs_2_ = bf16[2,96,768]{2,1,0:T(8,128)(2,1)} collective-permute-done((bf16[2,96,768]{2,1,0:T(8,128)(2,1)}, bf16[2,96,768]{2,1,0:T(8,128)(2,1)}, u32[]{:S(2)}, u32[]{:S(2)}) %collective-permute-start.7) | collective-permute-done | bytes 294944 | tf_op jit(solution)/shard_map/ppermute | solution.py:266
  37.9 3.3 %collective-permute-done.9.refs_3_ = bf16[2,96,768]{2,1,0:T(8,128)(2,1)} collective-permute-done((bf16[2,96,768]{2,1,0:T(8,128)(2,1)}, bf16[2,96,768]{2,1,0:T(8,128)(2,1)}, u32[]{:S(2)}, u32[]{:S(2)}) %collective-permute-start.9) | collective-permute-done | bytes 294944 | tf_op jit(solution)/shard_map/ppermute | solution.py:266
  42.4 15.5 %shard_map.87 = (bf16[2,96,768]{2,1,0:T(8,128)(2,1)S(1)}, bf16[2,96,768]{2,1,0:T(8,128)(2,1)S(1)}, bf16[2,96,768]{2,1,0:T(8,128)(2,1)S(1)}, bf16[2,96,768]{2,1,0...) custom-call(f32[384,1152]{1,0:T(8,128)S(1)} %fusion.bias_ref, ...), custom_call_target="tpu_custom_call" | custom-call | flops 4076863488 | bytes 16777216 | tf_op jit(solution)/shard_map/pallas_call | solution.py:183
  58.0 1.4 %collective-permute-start.14 = (bf16[4,2,96,768]{3,2,1,0:T(8,128)(2,1)S(1)}, bf16[4,2,96,768]{3,2,1,0:T(8,128)(2,1)S(1)}, u32[]{:S(2)}, u32[]{:S(2)}) collective-permute-start(bf16[4,2,96,768]{3,2,1,0:T(8,128)(2,1)S(1)} %get-tuple-element.66), channel_id=1, source_target_pairs={{0,1},{1,0},{2,3},{3,2},{4,5},{5,4},{6,7},{7,6},{8,9},{9,8},{10,11... | collective-permute-start | bytes 3538952 | tf_op jit(solution)/shard_map/ppermute | solution.py:274
  60.1 3.5 %collective-permute-start.11 = (bf16[2,96,768]{2,1,0:T(8,128)(2,1)S(1)}, bf16[2,96,768]{2,1,0:T(8,128)(2,1)S(1)}, u32[]{:S(2)}, u32[]{:S(2)}) collective-permute-start(bf16[2,96,768]{2,1,0:T(8,128)(2,1)S(1)} %get-tuple-element.63), channel_id=1, source_target_pairs={{6,0},{2,1},{4,2},{0,3},{7,4},{3,5},{5,6},{1,7},{14,8},{10,9},{12,... | collective-permute-start | bytes 884744 | tf_op jit(solution)/shard_map/ppermute | solution.py:270
  65.4 3.5 %collective-permute-start.15 = (bf16[2,96,768]{2,1,0:T(8,128)(2,1)S(1)}, bf16[2,96,768]{2,1,0:T(8,128)(2,1)S(1)}, u32[]{:S(2)}, u32[]{:S(2)}) collective-permute-start(bf16[2,96,768]{2,1,0:T(8,128)(2,1)S(1)} %get-tuple-element.68), channel_id=1, source_target_pairs={{4,0},{0,1},{6,2},{2,3},{5,4},{1,5},{7,6},{3,7},{12,8},{8,9},{14,1... | collective-permute-start | bytes 884744 | tf_op jit(solution)/shard_map/ppermute | solution.py:270
  69.8 8.9 %collective-permute-start.17 = (bf16[2,96,768]{2,1,0:T(8,128)(2,1)S(1)}, bf16[2,96,768]{2,1,0:T(8,128)(2,1)S(1)}, u32[]{:S(2)}, u32[]{:S(2)}) collective-permute-start(bf16[2,96,768]{2,1,0:T(8,128)(2,1)S(1)} %get-tuple-element.74), channel_id=1, source_target_pairs={{6,0},{2,1},{4,2},{0,3},{7,4},{3,5},{5,6},{1,7},{14,8},{10,9},{12,... | collective-permute-start | bytes 884744 | tf_op jit(solution)/shard_map/ppermute | solution.py:270
  80.5 3.3 %collective-permute-start.20 = (bf16[2,96,768]{2,1,0:T(8,128)(2,1)S(1)}, bf16[2,96,768]{2,1,0:T(8,128)(2,1)S(1)}, u32[]{:S(2)}, u32[]{:S(2)}) collective-permute-start(bf16[2,96,768]{2,1,0:T(8,128)(2,1)S(1)} %get-tuple-element.77), channel_id=1, source_target_pairs={{4,0},{0,1},{6,2},{2,3},{5,4},{1,5},{7,6},{3,7},{12,8},{8,9},{14,1... | collective-permute-start | bytes 884744 | tf_op jit(solution)/shard_map/ppermute | solution.py:270
  83.8 1.3 %shard_map.88 = (bf16[96,3072]{1,0:T(8,128)(2,1)}, bf16[96,3072]{1,0:T(8,128)(2,1)}) custom-call(bf16[2,96,768]{2,1,0:T(8,128)(2,1)S(1)} %collective-permute-done.11.refs_0_, bf16[2,96,768]{2,1,0:T(8,128)(2,1)S(1)} %collective-permute-done.12.refs_1_, bf16[2,96,768]{2,1,0:T(8,128)(2,1)S(1)} %collective-permute-done.13.refs_2_, ...), custom_call_target="tpu_custom_call" | custom-call | bytes 2359296 | tf_op jit(solution)/shard_map/pallas_call | solution.py:92
  85.2 7.2 %collective-permute-done.19.refs_2_ = bf16[2,96,768]{2,1,0:T(8,128)(2,1)S(1)} collective-permute-done((bf16[2,96,768]{2,1,0:T(8,128)(2,1)S(1)}, bf16[2,96,768]{2,1,0:T(8,128)(2,1)S(1)}, u32[]{:S(2)}, u32[]{:S(2)}) %collective-permute-start.19) | collective-permute-done | bytes 294944 | tf_op jit(solution)/shard_map/ppermute | solution.py:270
  92.4 2.3 %collective-permute-done.20.refs_3_ = bf16[2,96,768]{2,1,0:T(8,128)(2,1)S(1)} collective-permute-done((bf16[2,96,768]{2,1,0:T(8,128)(2,1)S(1)}, bf16[2,96,768]{2,1,0:T(8,128)(2,1)S(1)}, u32[]{:S(2)}, u32[]{:S(2)}) %collective-permute-start.20) | collective-permute-done | bytes 294944 | tf_op jit(solution)/shard_map/ppermute | solution.py:270
  94.7 1.3 %shard_map.90 = (bf16[96,3072]{1,0:T(8,128)(2,1)}, bf16[96,3072]{1,0:T(8,128)(2,1)}) custom-call(bf16[2,96,768]{2,1,0:T(8,128)(2,1)S(1)} %collective-permute-done.17.refs_0_, bf16[2,96,768]{2,1,0:T(8,128)(2,1)S(1)} %collective-permute-done.18.refs_1_, bf16[2,96,768]{2,1,0:T(8,128)(2,1)S(1)} %collective-permute-done.19.refs_2_, ...), custom_call_target="tpu_custom_call" | custom-call | bytes 2359296 | tf_op jit(solution)/shard_map/pallas_call | solution.py:92
  (41 shorter events, 11.7 us)
Async XLA Ops:
  0.6 9.9 %copy-start.2 = (s32[6,16]{1,0:T(8,128)S(1)}, s32[6,16]{1,0:T(8,128)}, u32[]{:S(2)}) copy-start(s32[6,16]{1,0:T(8,128)} %param.9) | copy-start | bytes 1156
  2.8 11.1 %collective-permute-start.1 = (bf16[2,96,768]{2,1,0:T(8,128)(2,1)}, bf16[2,96,768]{2,1,0:T(8,128)(2,1)S(1)}, u32[]{:S(2)}, u32[]{:S(2)}) collective-permute-start(bf16[2,96,768]{2,1,0:T(8,128)(2,1)} %get-tuple-element.52), channel_id=1, source_target_pairs={{0,6},{1,2},{2,4},{3,0},{4,7},{5,3},{6,5},{7,1},{8,14},{9,10},{10,... | collective-permute-start | bytes 884744 | tf_op jit(solution)/shard_map/ppermute | solution.py:266
  6.8 7.1 %collective-permute-start.2 = (bf16[2,96,768]{2,1,0:T(8,128)(2,1)}, bf16[2,96,768]{2,1,0:T(8,128)(2,1)S(1)}, u32[]{:S(2)}, u32[]{:S(2)}) collective-permute-start(bf16[2,96,768]{2,1,0:T(8,128)(2,1)} %get-tuple-element.53), channel_id=1, source_target_pairs={{0,0},{1,4},{2,2},{3,6},{4,1},{5,5},{6,3},{7,7},{8,8},{9,12},{10,1... | collective-permute-start | bytes 884744 | tf_op jit(solution)/shard_map/ppermute | solution.py:266
  8.4 9.4 %collective-permute-start.3 = (bf16[2,96,768]{2,1,0:T(8,128)(2,1)}, bf16[2,96,768]{2,1,0:T(8,128)(2,1)S(1)}, u32[]{:S(2)}, u32[]{:S(2)}) collective-permute-start(bf16[2,96,768]{2,1,0:T(8,128)(2,1)} %get-tuple-element.54), channel_id=1, source_target_pairs={{0,2},{1,6},{2,0},{3,4},{4,3},{5,7},{6,1},{7,5},{8,10},{9,14},{10,... | collective-permute-start | bytes 884744 | tf_op jit(solution)/shard_map/ppermute | solution.py:266
  8.9 10.7 %collective-permute-start.4 = (bf16[2,96,768]{2,1,0:T(8,128)(2,1)}, bf16[2,96,768]{2,1,0:T(8,128)(2,1)S(1)}, u32[]{:S(2)}, u32[]{:S(2)}) collective-permute-start(bf16[2,96,768]{2,1,0:T(8,128)(2,1)} %get-tuple-element.55), channel_id=1, source_target_pairs={{0,4},{1,0},{2,6},{3,2},{4,5},{5,1},{6,7},{7,3},{8,12},{9,8},{10,1... | collective-permute-start | bytes 884744 | tf_op jit(solution)/shard_map/ppermute | solution.py:266
  10.5 13.1 %collective-permute-start = (s32[6,16]{1,0:T(8,128)S(1)}, s32[6,16]{1,0:T(8,128)S(1)}, u32[]{:S(2)}, u32[]{:S(2)}) collective-permute-start(s32[6,16]{1,0:T(8,128)S(1)} %copy-done.2), channel_id=1, source_target_pairs={{0,0},{1,4},{2,2},{3,6},{4,1},{5,5},{6,3},{7,7},{8,8},{9,12},{10,1... | collective-permute-start | bytes 1160 | tf_op jit(solution)/shard_map/ppermute | solution.py:226
  20.2 8.8 %collective-permute-start.8 = (bf16[4,2,96,768]{3,2,1,0:T(8,128)(2,1)S(1)}, bf16[4,2,96,768]{3,2,1,0:T(8,128)(2,1)S(1)}, u32[]{:S(2)}, u32[]{:S(2)}) collective-permute-start(bf16[4,2,96,768]{3,2,1,0:T(8,128)(2,1)S(1)} %shard_map.86.refs_4_), channel_id=1, source_target_pairs={{0,1},{1,0},{2,3},{3,2},{4,5},{5,4},{6,7},{7,6},{8,9},{9,8},{10,11... | collective-permute-start | bytes 3538952 | tf_op jit(solution)/shard_map/ppermute | solution.py:274
  21.9 16.0 %collective-permute-start.10 = (bf16[4,2,96,768]{3,2,1,0:T(8,128)(2,1)S(1)}, bf16[4,2,96,768]{3,2,1,0:T(8,128)(2,1)}, u32[]{:S(2)}, u32[]{:S(2)}) collective-permute-start(bf16[4,2,96,768]{3,2,1,0:T(8,128)(2,1)S(1)} %shard_map.86.refs_4_), channel_id=1, source_target_pairs={{1,8},{3,10},{5,12},{7,14},{8,1},{9,16},{10,3},{11,18},{12,5},{13,... | collective-permute-start | bytes 3538952 | tf_op jit(solution)/shard_map/ppermute | solution.py:277
  23.6 11.2 %collective-permute-start.5 = (bf16[2,96,768]{2,1,0:T(8,128)(2,1)}, bf16[2,96,768]{2,1,0:T(8,128)(2,1)S(1)}, u32[]{:S(2)}, u32[]{:S(2)}) collective-permute-start(bf16[2,96,768]{2,1,0:T(8,128)(2,1)} %get-tuple-element.56), channel_id=1, source_target_pairs={{0,6},{1,2},{2,4},{3,0},{4,7},{5,3},{6,5},{7,1},{8,14},{9,10},{10,... | collective-permute-start | bytes 884744 | tf_op jit(solution)/shard_map/ppermute | solution.py:266
  26.9 8.0 %collective-permute-start.6 = (bf16[2,96,768]{2,1,0:T(8,128)(2,1)}, bf16[2,96,768]{2,1,0:T(8,128)(2,1)S(1)}, u32[]{:S(2)}, u32[]{:S(2)}) collective-permute-start(bf16[2,96,768]{2,1,0:T(8,128)(2,1)} %get-tuple-element.57), channel_id=1, source_target_pairs={{0,0},{1,4},{2,2},{3,6},{4,1},{5,5},{6,3},{7,7},{8,8},{9,12},{10,1... | collective-permute-start | bytes 884744 | tf_op jit(solution)/shard_map/ppermute | solution.py:266
  28.5 9.4 %collective-permute-start.7 = (bf16[2,96,768]{2,1,0:T(8,128)(2,1)}, bf16[2,96,768]{2,1,0:T(8,128)(2,1)}, u32[]{:S(2)}, u32[]{:S(2)}) collective-permute-start(bf16[2,96,768]{2,1,0:T(8,128)(2,1)} %get-tuple-element.58), channel_id=1, source_target_pairs={{0,2},{1,6},{2,0},{3,4},{4,3},{5,7},{6,1},{7,5},{8,10},{9,14},{10,... | collective-permute-start | bytes 884744 | tf_op jit(solution)/shard_map/ppermute | solution.py:266
  29.0 1.0 %copy-start = (bf16[4,2,96,768]{3,2,1,0:T(8,128)(2,1)}, bf16[4,2,96,768]{3,2,1,0:T(8,128)(2,1)S(1)}, u32[]{:S(2)}) copy-start(bf16[4,2,96,768]{3,2,1,0:T(8,128)(2,1)S(1)} %collective-permute-done.8.refs_5_) | copy-start | bytes 3538948
  30.0 11.1 %collective-permute-start.9 = (bf16[2,96,768]{2,1,0:T(8,128)(2,1)}, bf16[2,96,768]{2,1,0:T(8,128)(2,1)}, u32[]{:S(2)}, u32[]{:S(2)}) collective-permute-start(bf16[2,96,768]{2,1,0:T(8,128)(2,1)} %get-tuple-element.61), channel_id=1, source_target_pairs={{0,4},{1,0},{2,6},{3,2},{4,5},{5,1},{6,7},{7,3},{8,12},{9,8},{10,1... | collective-permute-start | bytes 884744 | tf_op jit(solution)/shard_map/ppermute | solution.py:266
  41.2 1.3 %copy-start.1 = (bf16[4,2,96,768]{3,2,1,0:T(8,128)(2,1)S(1)}, bf16[4,2,96,768]{3,2,1,0:T(8,128)(2,1)}, u32[]{:S(2)}) copy-start(bf16[4,2,96,768]{3,2,1,0:T(8,128)(2,1)} %copy-done) | copy-start | bytes 3538948
  58.0 7.4 %collective-permute-start.14 = (bf16[4,2,96,768]{3,2,1,0:T(8,128)(2,1)S(1)}, bf16[4,2,96,768]{3,2,1,0:T(8,128)(2,1)S(1)}, u32[]{:S(2)}, u32[]{:S(2)}) collective-permute-start(bf16[4,2,96,768]{3,2,1,0:T(8,128)(2,1)S(1)} %get-tuple-element.66), channel_id=1, source_target_pairs={{0,1},{1,0},{2,3},{3,2},{4,5},{5,4},{6,7},{7,6},{8,9},{9,8},{10,11... | collective-permute-start | bytes 3538952 | tf_op jit(solution)/shard_map/ppermute | solution.py:274
  59.4 9.6 %collective-permute-start.16 = (bf16[4,2,96,768]{3,2,1,0:T(8,128)(2,1)S(1)}, bf16[4,2,96,768]{3,2,1,0:T(8,128)(2,1)S(1)}, u32[]{:S(2)}, u32[]{:S(2)}) collective-permute-start(bf16[4,2,96,768]{3,2,1,0:T(8,128)(2,1)S(1)} %get-tuple-element.73), channel_id=1, source_target_pairs={{1,8},{3,10},{5,12},{7,14},{8,1},{9,16},{10,3},{11,18},{12,5},{13,... | collective-permute-start | bytes 3538952 | tf_op jit(solution)/shard_map/ppermute | solution.py:277
  60.1 18.6 %collective-permute-start.11 = (bf16[2,96,768]{2,1,0:T(8,128)(2,1)S(1)}, bf16[2,96,768]{2,1,0:T(8,128)(2,1)S(1)}, u32[]{:S(2)}, u32[]{:S(2)}) collective-permute-start(bf16[2,96,768]{2,1,0:T(8,128)(2,1)S(1)} %get-tuple-element.63), channel_id=1, source_target_pairs={{6,0},{2,1},{4,2},{0,3},{7,4},{3,5},{5,6},{1,7},{14,8},{10,9},{12,... | collective-permute-start | bytes 884744 | tf_op jit(solution)/shard_map/ppermute | solution.py:270
  63.6 15.7 %collective-permute-start.12 = (bf16[2,96,768]{2,1,0:T(8,128)(2,1)S(1)}, bf16[2,96,768]{2,1,0:T(8,128)(2,1)S(1)}, u32[]{:S(2)}, u32[]{:S(2)}) collective-permute-start(bf16[2,96,768]{2,1,0:T(8,128)(2,1)S(1)} %get-tuple-element.64), channel_id=1, source_target_pairs={{0,0},{4,1},{2,2},{6,3},{1,4},{5,5},{3,6},{7,7},{8,8},{12,9},{10,1... | collective-permute-start | bytes 884744 | tf_op jit(solution)/shard_map/ppermute | solution.py:270
  64.3 16.2 %collective-permute-start.13 = (bf16[2,96,768]{2,1,0:T(8,128)(2,1)S(1)}, bf16[2,96,768]{2,1,0:T(8,128)(2,1)S(1)}, u32[]{:S(2)}, u32[]{:S(2)}) collective-permute-start(bf16[2,96,768]{2,1,0:T(8,128)(2,1)S(1)} %get-tuple-element.65), channel_id=1, source_target_pairs={{2,0},{6,1},{0,2},{4,3},{3,4},{7,5},{1,6},{5,7},{10,8},{14,9},{8,1... | collective-permute-start | bytes 884744 | tf_op jit(solution)/shard_map/ppermute | solution.py:270
  65.4 18.4 %collective-permute-start.15 = (bf16[2,96,768]{2,1,0:T(8,128)(2,1)S(1)}, bf16[2,96,768]{2,1,0:T(8,128)(2,1)S(1)}, u32[]{:S(2)}, u32[]{:S(2)}) collective-permute-start(bf16[2,96,768]{2,1,0:T(8,128)(2,1)S(1)} %get-tuple-element.68), channel_id=1, source_target_pairs={{4,0},{0,1},{6,2},{2,3},{5,4},{1,5},{7,6},{3,7},{12,8},{8,9},{14,1... | collective-permute-start | bytes 884744 | tf_op jit(solution)/shard_map/ppermute | solution.py:270
  69.8 15.5 %collective-permute-start.17 = (bf16[2,96,768]{2,1,0:T(8,128)(2,1)S(1)}, bf16[2,96,768]{2,1,0:T(8,128)(2,1)S(1)}, u32[]{:S(2)}, u32[]{:S(2)}) collective-permute-start(bf16[2,96,768]{2,1,0:T(8,128)(2,1)S(1)} %get-tuple-element.74), channel_id=1, source_target_pairs={{6,0},{2,1},{4,2},{0,3},{7,4},{3,5},{5,6},{1,7},{14,8},{10,9},{12,... | collective-permute-start | bytes 884744 | tf_op jit(solution)/shard_map/ppermute | solution.py:270
  78.7 6.6 %collective-permute-start.18 = (bf16[2,96,768]{2,1,0:T(8,128)(2,1)S(1)}, bf16[2,96,768]{2,1,0:T(8,128)(2,1)S(1)}, u32[]{:S(2)}, u32[]{:S(2)}) collective-permute-start(bf16[2,96,768]{2,1,0:T(8,128)(2,1)S(1)} %get-tuple-element.75), channel_id=1, source_target_pairs={{0,0},{4,1},{2,2},{6,3},{1,4},{5,5},{3,6},{7,7},{8,8},{12,9},{10,1... | collective-permute-start | bytes 884744 | tf_op jit(solution)/shard_map/ppermute | solution.py:270
  79.4 13.0 %collective-permute-start.19 = (bf16[2,96,768]{2,1,0:T(8,128)(2,1)S(1)}, bf16[2,96,768]{2,1,0:T(8,128)(2,1)S(1)}, u32[]{:S(2)}, u32[]{:S(2)}) collective-permute-start(bf16[2,96,768]{2,1,0:T(8,128)(2,1)S(1)} %get-tuple-element.76), channel_id=1, source_target_pairs={{2,0},{6,1},{0,2},{4,3},{3,4},{7,5},{1,6},{5,7},{10,8},{14,9},{8,1... | collective-permute-start | bytes 884744 | tf_op jit(solution)/shard_map/ppermute | solution.py:270
  80.5 14.2 %collective-permute-start.20 = (bf16[2,96,768]{2,1,0:T(8,128)(2,1)S(1)}, bf16[2,96,768]{2,1,0:T(8,128)(2,1)S(1)}, u32[]{:S(2)}, u32[]{:S(2)}) collective-permute-start(bf16[2,96,768]{2,1,0:T(8,128)(2,1)S(1)} %get-tuple-element.77), channel_id=1, source_target_pairs={{4,0},{0,1},{6,2},{2,3},{5,4},{1,5},{7,6},{3,7},{12,8},{8,9},{14,1... | collective-permute-start | bytes 884744 | tf_op jit(solution)/shard_map/ppermute | solution.py:270

commit v4 on v3

--- a/solution.py
+++ b/solution.py
@@ -11,6 +11,8 @@
 
 HD = 128
 TILE = 64
+EARLY = 1
+ABREAST = 2
 MASKED = -1e30
 AXES = ("group", "pair", "row", "core")
 PLANE = ("pair", "row", "core")
@@ -135,59 +137,69 @@
 
 
 def attend_kernel(bias_ref, *refs):
-    queries, own_ref, other_ref, halo_ref = refs[:4], refs[4], refs[5], refs[6]
-    oq_refs, own_out, other_out, halo_out = refs[7:11], refs[11], refs[12], refs[13]
+    queries, windows = refs[:4], refs[4:7]
+    oq_refs, grad_refs = refs[7:11], refs[11:14]
     scale = 1.0 / math.sqrt(HD)
     log2_scale = scale * math.log2(math.e)
-    rows = other_ref.shape[2]
+    rows = queries[0].shape[1]
     slab = 4 * rows
-
-    def window(which):
-        return jnp.concatenate([ref[:, which].reshape(slab, HD) for ref in (own_ref, other_ref, halo_ref)], axis=0)
+    heads = [slice(h * HD, (h + 1) * HD) for h in range(ABREAST)]
+
+    def window(which, head):
+        return jnp.concatenate([ref[:, which, :, head].reshape(slab, HD) for ref in windows], axis=0)
+
+    def tokens(which, head):
+        return jnp.concatenate([m[which, :, head] for m in queries], axis=0)
+
+    def each(function, *lists):
+        return [function(*one) for one in zip(*lists)]
 
     nt = (((1,), (1,)), ((), ()))
     nn = (((1,), (0,)), ((), ()))
     tn = (((0,), (0,)), ((), ()))
     dot = functools.partial(lax.dot_general, preferred_element_type=jnp.float32)
-    key_win, val_win = window(0), window(1)
-    query = jnp.concatenate([m[0] for m in queries], axis=0)
-    grad = jnp.concatenate([m[1] for m in queries], axis=0)
-    scores = dot(query, key_win, nt) + bias_ref[...]
-    peak = jnp.max(scores, axis=1, keepdims=True)
-    weights = jnp.exp2((scores - peak) * log2_scale)
-    weights = weights * (1.0 / jnp.sum(weights, axis=1, keepdims=True))
-    weights_low = weights.astype(BF16)
-    out = dot(weights_low, val_win, nn).astype(BF16)
-    out_dot = jnp.sum(grad.astype(jnp.float32) * out.astype(jnp.float32), axis=1, keepdims=True)
-    dweights = dot(grad, val_win, nt)
-    dscores = (weights * (dweights - out_dot)).astype(BF16)
-    dquery = (dot(dscores, key_win, nn) * scale).astype(BF16)
-    for i, ref in enumerate(oq_refs):
-        ref[0] = out[i * rows : (i + 1) * rows]
-        ref[1] = dquery[i * rows : (i + 1) * rows]
-    grads = (dot(dscores, query, tn) * scale, dot(weights_low, grad, tn))
-    for which, value in enumerate(grads):
-        for third, ref in enumerate((own_out, other_out, halo_out)):
-            piece = value[third * slab : (third + 1) * slab]
-            ref[:, which] = piece.reshape(4, rows, HD).astype(ref.dtype)
+    keys, vals = [window(0, h) for h in heads], [window(1, h) for h in heads]
+    query, grad = [tokens(0, h) for h in heads], [tokens(1, h) for h in heads]
+    scores = each(lambda q, k: dot(q, k, nt) + bias_ref[...], query, keys)
+    dweights = each(lambda g, v: dot(g, v, nt), grad, vals)
+    peak = each(lambda s: jnp.max(s, axis=1, keepdims=True), scores)
+    weights = each(lambda s, m: jnp.exp2((s - m) * log2_scale), scores, peak)
+    weights = each(lambda w: w * (1.0 / jnp.sum(w, axis=1, keepdims=True)), weights)
+    weights_low = each(lambda w: w.astype(BF16), weights)
+    out = each(lambda w, v: dot(w, v, nn).astype(BF16), weights_low, vals)
+    out_dot = each(
+        lambda g, o: jnp.sum(g.astype(jnp.float32) * o.astype(jnp.float32), axis=1, keepdims=True), grad, out
+    )
+    dscores = each(lambda w, d, o: (w * (d - o)).astype(BF16), weights, dweights, out_dot)
+    for h, head in enumerate(heads):
+        dquery = (dot(dscores[h], keys[h], nn) * scale).astype(BF16)
+        for i, ref in enumerate(oq_refs):
+            ref[0, :, head] = out[h][i * rows : (i + 1) * rows]
+            ref[1, :, head] = dquery[i * rows : (i + 1) * rows]
+        grads = (dot(dscores[h], query[h], tn) * scale, dot(weights_low[h], grad[h], tn))
+        for which, value in enumerate(grads):
+            for third, ref in enumerate(grad_refs):
+                piece = value[third * slab : (third + 1) * slab]
+                ref[:, which, :, head] = piece.reshape(4, rows, HD).astype(BF16)
 
 
 def attend(bias, queries, own, other, halo):
-    _, rows, width = queries[0].shape
+    _, _, rows, width = own.shape
     heads = width // HD
-    two = pl.BlockSpec((2, rows, HD), lambda h: (0, 0, h))
-    joined = pl.BlockSpec((4, 2, rows, HD), lambda h: (0, 0, 0, h))
+    block = ABREAST * HD
+    two = pl.BlockSpec((2, rows, block), lambda h: (0, 0, h))
+    joined = pl.BlockSpec((4, 2, rows, block), lambda h: (0, 0, 0, h))
     pairs = bias.shape[0] * bias.shape[1] * heads
     shapes = [jax.ShapeDtypeStruct((2, rows, width), BF16)] * 4
-    shapes += [jax.ShapeDtypeStruct((4, 2, rows, width), t) for t in (BF16, BF16, BF16)]
+    shapes += [jax.ShapeDtypeStruct((4, 2, rows, width), BF16)] * 3
     outs = pl.pallas_call(
         attend_kernel,
-        grid=(heads,),
+        grid=(heads // ABREAST,),
         in_specs=[pl.BlockSpec(bias.shape, lambda h: (0, 0))] + [two] * 4 + [joined] * 3,
         out_specs=[two] * 4 + [joined] * 3,
         out_shape=shapes,
-        compiler_params=limit(20),
-        cost_estimate=pl.CostEstimate(flops=12 * pairs * HD, bytes_accessed=16 * 2**20, transcendentals=pairs),
+        compiler_params=limit(40),
+        cost_estimate=pl.CostEstimate(flops=12 * pairs * HD, bytes_accessed=16 * MIB, transcendentals=pairs),
     )(bias, *queries, own, other, halo)
     return list(outs[:4]), outs[4], outs[5], outs[6]
 
@@ -213,33 +225,52 @@
     )(own, other, halo)
 
 
-def window_bias(neighbours, rows):
-    tiles = neighbours.shape[0]
-    slab_rows = tiles * TILE
-    core = lax.axis_index("core")
+def bias_kernel(rows, ids_ref, bias_ref):
+    tiles, entries = ids_ref.shape
+    rings = lax.axis_size("row")
+    core, pair, row = lax.axis_index("core"), lax.axis_index("pair"), lax.axis_index("row")
+    first = (lax.axis_index("group") * 2 + core - 1) * tiles
+    near = jnp.where(core == 0, 2 * tiles, 0)
+    blocks = [lax.rem(row - b + rings, rings) * 2 + (pair ^ a) for a, b in SHIFTS]
+    token = lax.broadcasted_iota(jnp.int32, (1, rows), 1)
+    own = jnp.concatenate([(token + block * rows) // TILE for block in blocks], axis=1)
+    columns = jnp.concatenate([own + tiles, own + near, own + 2 * tiles - near], axis=1) + first
+    lists = []
+    for t in range(tiles):
+        listed = columns < 0
+        for n in range(entries):
+            key = ids_ref[t, n]
+            listed = listed | (columns == jnp.where(key >= 0, key, -7 * tiles))
+        lists.append(jnp.where(listed & (columns >= 0), 0.0, MASKED))
+    token = lax.broadcasted_iota(jnp.int32, (rows, 1), 0)
+    for i, block in enumerate(blocks):
+        tile = (token + block * rows) // TILE
+        bias = jnp.broadcast_to(lists[0], (rows, columns.shape[1]))
+        for t in range(1, tiles):
+            bias = jnp.where(tile == t, lists[t], bias)
+        bias_ref[i * rows : (i + 1) * rows] = bias
+
+
+def slab_ids(neighbours):
     rings = lax.axis_size("row")
     swap = []
     for p in range(2):
         for r in range(rings):
             for c in range(2):
                 swap.append(((p * rings + r) * 2 + c, (c * rings + r) * 2 + p))
-    ids = lax.ppermute(neighbours, PLANE, swap)
-    slab = lax.axis_index("group") * 2 + core
-    window_ids = (slab - 1) * tiles + jnp.arange(3 * tiles, dtype=jnp.int32)
-    listed = jnp.any((ids[:, :, None] == window_ids[None, None, :]) & (ids[:, :, None] >= 0), axis=1)
-    blocks = []
-    for a, b in SHIFTS:
-        source_row = lax.rem(lax.axis_index("row") - b + rings, rings)
-        blocks.append(source_row * 2 + (lax.axis_index("pair") ^ a))
-    token = (jnp.stack(blocks)[:, None] * rows + jnp.arange(rows, dtype=jnp.int32)[None, :]).reshape(slab_rows)
-    tile = token // TILE
-    other = jnp.where(core == 0, 2 * tiles, 0)
-    columns = jnp.concatenate([tile + tiles, tile + other, tile + 2 * tiles - other])
-    pick_rows = (tile[:, None] == jnp.arange(tiles)[None, :]).astype(BF16)
-    pick_columns = (jnp.arange(3 * tiles)[:, None] == columns[None, :]).astype(BF16)
-    spread = jnp.dot(listed.astype(BF16), pick_columns)
-    allowed = jnp.dot(pick_rows, spread, preferred_element_type=jnp.float32)
-    return jnp.where(allowed > 0.5, 0.0, MASKED).astype(jnp.float32)
+    return lax.ppermute(neighbours, PLANE, swap)
+
+
+def window_bias(ids, rows):
+    slab = 4 * rows
+    return pl.pallas_call(
+        functools.partial(bias_kernel, rows),
+        in_specs=[pl.BlockSpec(memory_space=pltpu.SMEM)],
+        out_specs=pl.BlockSpec(memory_space=pltpu.VMEM),
+        out_shape=jax.ShapeDtypeStruct((slab, 3 * slab), jnp.float32),
+        compiler_params=limit(8),
+        cost_estimate=pl.CostEstimate(flops=20 * slab * slab, bytes_accessed=12 * slab * slab, transcendentals=0),
+    )(ids)
 
 
 def per_device(query_in, key_in, value_in, grad_out, neighbours):
@@ -259,8 +290,8 @@
     beside = []
     for g, p, r, c in everyone:
         to = g + 1 if c == 1 else g - 1
-        if 0 <= to < groups:
-            beside.append((place(g, p, r, c), place(to, p, r, 1 - c)))
+        inside = 0 <= to < groups
+        beside.append((place(g, p, r, c), place(to, p, r, 1 - c) if inside else place(g, p, r, c)))
 
     def send(messages):
         return [lax.ppermute(m, AXES, spread_pairs(s)) for m, s in zip(messages, SHIFTS)]
@@ -278,15 +309,15 @@
 
     key_out = pack(key_in, value_in, group_width)
     key_out, query_in, neighbours = lax.optimization_barrier((key_out, query_in, neighbours))
-    query_out = pack(query_in, grad_out, group_width)
-    bias = window_bias(neighbours, rows)
-    own = join(send(key_out))
-    query_out, own = lax.optimization_barrier((query_out, own))
-    query_out = list(query_out)
+    query_out = list(pack(query_in, grad_out, group_width))
+    owns, ids = lax.optimization_barrier((send(key_out), slab_ids(neighbours)))
+    own = join(owns)
+    query_out[EARLY:], own = lax.optimization_barrier((query_out[EARLY:], own))
     other = across(own)
-    other, query_out[3] = lax.optimization_barrier((other, query_out[3]))
+    query_out[3], other = lax.optimization_barrier((query_out[3], other))
     far = halo(own)
     queries = send(query_out)
+    bias = window_bias(ids, rows)
     oq, own_part, other_part, far_part = attend(bias, queries, own, other, far)
     other_part = across(other_part)
     other_part, oq[3] = lax.optimization_barrier((other_part, oq[3]))

time: 96.4 us -> 90.5 us (0.939)
  local copies, waits for them, and re-layouts: 2.38 us -> 0.03 us
  Pallas kernels: 24 us -> 21.9 us
  waiting for transfers between devices: 22.6 us -> 21.2 us
    unnamed x6 -> x10, local copies, waits for them, and re-layouts: 2.29 us -> 0.03 us
    pallas_call x1 -> x2, Pallas kernels: 15.5 us -> 13.4 us  [the longest x1 11.6 us: attend(): pl.pallas_call(attend_kernel, grid=(heads // ABREAST,), in_specs=[pl.Bloc...]
    ppermute x8, waiting for transfers between devices: 13 us -> 11.7 us  [send(): lax.ppermute(m, AXES, spread_pairs(s))]
    ppermute x8, starting transfers between devices: 16.7 us -> 17.7 us  [send(): lax.ppermute(m, AXES, spread_pairs(s))]
  transfers between devices with their start and end apart: 21 -> 21, of which waited for: 9 -> 7; matrix products, arithmetic and copies ran while one was open for 1% -> 0% of each run, Pallas kernels for 5% -> 7%
where the time goes in v4:
time: 90.5 us; the launch traced here: 90.2 us
  starting transfers between devices  46.3 us (51%)
  Pallas kernels  21.9 us (24%)
  waiting for transfers between devices  21.2 us (23%)
    ppermute x8, starting transfers between devices, send_back(): lax.ppermute(m, AXES, [(d, s) for s, d in spread_pairs(shift)])  22.9 us
    ppermute x8, starting transfers between devices, send(): lax.ppermute(m, AXES, spread_pairs(s))  17.7 us
    ppermute x8, waiting for transfers between devices, send(): lax.ppermute(m, AXES, spread_pairs(s))  11.7 us
    pallas_call x1, Pallas kernels, attend(): pl.pallas_call(attend_kernel, grid=(heads // ABREAST,), in_specs=[pl.Bloc...  11.6 us
    ppermute x8, waiting for transfers between devices, send_back(): lax.ppermute(m, AXES, [(d, s) for s, d in spread_pairs(shift)])  9.41 us
    pallas_call x2, Pallas kernels, pack(): pl.pallas_call(pack_kernel, in_specs=[ANY, ANY], out_specs=[ANY] * 4, out...  4.39 us
    ppermute x2, starting transfers between devices, across(): return lax.ppermute(x, 'core', [(0, 1), (1, 0)])  3.51 us
    pallas_call x2, Pallas kernels, unpack(): pl.pallas_call(unpack_kernel, in_specs=[ANY] * 4, out_specs=[ANY] * 2, ou...  2.69 us
  transfers between devices with their start and end apart: 21, of which 7 were waited for; matrix products, arithmetic and copies ran while one was open for 0% of the time, Pallas kernels for 7%

profile of v4, /device:TPU:0, one launch (start us, length us, event | category | flops | bytes accessed | tf_op | source)
XLA Modules:
  0.0 90.2 jit_solution(8286538885087797960)
XLA Ops:
  0.6 2.2 %shard_map.84 = (bf16[2,96,768]{2,1,0:T(8,128)(2,1)}, bf16[2,96,768]{2,1,0:T(8,128)(2,1)}, bf16[2,96,768]{2,1,0:T(8,128)(2,1)}, bf16[2,96,768]{2,1,0:T(8,128)(2,1)}) custom-call(bf16[96,3072]{1,0:T(8,128)(2,1)} %first.1, bf16[96,3072]{1,0:T(8,128)(2,1)} %second.2), custom_call_target="tpu_custom_call" | custom-call | bytes 2359296 | tf_op jit(solution)/shard_map/pallas_call | solution.py:58
  2.9 4.0 %collective-permute-start = (bf16[2,96,768]{2,1,0:T(8,128)(2,1)}, bf16[2,96,768]{2,1,0:T(8,128)(2,1)S(1)}, u32[]{:S(2)}, u32[]{:S(2)}) collective-permute-start(bf16[2,96,768]{2,1,0:T(8,128)(2,1)} %get-tuple-element.50), channel_id=1, source_target_pairs={{0,6},{1,2},{2,4},{3,0},{4,7},{5,3},{6,5},{7,1},{8,14},{9,10},{10,... | collective-permute-start | bytes 884744 | tf_op jit(solution)/shard_map/ppermute | solution.py:297
  6.8 1.6 %collective-permute-start.1 = (bf16[2,96,768]{2,1,0:T(8,128)(2,1)}, bf16[2,96,768]{2,1,0:T(8,128)(2,1)S(1)}, u32[]{:S(2)}, u32[]{:S(2)}) collective-permute-start(bf16[2,96,768]{2,1,0:T(8,128)(2,1)} %get-tuple-element.51), channel_id=1, source_target_pairs={{0,0},{1,4},{2,2},{3,6},{4,1},{5,5},{6,3},{7,7},{8,8},{9,12},{10,1... | collective-permute-start | bytes 884744 | tf_op jit(solution)/shard_map/ppermute | solution.py:297
  8.9 1.6 %collective-permute-start.3 = (bf16[2,96,768]{2,1,0:T(8,128)(2,1)}, bf16[2,96,768]{2,1,0:T(8,128)(2,1)S(1)}, u32[]{:S(2)}, u32[]{:S(2)}) collective-permute-start(bf16[2,96,768]{2,1,0:T(8,128)(2,1)} %get-tuple-element.53), channel_id=1, source_target_pairs={{0,4},{1,0},{2,6},{3,2},{4,5},{5,1},{6,7},{7,3},{8,12},{9,8},{10,1... | collective-permute-start | bytes 884744 | tf_op jit(solution)/shard_map/ppermute | solution.py:297
  11.2 2.2 %shard_map.86 = (bf16[2,96,768]{2,1,0:T(8,128)(2,1)}, bf16[2,96,768]{2,1,0:T(8,128)(2,1)}, bf16[2,96,768]{2,1,0:T(8,128)(2,1)}, bf16[2,96,768]{2,1,0:T(8,128)(2,1)}) custom-call(bf16[96,3072]{1,0:T(8,128)(2,1)} %first.2, bf16[96,3072]{1,0:T(8,128)(2,1)} %second.3), custom_call_target="tpu_custom_call" | custom-call | bytes 2359296 | tf_op jit(solution)/shard_map/pallas_call | solution.py:58
  13.9 3.9 %collective-permute-done.2.refs_2_ = bf16[2,96,768]{2,1,0:T(8,128)(2,1)S(1)} collective-permute-done((bf16[2,96,768]{2,1,0:T(8,128)(2,1)}, bf16[2,96,768]{2,1,0:T(8,128)(2,1)S(1)}, u32[]{:S(2)}, u32[]{:S(2)}) %collective-permute-start.2) | collective-permute-done | bytes 294944 | tf_op jit(solution)/shard_map/ppermute | solution.py:297
  17.8 1.7 %collective-permute-done.3.refs_3_ = bf16[2,96,768]{2,1,0:T(8,128)(2,1)S(1)} collective-permute-done((bf16[2,96,768]{2,1,0:T(8,128)(2,1)}, bf16[2,96,768]{2,1,0:T(8,128)(2,1)S(1)}, u32[]{:S(2)}, u32[]{:S(2)}) %collective-permute-start.3) | collective-permute-done | bytes 294944 | tf_op jit(solution)/shard_map/ppermute | solution.py:297
  20.2 1.5 %collective-permute-start.8 = (bf16[4,2,96,768]{3,2,1,0:T(8,128)(2,1)S(1)}, bf16[4,2,96,768]{3,2,1,0:T(8,128)(2,1)S(1)}, u32[]{:S(2)}, u32[]{:S(2)}) collective-permute-start(bf16[4,2,96,768]{3,2,1,0:T(8,128)(2,1)S(1)} %shard_map.87.refs_4_), channel_id=1, source_target_pairs={{0,1},{1,0},{2,3},{3,2},{4,5},{5,4},{6,7},{7,6},{8,9},{9,8},{10,11... | collective-permute-start | bytes 3538952 | tf_op jit(solution)/shard_map/ppermute | solution.py:305
  22.4 3.2 %collective-permute-start.5 = (bf16[2,96,768]{2,1,0:T(8,128)(2,1)S(1)}, bf16[2,96,768]{2,1,0:T(8,128)(2,1)S(1)}, u32[]{:S(2)}, u32[]{:S(2)}) collective-permute-start(bf16[2,96,768]{2,1,0:T(8,128)(2,1)S(1)} %copy-done.3), channel_id=1, source_target_pairs={{0,6},{1,2},{2,4},{3,0},{4,7},{5,3},{6,5},{7,1},{8,14},{9,10},{10,... | collective-permute-start | bytes 884744 | tf_op jit(solution)/shard_map/ppermute | solution.py:297
  27.0 5.4 %collective-permute-start.9 = (bf16[2,96,768]{2,1,0:T(8,128)(2,1)S(1)}, bf16[2,96,768]{2,1,0:T(8,128)(2,1)S(1)}, u32[]{:S(2)}, u32[]{:S(2)}) collective-permute-start(bf16[2,96,768]{2,1,0:T(8,128)(2,1)S(1)} %copy-done), channel_id=1, source_target_pairs={{0,4},{1,0},{2,6},{3,2},{4,5},{5,1},{6,7},{7,3},{8,12},{9,8},{10,1... | collective-permute-start | bytes 884744 | tf_op jit(solution)/shard_map/ppermute | solution.py:297
  32.5 1.8 %shard_map.85.bias_ref = f32[384,1152]{1,0:T(8,128)S(1)} custom-call(s32[6,16]{1,0:T(8,128)S(1)} %collective-permute-done.4.ids_ref), custom_call_target="tpu_custom_call" | custom-call | flops 2949120 | bytes 1769472 | tf_op jit(solution)/shard_map/pallas_call | solution.py:266
  34.3 2.3 %collective-permute-done.7.refs_2_ = bf16[2,96,768]{2,1,0:T(8,128)(2,1)S(1)} collective-permute-done((bf16[2,96,768]{2,1,0:T(8,128)(2,1)S(1)}, bf16[2,96,768]{2,1,0:T(8,128)(2,1)S(1)}, u32[]{:S(2)}, u32[]{:S(2)}) %collective-permute-start.7) | collective-permute-done | bytes 294944 | tf_op jit(solution)/shard_map/ppermute | solution.py:297
  36.7 3.3 %collective-permute-done.9.refs_3_ = bf16[2,96,768]{2,1,0:T(8,128)(2,1)S(1)} collective-permute-done((bf16[2,96,768]{2,1,0:T(8,128)(2,1)S(1)}, bf16[2,96,768]{2,1,0:T(8,128)(2,1)S(1)}, u32[]{:S(2)}, u32[]{:S(2)}) %collective-permute-start.9) | collective-permute-done | bytes 294944 | tf_op jit(solution)/shard_map/ppermute | solution.py:297
  39.9 11.6 %shard_map.88 = (bf16[2,96,768]{2,1,0:T(8,128)(2,1)S(1)}, bf16[2,96,768]{2,1,0:T(8,128)(2,1)S(1)}, bf16[2,96,768]{2,1,0:T(8,128)(2,1)S(1)}, bf16[2,96,768]{2,1,0...) custom-call(f32[384,1152]{1,0:T(8,128)S(1)} %shard_map.85.bias_ref, ...), custom_call_target="tpu_custom_call" | custom-call | flops 4076863488 | bytes 16777216 | tf_op jit(solution)/shard_map/pallas_call | solution.py:195
  51.5 2.0 %collective-permute-start.14 = (bf16[4,2,96,768]{3,2,1,0:T(8,128)(2,1)S(1)}, bf16[4,2,96,768]{3,2,1,0:T(8,128)(2,1)S(1)}, u32[]{:S(2)}, u32[]{:S(2)}) collective-permute-start(bf16[4,2,96,768]{3,2,1,0:T(8,128)(2,1)S(1)} %get-tuple-element.74), channel_id=1, source_target_pairs={{0,1},{1,0},{2,3},{3,2},{4,5},{5,4},{6,7},{7,6},{8,9},{9,8},{10,11... | collective-permute-start | bytes 3538952 | tf_op jit(solution)/shard_map/ppermute | solution.py:305
  54.3 3.5 %collective-permute-start.11 = (bf16[2,96,768]{2,1,0:T(8,128)(2,1)S(1)}, bf16[2,96,768]{2,1,0:T(8,128)(2,1)S(1)}, u32[]{:S(2)}, u32[]{:S(2)}) collective-permute-start(bf16[2,96,768]{2,1,0:T(8,128)(2,1)S(1)} %get-tuple-element.71), channel_id=1, source_target_pairs={{6,0},{2,1},{4,2},{0,3},{7,4},{3,5},{5,6},{1,7},{14,8},{10,9},{12,... | collective-permute-start | bytes 884744 | tf_op jit(solution)/shard_map/ppermute | solution.py:301
  58.5 1.1 %collective-permute-start.13 = (bf16[2,96,768]{2,1,0:T(8,128)(2,1)S(1)}, bf16[2,96,768]{2,1,0:T(8,128)(2,1)S(1)}, u32[]{:S(2)}, u32[]{:S(2)}) collective-permute-start(bf16[2,96,768]{2,1,0:T(8,128)(2,1)S(1)} %get-tuple-element.73), channel_id=1, source_target_pairs={{2,0},{6,1},{0,2},{4,3},{3,4},{7,5},{1,6},{5,7},{10,8},{14,9},{8,1... | collective-permute-start | bytes 884744 | tf_op jit(solution)/shard_map/ppermute | solution.py:301
  59.6 3.8 %collective-permute-start.15 = (bf16[2,96,768]{2,1,0:T(8,128)(2,1)S(1)}, bf16[2,96,768]{2,1,0:T(8,128)(2,1)S(1)}, u32[]{:S(2)}, u32[]{:S(2)}) collective-permute-start(bf16[2,96,768]{2,1,0:T(8,128)(2,1)S(1)} %get-tuple-element.76), channel_id=1, source_target_pairs={{4,0},{0,1},{6,2},{2,3},{5,4},{1,5},{7,6},{3,7},{12,8},{8,9},{14,1... | collective-permute-start | bytes 884744 | tf_op jit(solution)/shard_map/ppermute | solution.py:301
  64.2 8.7 %collective-permute-start.17 = (bf16[2,96,768]{2,1,0:T(8,128)(2,1)S(1)}, bf16[2,96,768]{2,1,0:T(8,128)(2,1)S(1)}, u32[]{:S(2)}, u32[]{:S(2)}) collective-permute-start(bf16[2,96,768]{2,1,0:T(8,128)(2,1)S(1)} %get-tuple-element.82), channel_id=1, source_target_pairs={{6,0},{2,1},{4,2},{0,3},{7,4},{3,5},{5,6},{1,7},{14,8},{10,9},{12,... | collective-permute-start | bytes 884744 | tf_op jit(solution)/shard_map/ppermute | solution.py:301
  74.6 3.4 %collective-permute-start.20 = (bf16[2,96,768]{2,1,0:T(8,128)(2,1)S(1)}, bf16[2,96,768]{2,1,0:T(8,128)(2,1)S(1)}, u32[]{:S(2)}, u32[]{:S(2)}) collective-permute-start(bf16[2,96,768]{2,1,0:T(8,128)(2,1)S(1)} %get-tuple-element.85), channel_id=1, source_target_pairs={{4,0},{0,1},{6,2},{2,3},{5,4},{1,5},{7,6},{3,7},{12,8},{8,9},{14,1... | collective-permute-start | bytes 884744 | tf_op jit(solution)/shard_map/ppermute | solution.py:301
  78.1 1.3 %shard_map.89 = (bf16[96,3072]{1,0:T(8,128)(2,1)}, bf16[96,3072]{1,0:T(8,128)(2,1)}) custom-call(bf16[2,96,768]{2,1,0:T(8,128)(2,1)S(1)} %collective-permute-done.11.refs_0_, bf16[2,96,768]{2,1,0:T(8,128)(2,1)S(1)} %collective-permute-done.12.refs_1_, bf16[2,96,768]{2,1,0:T(8,128)(2,1)S(1)} %collective-permute-done.13.refs_2_, ...), custom_call_target="tpu_custom_call" | custom-call | bytes 2359296 | tf_op jit(solution)/shard_map/pallas_call | solution.py:94
  79.5 7.4 %collective-permute-done.19.refs_2_ = bf16[2,96,768]{2,1,0:T(8,128)(2,1)S(1)} collective-permute-done((bf16[2,96,768]{2,1,0:T(8,128)(2,1)S(1)}, bf16[2,96,768]{2,1,0:T(8,128)(2,1)S(1)}, u32[]{:S(2)}, u32[]{:S(2)}) %collective-permute-start.19) | collective-permute-done | bytes 294944 | tf_op jit(solution)/shard_map/ppermute | solution.py:301
  86.9 2.0 %collective-permute-done.20.refs_3_ = bf16[2,96,768]{2,1,0:T(8,128)(2,1)S(1)} collective-permute-done((bf16[2,96,768]{2,1,0:T(8,128)(2,1)S(1)}, bf16[2,96,768]{2,1,0:T(8,128)(2,1)S(1)}, u32[]{:S(2)}, u32[]{:S(2)}) %collective-permute-start.20) | collective-permute-done | bytes 294944 | tf_op jit(solution)/shard_map/ppermute | solution.py:301
  88.9 1.3 %shard_map.91 = (bf16[96,3072]{1,0:T(8,128)(2,1)}, bf16[96,3072]{1,0:T(8,128)(2,1)}) custom-call(bf16[2,96,768]{2,1,0:T(8,128)(2,1)S(1)} %collective-permute-done.17.refs_0_, bf16[2,96,768]{2,1,0:T(8,128)(2,1)S(1)} %collective-permute-done.18.refs_1_, bf16[2,96,768]{2,1,0:T(8,128)(2,1)S(1)} %collective-permute-done.19.refs_2_, ...), custom_call_target="tpu_custom_call" | custom-call | bytes 2359296 | tf_op jit(solution)/shard_map/pallas_call | solution.py:94
  (36 shorter events, 8.3 us)
Async XLA Ops:
  2.9 11.1 %collective-permute-start = (bf16[2,96,768]{2,1,0:T(8,128)(2,1)}, bf16[2,96,768]{2,1,0:T(8,128)(2,1)S(1)}, u32[]{:S(2)}, u32[]{:S(2)}) collective-permute-start(bf16[2,96,768]{2,1,0:T(8,128)(2,1)} %get-tuple-element.50), channel_id=1, source_target_pairs={{0,6},{1,2},{2,4},{3,0},{4,7},{5,3},{6,5},{7,1},{8,14},{9,10},{10,... | collective-permute-start | bytes 884744 | tf_op jit(solution)/shard_map/ppermute | solution.py:297
  6.8 7.1 %collective-permute-start.1 = (bf16[2,96,768]{2,1,0:T(8,128)(2,1)}, bf16[2,96,768]{2,1,0:T(8,128)(2,1)S(1)}, u32[]{:S(2)}, u32[]{:S(2)}) collective-permute-start(bf16[2,96,768]{2,1,0:T(8,128)(2,1)} %get-tuple-element.51), channel_id=1, source_target_pairs={{0,0},{1,4},{2,2},{3,6},{4,1},{5,5},{6,3},{7,7},{8,8},{9,12},{10,1... | collective-permute-start | bytes 884744 | tf_op jit(solution)/shard_map/ppermute | solution.py:297
  8.4 9.4 %collective-permute-start.2 = (bf16[2,96,768]{2,1,0:T(8,128)(2,1)}, bf16[2,96,768]{2,1,0:T(8,128)(2,1)S(1)}, u32[]{:S(2)}, u32[]{:S(2)}) collective-permute-start(bf16[2,96,768]{2,1,0:T(8,128)(2,1)} %get-tuple-element.52), channel_id=1, source_target_pairs={{0,2},{1,6},{2,0},{3,4},{4,3},{5,7},{6,1},{7,5},{8,10},{9,14},{10,... | collective-permute-start | bytes 884744 | tf_op jit(solution)/shard_map/ppermute | solution.py:297
  8.9 10.7 %collective-permute-start.3 = (bf16[2,96,768]{2,1,0:T(8,128)(2,1)}, bf16[2,96,768]{2,1,0:T(8,128)(2,1)S(1)}, u32[]{:S(2)}, u32[]{:S(2)}) collective-permute-start(bf16[2,96,768]{2,1,0:T(8,128)(2,1)} %get-tuple-element.53), channel_id=1, source_target_pairs={{0,4},{1,0},{2,6},{3,2},{4,5},{5,1},{6,7},{7,3},{8,12},{9,8},{10,1... | collective-permute-start | bytes 884744 | tf_op jit(solution)/shard_map/ppermute | solution.py:297
  10.6 2.9 %collective-permute-start.4 = (s32[6,16]{1,0:T(8,128)S(1)}, s32[6,16]{1,0:T(8,128)S(1)}, u32[]{:S(2)}, u32[]{:S(2)}) collective-permute-start(s32[6,16]{1,0:T(8,128)S(1)} %copy-done.4), channel_id=1, source_target_pairs={{0,0},{1,4},{2,2},{3,6},{4,1},{5,5},{6,3},{7,7},{8,8},{9,12},{10,1... | collective-permute-start | bytes 1160 | tf_op jit(solution)/shard_map/ppermute | solution.py:261
  13.4 12.2 %copy-start.2 = (bf16[2,96,768]{2,1,0:T(8,128)(2,1)S(1)}, bf16[2,96,768]{2,1,0:T(8,128)(2,1)}, u32[]{:S(2)}) copy-start(bf16[2,96,768]{2,1,0:T(8,128)(2,1)} %get-tuple-element.65) | copy-start | bytes 884740
  13.4 12.9 %copy-start.1 = (bf16[2,96,768]{2,1,0:T(8,128)(2,1)S(1)}, bf16[2,96,768]{2,1,0:T(8,128)(2,1)}, u32[]{:S(2)}) copy-start(bf16[2,96,768]{2,1,0:T(8,128)(2,1)} %get-tuple-element.66) | copy-start | bytes 884740
  13.4 13.6 %copy-start = (bf16[2,96,768]{2,1,0:T(8,128)(2,1)S(1)}, bf16[2,96,768]{2,1,0:T(8,128)(2,1)}, u32[]{:S(2)}) copy-start(bf16[2,96,768]{2,1,0:T(8,128)(2,1)} %get-tuple-element.69) | copy-start | bytes 884740
  20.2 6.9 %collective-permute-start.8 = (bf16[4,2,96,768]{3,2,1,0:T(8,128)(2,1)S(1)}, bf16[4,2,96,768]{3,2,1,0:T(8,128)(2,1)S(1)}, u32[]{:S(2)}, u32[]{:S(2)}) collective-permute-start(bf16[4,2,96,768]{3,2,1,0:T(8,128)(2,1)S(1)} %shard_map.87.refs_4_), channel_id=1, source_target_pairs={{0,1},{1,0},{2,3},{3,2},{4,5},{5,4},{6,7},{7,6},{8,9},{9,8},{10,11... | collective-permute-start | bytes 3538952 | tf_op jit(solution)/shard_map/ppermute | solution.py:305
  21.7 15.0 %collective-permute-start.10 = (bf16[4,2,96,768]{3,2,1,0:T(8,128)(2,1)S(1)}, bf16[4,2,96,768]{3,2,1,0:T(8,128)(2,1)S(1)}, u32[]{:S(2)}, u32[]{:S(2)}) collective-permute-start(bf16[4,2,96,768]{3,2,1,0:T(8,128)(2,1)S(1)} %shard_map.87.refs_4_), channel_id=1, source_target_pairs={{0,0},{1,8},{2,2},{3,10},{4,4},{5,12},{6,6},{7,14},{8,1},{9,16},{1... | collective-permute-start | bytes 3538952 | tf_op jit(solution)/shard_map/ppermute | solution.py:308
  22.4 11.9 %collective-permute-start.5 = (bf16[2,96,768]{2,1,0:T(8,128)(2,1)S(1)}, bf16[2,96,768]{2,1,0:T(8,128)(2,1)S(1)}, u32[]{:S(2)}, u32[]{:S(2)}) collective-permute-start(bf16[2,96,768]{2,1,0:T(8,128)(2,1)S(1)} %copy-done.3), channel_id=1, source_target_pairs={{0,6},{1,2},{2,4},{3,0},{4,7},{5,3},{6,5},{7,1},{8,14},{9,10},{10,... | collective-permute-start | bytes 884744 | tf_op jit(solution)/shard_map/ppermute | solution.py:297
  25.6 8.7 %collective-permute-start.6 = (bf16[2,96,768]{2,1,0:T(8,128)(2,1)S(1)}, bf16[2,96,768]{2,1,0:T(8,128)(2,1)S(1)}, u32[]{:S(2)}, u32[]{:S(2)}) collective-permute-start(bf16[2,96,768]{2,1,0:T(8,128)(2,1)S(1)} %copy-done.2), channel_id=1, source_target_pairs={{0,0},{1,4},{2,2},{3,6},{4,1},{5,5},{6,3},{7,7},{8,8},{9,12},{10,1... | collective-permute-start | bytes 884744 | tf_op jit(solution)/shard_map/ppermute | solution.py:297
  26.3 10.3 %collective-permute-start.7 = (bf16[2,96,768]{2,1,0:T(8,128)(2,1)S(1)}, bf16[2,96,768]{2,1,0:T(8,128)(2,1)S(1)}, u32[]{:S(2)}, u32[]{:S(2)}) collective-permute-start(bf16[2,96,768]{2,1,0:T(8,128)(2,1)S(1)} %copy-done.1), channel_id=1, source_target_pairs={{0,2},{1,6},{2,0},{3,4},{4,3},{5,7},{6,1},{7,5},{8,10},{9,14},{10,... | collective-permute-start | bytes 884744 | tf_op jit(solution)/shard_map/ppermute | solution.py:297
  27.0 12.9 %collective-permute-start.9 = (bf16[2,96,768]{2,1,0:T(8,128)(2,1)S(1)}, bf16[2,96,768]{2,1,0:T(8,128)(2,1)S(1)}, u32[]{:S(2)}, u32[]{:S(2)}) collective-permute-start(bf16[2,96,768]{2,1,0:T(8,128)(2,1)S(1)} %copy-done), channel_id=1, source_target_pairs={{0,4},{1,0},{2,6},{3,2},{4,5},{5,1},{6,7},{7,3},{8,12},{9,8},{10,1... | collective-permute-start | bytes 884744 | tf_op jit(solution)/shard_map/ppermute | solution.py:297
  51.5 8.0 %collective-permute-start.14 = (bf16[4,2,96,768]{3,2,1,0:T(8,128)(2,1)S(1)}, bf16[4,2,96,768]{3,2,1,0:T(8,128)(2,1)S(1)}, u32[]{:S(2)}, u32[]{:S(2)}) collective-permute-start(bf16[4,2,96,768]{3,2,1,0:T(8,128)(2,1)S(1)} %get-tuple-element.74), channel_id=1, source_target_pairs={{0,1},{1,0},{2,3},{3,2},{4,5},{5,4},{6,7},{7,6},{8,9},{9,8},{10,11... | collective-permute-start | bytes 3538952 | tf_op jit(solution)/shard_map/ppermute | solution.py:305
  53.5 9.8 %collective-permute-start.16 = (bf16[4,2,96,768]{3,2,1,0:T(8,128)(2,1)S(1)}, bf16[4,2,96,768]{3,2,1,0:T(8,128)(2,1)S(1)}, u32[]{:S(2)}, u32[]{:S(2)}) collective-permute-start(bf16[4,2,96,768]{3,2,1,0:T(8,128)(2,1)S(1)} %get-tuple-element.81), channel_id=1, source_target_pairs={{0,0},{1,8},{2,2},{3,10},{4,4},{5,12},{6,6},{7,14},{8,1},{9,16},{1... | collective-permute-start | bytes 3538952 | tf_op jit(solution)/shard_map/ppermute | solution.py:308
  54.3 18.6 %collective-permute-start.11 = (bf16[2,96,768]{2,1,0:T(8,128)(2,1)S(1)}, bf16[2,96,768]{2,1,0:T(8,128)(2,1)S(1)}, u32[]{:S(2)}, u32[]{:S(2)}) collective-permute-start(bf16[2,96,768]{2,1,0:T(8,128)(2,1)S(1)} %get-tuple-element.71), channel_id=1, source_target_pairs={{6,0},{2,1},{4,2},{0,3},{7,4},{3,5},{5,6},{1,7},{14,8},{10,9},{12,... | collective-permute-start | bytes 884744 | tf_op jit(solution)/shard_map/ppermute | solution.py:301
  57.8 15.7 %collective-permute-start.12 = (bf16[2,96,768]{2,1,0:T(8,128)(2,1)S(1)}, bf16[2,96,768]{2,1,0:T(8,128)(2,1)S(1)}, u32[]{:S(2)}, u32[]{:S(2)}) collective-permute-start(bf16[2,96,768]{2,1,0:T(8,128)(2,1)S(1)} %get-tuple-element.72), channel_id=1, source_target_pairs={{0,0},{4,1},{2,2},{6,3},{1,4},{5,5},{3,6},{7,7},{8,8},{12,9},{10,1... | collective-permute-start | bytes 884744 | tf_op jit(solution)/shard_map/ppermute | solution.py:301
  58.5 16.2 %collective-permute-start.13 = (bf16[2,96,768]{2,1,0:T(8,128)(2,1)S(1)}, bf16[2,96,768]{2,1,0:T(8,128)(2,1)S(1)}, u32[]{:S(2)}, u32[]{:S(2)}) collective-permute-start(bf16[2,96,768]{2,1,0:T(8,128)(2,1)S(1)} %get-tuple-element.73), channel_id=1, source_target_pairs={{2,0},{6,1},{0,2},{4,3},{3,4},{7,5},{1,6},{5,7},{10,8},{14,9},{8,1... | collective-permute-start | bytes 884744 | tf_op jit(solution)/shard_map/ppermute | solution.py:301
  59.6 18.5 %collective-permute-start.15 = (bf16[2,96,768]{2,1,0:T(8,128)(2,1)S(1)}, bf16[2,96,768]{2,1,0:T(8,128)(2,1)S(1)}, u32[]{:S(2)}, u32[]{:S(2)}) collective-permute-start(bf16[2,96,768]{2,1,0:T(8,128)(2,1)S(1)} %get-tuple-element.76), channel_id=1, source_target_pairs={{4,0},{0,1},{6,2},{2,3},{5,4},{1,5},{7,6},{3,7},{12,8},{8,9},{14,1... | collective-permute-start | bytes 884744 | tf_op jit(solution)/shard_map/ppermute | solution.py:301
  64.2 15.2 %collective-permute-start.17 = (bf16[2,96,768]{2,1,0:T(8,128)(2,1)S(1)}, bf16[2,96,768]{2,1,0:T(8,128)(2,1)S(1)}, u32[]{:S(2)}, u32[]{:S(2)}) collective-permute-start(bf16[2,96,768]{2,1,0:T(8,128)(2,1)S(1)} %get-tuple-element.82), channel_id=1, source_target_pairs={{6,0},{2,1},{4,2},{0,3},{7,4},{3,5},{5,6},{1,7},{14,8},{10,9},{12,... | collective-permute-start | bytes 884744 | tf_op jit(solution)/shard_map/ppermute | solution.py:301
  72.9 6.6 %collective-permute-start.18 = (bf16[2,96,768]{2,1,0:T(8,128)(2,1)S(1)}, bf16[2,96,768]{2,1,0:T(8,128)(2,1)S(1)}, u32[]{:S(2)}, u32[]{:S(2)}) collective-permute-start(bf16[2,96,768]{2,1,0:T(8,128)(2,1)S(1)} %get-tuple-element.83), channel_id=1, source_target_pairs={{0,0},{4,1},{2,2},{6,3},{1,4},{5,5},{3,6},{7,7},{8,8},{12,9},{10,1... | collective-permute-start | bytes 884744 | tf_op jit(solution)/shard_map/ppermute | solution.py:301
  73.6 13.3 %collective-permute-start.19 = (bf16[2,96,768]{2,1,0:T(8,128)(2,1)S(1)}, bf16[2,96,768]{2,1,0:T(8,128)(2,1)S(1)}, u32[]{:S(2)}, u32[]{:S(2)}) collective-permute-start(bf16[2,96,768]{2,1,0:T(8,128)(2,1)S(1)} %get-tuple-element.84), channel_id=1, source_target_pairs={{2,0},{6,1},{0,2},{4,3},{3,4},{7,5},{1,6},{5,7},{10,8},{14,9},{8,1... | collective-permute-start | bytes 884744 | tf_op jit(solution)/shard_map/ppermute | solution.py:301
  74.6 14.2 %collective-permute-start.20 = (bf16[2,96,768]{2,1,0:T(8,128)(2,1)S(1)}, bf16[2,96,768]{2,1,0:T(8,128)(2,1)S(1)}, u32[]{:S(2)}, u32[]{:S(2)}) collective-permute-start(bf16[2,96,768]{2,1,0:T(8,128)(2,1)S(1)} %get-tuple-element.85), channel_id=1, source_target_pairs={{4,0},{0,1},{6,2},{2,3},{5,4},{1,5},{7,6},{3,7},{12,8},{8,9},{14,1... | collective-permute-start | bytes 884744 | tf_op jit(solution)/shard_map/ppermute | solution.py:301
  (2 other events, 18.9 us)

commit v5 on v4

--- a/solution.py
+++ b/solution.py
@@ -19,6 +19,15 @@
 SHIFTS = ((1, 1), (0, 0), (0, 1), (1, 0))
 BF16 = jnp.bfloat16
 ANY = pl.BlockSpec(memory_space=pl.ANY)
+FAR = pl.BlockSpec(memory_space=pltpu.HBM)
+NEAR = pl.BlockSpec(memory_space=pltpu.VMEM)
+
+
+def run_copies(copies):
+    for copy in copies:
+        copy.start()
+    for copy in copies:
+        copy.wait()
 
 
 def head_group(shift):
@@ -35,103 +44,66 @@
 
 
 def pack_kernel(first, second, *refs):
-    messages, held, loads, stores = refs[:4], refs[4], refs[5], refs[6]
-    width = held.shape[3]
-    ins, outs = [], []
+    messages, sem = refs[:4], refs[4]
+    width = messages[0].shape[2]
+    copies = []
     for i, message in enumerate(messages):
         columns = pl.ds(pl.multiple_of(head_group(SHIFTS[i]) * width, HD), width)
-        ins.append([pltpu.make_async_copy(a.at[:, columns], held.at[i, j], loads.at[i, j]) for j, a in enumerate((first, second))])
-        outs.append(pltpu.make_async_copy(held.at[i], message, stores.at[i]))
-    for pair in ins:
-        for copy in pair:
-            copy.start()
-    for pair, out in zip(ins, outs):
-        for copy in pair:
-            copy.wait()
-        out.start()
-    for out in outs:
-        out.wait()
+        for j, array in enumerate((first, second)):
+            copies.append(pltpu.make_async_copy(array.at[:, columns], message.at[j], sem.at[i, j]))
+    run_copies(copies)
 
 
 def pack(first, second, group_width):
     rows = first.shape[0]
     return pl.pallas_call(
         pack_kernel,
-        in_specs=[ANY, ANY],
-        out_specs=[ANY] * 4,
+        in_specs=[FAR, FAR],
+        out_specs=[NEAR] * 4,
         out_shape=[jax.ShapeDtypeStruct((2, rows, group_width), BF16)] * 4,
-        scratch_shapes=[
-            pltpu.VMEM((4, 2, rows, group_width), BF16),
-            pltpu.SemaphoreType.DMA((4, 2)),
-            pltpu.SemaphoreType.DMA((4,)),
-        ],
-        compiler_params=limit(60),
+        scratch_shapes=[pltpu.SemaphoreType.DMA((4, 2))],
+        compiler_params=limit(8),
         cost_estimate=pl.CostEstimate(flops=0, bytes_accessed=32 * rows * group_width, transcendentals=0),
     )(first, second)
 
 
 def unpack_kernel(*refs):
-    messages, arrays, held, loads, stores = refs[:4], refs[4:6], refs[6], refs[7], refs[8]
-    width = held.shape[3]
-    ins, outs = [], []
+    messages, arrays, sem = refs[:4], refs[4:6], refs[6]
+    width = messages[0].shape[2]
+    copies = []
     for i, message in enumerate(messages):
         columns = pl.ds(pl.multiple_of(head_group(SHIFTS[i]) * width, HD), width)
-        ins.append(pltpu.make_async_copy(message, held.at[i], loads.at[i]))
-        outs.append([pltpu.make_async_copy(held.at[i, j], a.at[:, columns], stores.at[i, j]) for j, a in enumerate(arrays)])
-    for copy in ins:
-        copy.start()
-    for copy, pair in zip(ins, outs):
-        copy.wait()
-        for out in pair:
-            out.start()
-    for pair in outs:
-        for out in pair:
-            out.wait()
+        for j, array in enumerate(arrays):
+            copies.append(pltpu.make_async_copy(message.at[j], array.at[:, columns], sem.at[i, j]))
+    run_copies(copies)
 
 
 def unpack(messages, full_width):
     _, rows, width = messages[0].shape
     return pl.pallas_call(
         unpack_kernel,
-        in_specs=[ANY] * 4,
+        in_specs=[NEAR] * 4,
         out_specs=[ANY] * 2,
         out_shape=[jax.ShapeDtypeStruct((rows, full_width), BF16)] * 2,
-        scratch_shapes=[
-            pltpu.VMEM((4, 2, rows, width), BF16),
-            pltpu.SemaphoreType.DMA((4,)),
-            pltpu.SemaphoreType.DMA((4, 2)),
-        ],
-        compiler_params=limit(4),
+        scratch_shapes=[pltpu.SemaphoreType.DMA((4, 2))],
+        compiler_params=limit(8),
         cost_estimate=pl.CostEstimate(flops=0, bytes_accessed=8 * rows * full_width, transcendentals=0),
     )(*messages)
 
 
 def join_kernel(*refs):
-    messages, joined, held, loads, stores = refs[:4], refs[4], refs[5], refs[6], refs[7]
-    ins = [pltpu.make_async_copy(m, held.at[i], loads.at[i]) for i, m in enumerate(messages)]
-    outs = [pltpu.make_async_copy(held.at[i], joined.at[i], stores.at[i]) for i in range(4)]
-    for copy in ins:
-        copy.start()
-    for copy, out in zip(ins, outs):
-        copy.wait()
-        out.start()
-    for out in outs:
-        out.wait()
+    run_copies([pltpu.make_async_copy(m, refs[4].at[i], refs[5].at[i]) for i, m in enumerate(refs[:4])])
 
 
 def join(messages):
     _, rows, width = messages[0].shape
     return pl.pallas_call(
         join_kernel,
-        in_specs=[ANY] * 4,
-        out_specs=ANY,
+        in_specs=[NEAR] * 4,
+        out_specs=NEAR,
         out_shape=jax.ShapeDtypeStruct((4, 2, rows, width), BF16),
-        scratch_shapes=[
-            pltpu.VMEM((4, 2, rows, width), BF16),
-            pltpu.SemaphoreType.DMA((4,)),
-            pltpu.SemaphoreType.DMA((4,)),
-        ],
-        compiler_params=limit(4),
+        scratch_shapes=[pltpu.SemaphoreType.DMA((4,))],
+        compiler_params=limit(8),
         cost_estimate=pl.CostEstimate(flops=0, bytes_accessed=32 * rows * width, transcendentals=0),
     )(*messages)
 
@@ -143,7 +115,13 @@
     log2_scale = scale * math.log2(math.e)
     rows = queries[0].shape[1]
     slab = 4 * rows
-    heads = [slice(h * HD, (h + 1) * HD) for h in range(ABREAST)]
+    count = queries[0].shape[2] // HD
+    for first in range(0, count, ABREAST):
+        heads = [slice(h * HD, (h + 1) * HD) for h in range(first, first + ABREAST)]
+        attend_heads(heads, bias_ref, queries, windows, oq_refs, grad_refs, rows, slab, scale, log2_scale)
+
+
+def attend_heads(heads, bias_ref, queries, windows, oq_refs, grad_refs, rows, slab, scale, log2_scale):
 
     def window(which, head):
         return jnp.concatenate([ref[:, which, :, head].reshape(slab, HD) for ref in windows], axis=0)
@@ -186,19 +164,15 @@
 def attend(bias, queries, own, other, halo):
     _, _, rows, width = own.shape
     heads = width // HD
-    block = ABREAST * HD
-    two = pl.BlockSpec((2, rows, block), lambda h: (0, 0, h))
-    joined = pl.BlockSpec((4, 2, rows, block), lambda h: (0, 0, 0, h))
     pairs = bias.shape[0] * bias.shape[1] * heads
     shapes = [jax.ShapeDtypeStruct((2, rows, width), BF16)] * 4
     shapes += [jax.ShapeDtypeStruct((4, 2, rows, width), BF16)] * 3
     outs = pl.pallas_call(
         attend_kernel,
-        grid=(heads // ABREAST,),
-        in_specs=[pl.BlockSpec(bias.shape, lambda h: (0, 0))] + [two] * 4 + [joined] * 3,
-        out_specs=[two] * 4 + [joined] * 3,
+        in_specs=[NEAR] * 8,
+        out_specs=[NEAR] * 7,
         out_shape=shapes,
-        compiler_params=limit(40),
+        compiler_params=limit(32),
         cost_estimate=pl.CostEstimate(flops=12 * pairs * HD, bytes_accessed=16 * MIB, transcendentals=pairs),
     )(bias, *queries, own, other, halo)
     return list(outs[:4]), outs[4], outs[5], outs[6]
@@ -212,16 +186,13 @@
 
 def total(own, other, halo):
     _, _, rows, width = own.shape
-    piece = HD * 2
-    joined = pl.BlockSpec((4, 2, rows, piece), lambda k: (0, 0, 0, k))
     return pl.pallas_call(
         total_kernel,
-        grid=(width // piece,),
-        in_specs=[joined] * 3,
-        out_specs=[pl.BlockSpec((2, rows, piece), lambda k: (0, 0, k))] * 4,
+        in_specs=[NEAR] * 3,
+        out_specs=[NEAR] * 4,
         out_shape=[jax.ShapeDtypeStruct((2, rows, width), BF16)] * 4,
-        compiler_params=limit(8),
-        cost_estimate=pl.CostEstimate(flops=own.size * 2, bytes_accessed=own.size * 10, transcendentals=0),
+        compiler_params=limit(12),
+        cost_estimate=pl.CostEstimate(flops=own.size * 2, bytes_accessed=own.size * 8, transcendentals=0),
     )(own, other, halo)
 
 

time: 90.5 us -> 88.4 us (0.977)
  Pallas kernels: 21.9 us -> 15.7 us
  local copies, waits for them, and re-layouts: 0.03 us -> 2.13 us
  waiting for transfers between devices: 21.2 us -> 22.9 us
    pallas_call x7, Pallas kernels: 20 us -> 13.9 us  [the longest x1 10.5 us: attend(): pl.pallas_call(attend_kernel, in_specs=[NEAR] * 8, out_specs=[NEAR] * 7,...]
    unnamed x10, local copies, waits for them, and re-layouts: 0.03 us -> 2.13 us
    ppermute x8, waiting for transfers between devices: 11.7 us -> 13.2 us  [send(): lax.ppermute(m, AXES, spread_pairs(s))]
  transfers between devices with their start and end apart: 21 -> 21, of which waited for: 7 -> 8; matrix products, arithmetic and copies ran while one was open for 0% -> 0% of each run, Pallas kernels for 7% -> 4%
where the time goes in v5:
time: 88.4 us; the launch traced here: 88.1 us
  starting transfers between devices  46.5 us (53%)
  waiting for transfers between devices  22.9 us (26%)
  Pallas kernels  15.7 us (18%)
  local copies, waits for them, and re-layouts  2.13 us (2%)
    ppermute x8, starting transfers between devices, send_back(): lax.ppermute(m, AXES, [(d, s) for s, d in spread_pairs(shift)])  22.9 us
    ppermute x8, starting transfers between devices, send(): lax.ppermute(m, AXES, spread_pairs(s))  17.9 us
    ppermute x8, waiting for transfers between devices, send(): lax.ppermute(m, AXES, spread_pairs(s))  13.2 us
    pallas_call x1, Pallas kernels, attend(): pl.pallas_call(attend_kernel, in_specs=[NEAR] * 8, out_specs=[NEAR] * 7,...  10.5 us
    ppermute x8, waiting for transfers between devices, send_back(): lax.ppermute(m, AXES, [(d, s) for s, d in spread_pairs(shift)])  9.7 us
    ppermute x2, starting transfers between devices, across(): return lax.ppermute(x, 'core', [(0, 1), (1, 0)])  3.57 us
    pallas_call x2, Pallas kernels, unpack(): pl.pallas_call(unpack_kernel, in_specs=[NEAR] * 4, out_specs=[ANY] * 2, o...  2.14 us
    unnamed x10, local copies, waits for them, and re-layouts  2.13 us
  transfers between devices with their start and end apart: 21, of which 8 were waited for; matrix products, arithmetic and copies ran while one was open for 0% of the time, Pallas kernels for 4%

profile of v5, /device:TPU:0, one launch (start us, length us, event | category | flops | bytes accessed | tf_op | source)
XLA Modules:
  0.0 88.1 jit_solution(17947228964209334396)
XLA Ops:
  1.7 1.1 %copy-done.1 = bf16[96,3072]{1,0:T(8,128)(2,1)S(1)} copy-done((bf16[96,3072]{1,0:T(8,128)(2,1)S(1)}, bf16[96,3072]{1,0:T(8,128)(2,1)}, u32[]{:S(2)}) %copy-start.1) | copy-done | bytes 589848
  3.0 4.0 %collective-permute-start = (bf16[2,96,768]{2,1,0:T(8,128)(2,1)S(1)}, bf16[2,96,768]{2,1,0:T(8,128)(2,1)S(1)}, u32[]{:S(2)}, u32[]{:S(2)}) collective-permute-start(bf16[2,96,768]{2,1,0:T(8,128)(2,1)S(1)} %get-tuple-element.50), channel_id=1, source_target_pairs={{0,6},{1,2},{2,4},{3,0},{4,7},{5,3},{6,5},{7,1},{8,14},{9,10},{10,... | collective-permute-start | bytes 884744 | tf_op jit(solution)/shard_map/ppermute | solution.py:268
  8.2 2.6 %collective-permute-start.3 = (bf16[2,96,768]{2,1,0:T(8,128)(2,1)S(1)}, bf16[2,96,768]{2,1,0:T(8,128)(2,1)S(1)}, u32[]{:S(2)}, u32[]{:S(2)}) collective-permute-start(bf16[2,96,768]{2,1,0:T(8,128)(2,1)S(1)} %get-tuple-element.53), channel_id=1, source_target_pairs={{0,4},{1,0},{2,6},{3,2},{4,5},{5,1},{6,7},{7,3},{8,12},{9,8},{10,1... | collective-permute-start | bytes 884744 | tf_op jit(solution)/shard_map/ppermute | solution.py:268
  11.8 3.1 %collective-permute-done.refs_0_ = bf16[2,96,768]{2,1,0:T(8,128)(2,1)S(1)} collective-permute-done((bf16[2,96,768]{2,1,0:T(8,128)(2,1)S(1)}, bf16[2,96,768]{2,1,0:T(8,128)(2,1)S(1)}, u32[]{:S(2)}, u32[]{:S(2)}) %collective-permute-start) | collective-permute-done | bytes 294944 | tf_op jit(solution)/shard_map/ppermute | solution.py:268
  14.9 2.9 %collective-permute-done.2.refs_2_ = bf16[2,96,768]{2,1,0:T(8,128)(2,1)S(1)} collective-permute-done((bf16[2,96,768]{2,1,0:T(8,128)(2,1)S(1)}, bf16[2,96,768]{2,1,0:T(8,128)(2,1)S(1)}, u32[]{:S(2)}, u32[]{:S(2)}) %collective-permute-start.2) | collective-permute-done | bytes 294944 | tf_op jit(solution)/shard_map/ppermute | solution.py:268
  17.8 1.6 %collective-permute-done.3.refs_3_ = bf16[2,96,768]{2,1,0:T(8,128)(2,1)S(1)} collective-permute-done((bf16[2,96,768]{2,1,0:T(8,128)(2,1)S(1)}, bf16[2,96,768]{2,1,0:T(8,128)(2,1)S(1)}, u32[]{:S(2)}, u32[]{:S(2)}) %collective-permute-start.3) | collective-permute-done | bytes 294944 | tf_op jit(solution)/shard_map/ppermute | solution.py:268
  19.7 1.6 %collective-permute-start.8 = (bf16[4,2,96,768]{3,2,1,0:T(8,128)(2,1)S(1)}, bf16[4,2,96,768]{3,2,1,0:T(8,128)(2,1)S(1)}, u32[]{:S(2)}, u32[]{:S(2)}) collective-permute-start(bf16[4,2,96,768]{3,2,1,0:T(8,128)(2,1)S(1)} %shard_map.87.refs_4_), channel_id=1, source_target_pairs={{0,1},{1,0},{2,3},{3,2},{4,5},{5,4},{6,7},{7,6},{8,9},{9,8},{10,11... | collective-permute-start | bytes 3538952 | tf_op jit(solution)/shard_map/ppermute | solution.py:276
  22.0 3.3 %collective-permute-start.5 = (bf16[2,96,768]{2,1,0:T(8,128)(2,1)S(1)}, bf16[2,96,768]{2,1,0:T(8,128)(2,1)S(1)}, u32[]{:S(2)}, u32[]{:S(2)}) collective-permute-start(bf16[2,96,768]{2,1,0:T(8,128)(2,1)S(1)} %get-tuple-element.57), channel_id=1, source_target_pairs={{0,6},{1,2},{2,4},{3,0},{4,7},{5,3},{6,5},{7,1},{8,14},{9,10},{10,... | collective-permute-start | bytes 884744 | tf_op jit(solution)/shard_map/ppermute | solution.py:268
  26.7 5.4 %collective-permute-start.9 = (bf16[2,96,768]{2,1,0:T(8,128)(2,1)S(1)}, bf16[2,96,768]{2,1,0:T(8,128)(2,1)S(1)}, u32[]{:S(2)}, u32[]{:S(2)}) collective-permute-start(bf16[2,96,768]{2,1,0:T(8,128)(2,1)S(1)} %get-tuple-element.69), channel_id=1, source_target_pairs={{0,4},{1,0},{2,6},{3,2},{4,5},{5,1},{6,7},{7,3},{8,12},{9,8},{10,1... | collective-permute-start | bytes 884744 | tf_op jit(solution)/shard_map/ppermute | solution.py:268
  32.1 1.8 %shard_map.85.bias_ref = f32[384,1152]{1,0:T(8,128)S(1)} custom-call(s32[6,16]{1,0:T(8,128)S(1)} %collective-permute-done.4.ids_ref), custom_call_target="tpu_custom_call" | custom-call | flops 2949120 | bytes 1769472 | tf_op jit(solution)/shard_map/pallas_call | solution.py:237
  34.0 2.3 %collective-permute-done.7.refs_2_ = bf16[2,96,768]{2,1,0:T(8,128)(2,1)S(1)} collective-permute-done((bf16[2,96,768]{2,1,0:T(8,128)(2,1)S(1)}, bf16[2,96,768]{2,1,0:T(8,128)(2,1)S(1)}, u32[]{:S(2)}, u32[]{:S(2)}) %collective-permute-start.7) | collective-permute-done | bytes 294944 | tf_op jit(solution)/shard_map/ppermute | solution.py:268
  36.3 3.3 %collective-permute-done.9.refs_3_ = bf16[2,96,768]{2,1,0:T(8,128)(2,1)S(1)} collective-permute-done((bf16[2,96,768]{2,1,0:T(8,128)(2,1)S(1)}, bf16[2,96,768]{2,1,0:T(8,128)(2,1)S(1)}, u32[]{:S(2)}, u32[]{:S(2)}) %collective-permute-start.9) | collective-permute-done | bytes 294944 | tf_op jit(solution)/shard_map/ppermute | solution.py:268
  39.6 10.5 %shard_map.88 = (bf16[2,96,768]{2,1,0:T(8,128)(2,1)S(1)}, bf16[2,96,768]{2,1,0:T(8,128)(2,1)S(1)}, bf16[2,96,768]{2,1,0:T(8,128)(2,1)S(1)}, bf16[2,96,768]{2,1,0...) custom-call(f32[384,1152]{1,0:T(8,128)S(1)} %shard_map.85.bias_ref, ...), custom_call_target="tpu_custom_call" | custom-call | flops 4076863488 | bytes 16777216 | tf_op jit(solution)/shard_map/pallas_call | solution.py:170
  50.1 2.0 %collective-permute-start.14 = (bf16[4,2,96,768]{3,2,1,0:T(8,128)(2,1)S(1)}, bf16[4,2,96,768]{3,2,1,0:T(8,128)(2,1)S(1)}, u32[]{:S(2)}, u32[]{:S(2)}) collective-permute-start(bf16[4,2,96,768]{3,2,1,0:T(8,128)(2,1)S(1)} %get-tuple-element.74), channel_id=1, source_target_pairs={{0,1},{1,0},{2,3},{3,2},{4,5},{5,4},{6,7},{7,6},{8,9},{9,8},{10,11... | collective-permute-start | bytes 3538952 | tf_op jit(solution)/shard_map/ppermute | solution.py:276
  52.8 3.5 %collective-permute-start.11 = (bf16[2,96,768]{2,1,0:T(8,128)(2,1)S(1)}, bf16[2,96,768]{2,1,0:T(8,128)(2,1)S(1)}, u32[]{:S(2)}, u32[]{:S(2)}) collective-permute-start(bf16[2,96,768]{2,1,0:T(8,128)(2,1)S(1)} %get-tuple-element.71), channel_id=1, source_target_pairs={{6,0},{2,1},{4,2},{0,3},{7,4},{3,5},{5,6},{1,7},{14,8},{10,9},{12,... | collective-permute-start | bytes 884744 | tf_op jit(solution)/shard_map/ppermute | solution.py:272
  57.0 1.1 %collective-permute-start.13 = (bf16[2,96,768]{2,1,0:T(8,128)(2,1)S(1)}, bf16[2,96,768]{2,1,0:T(8,128)(2,1)S(1)}, u32[]{:S(2)}, u32[]{:S(2)}) collective-permute-start(bf16[2,96,768]{2,1,0:T(8,128)(2,1)S(1)} %get-tuple-element.73), channel_id=1, source_target_pairs={{2,0},{6,1},{0,2},{4,3},{3,4},{7,5},{1,6},{5,7},{10,8},{14,9},{8,1... | collective-permute-start | bytes 884744 | tf_op jit(solution)/shard_map/ppermute | solution.py:272
  58.1 3.8 %collective-permute-start.15 = (bf16[2,96,768]{2,1,0:T(8,128)(2,1)S(1)}, bf16[2,96,768]{2,1,0:T(8,128)(2,1)S(1)}, u32[]{:S(2)}, u32[]{:S(2)}) collective-permute-start(bf16[2,96,768]{2,1,0:T(8,128)(2,1)S(1)} %get-tuple-element.76), channel_id=1, source_target_pairs={{4,0},{0,1},{6,2},{2,3},{5,4},{1,5},{7,6},{3,7},{12,8},{8,9},{14,1... | collective-permute-start | bytes 884744 | tf_op jit(solution)/shard_map/ppermute | solution.py:272
  62.4 8.7 %collective-permute-start.17 = (bf16[2,96,768]{2,1,0:T(8,128)(2,1)S(1)}, bf16[2,96,768]{2,1,0:T(8,128)(2,1)S(1)}, u32[]{:S(2)}, u32[]{:S(2)}) collective-permute-start(bf16[2,96,768]{2,1,0:T(8,128)(2,1)S(1)} %get-tuple-element.82), channel_id=1, source_target_pairs={{6,0},{2,1},{4,2},{0,3},{7,4},{3,5},{5,6},{1,7},{14,8},{10,9},{12,... | collective-permute-start | bytes 884744 | tf_op jit(solution)/shard_map/ppermute | solution.py:272
  71.7 1.1 %collective-permute-start.19 = (bf16[2,96,768]{2,1,0:T(8,128)(2,1)S(1)}, bf16[2,96,768]{2,1,0:T(8,128)(2,1)S(1)}, u32[]{:S(2)}, u32[]{:S(2)}) collective-permute-start(bf16[2,96,768]{2,1,0:T(8,128)(2,1)S(1)} %get-tuple-element.84), channel_id=1, source_target_pairs={{2,0},{6,1},{0,2},{4,3},{3,4},{7,5},{1,6},{5,7},{10,8},{14,9},{8,1... | collective-permute-start | bytes 884744 | tf_op jit(solution)/shard_map/ppermute | solution.py:272
  72.8 3.4 %collective-permute-start.20 = (bf16[2,96,768]{2,1,0:T(8,128)(2,1)S(1)}, bf16[2,96,768]{2,1,0:T(8,128)(2,1)S(1)}, u32[]{:S(2)}, u32[]{:S(2)}) collective-permute-start(bf16[2,96,768]{2,1,0:T(8,128)(2,1)S(1)} %get-tuple-element.85), channel_id=1, source_target_pairs={{4,0},{0,1},{6,2},{2,3},{5,4},{1,5},{7,6},{3,7},{12,8},{8,9},{14,1... | collective-permute-start | bytes 884744 | tf_op jit(solution)/shard_map/ppermute | solution.py:272
  76.2 1.1 %shard_map.89 = (bf16[96,3072]{1,0:T(8,128)(2,1)}, bf16[96,3072]{1,0:T(8,128)(2,1)}) custom-call(bf16[2,96,768]{2,1,0:T(8,128)(2,1)S(1)} %collective-permute-done.11.refs_0_, bf16[2,96,768]{2,1,0:T(8,128)(2,1)S(1)} %collective-permute-done.12.refs_1_, bf16[2,96,768]{2,1,0:T(8,128)(2,1)S(1)} %collective-permute-done.13.refs_2_, ...), custom_call_target="tpu_custom_call" | custom-call | bytes 2359296 | tf_op jit(solution)/shard_map/pallas_call | solution.py:83
  78.0 7.5 %collective-permute-done.19.refs_2_ = bf16[2,96,768]{2,1,0:T(8,128)(2,1)S(1)} collective-permute-done((bf16[2,96,768]{2,1,0:T(8,128)(2,1)S(1)}, bf16[2,96,768]{2,1,0:T(8,128)(2,1)S(1)}, u32[]{:S(2)}, u32[]{:S(2)}) %collective-permute-start.19) | collective-permute-done | bytes 294944 | tf_op jit(solution)/shard_map/ppermute | solution.py:272
  85.4 1.6 %collective-permute-done.20.refs_3_ = bf16[2,96,768]{2,1,0:T(8,128)(2,1)S(1)} collective-permute-done((bf16[2,96,768]{2,1,0:T(8,128)(2,1)S(1)}, bf16[2,96,768]{2,1,0:T(8,128)(2,1)S(1)}, u32[]{:S(2)}, u32[]{:S(2)}) %collective-permute-start.20) | collective-permute-done | bytes 294944 | tf_op jit(solution)/shard_map/ppermute | solution.py:272
  87.0 1.1 %shard_map.91 = (bf16[96,3072]{1,0:T(8,128)(2,1)}, bf16[96,3072]{1,0:T(8,128)(2,1)}) custom-call(bf16[2,96,768]{2,1,0:T(8,128)(2,1)S(1)} %collective-permute-done.17.refs_0_, bf16[2,96,768]{2,1,0:T(8,128)(2,1)S(1)} %collective-permute-done.18.refs_1_, bf16[2,96,768]{2,1,0:T(8,128)(2,1)S(1)} %collective-permute-done.19.refs_2_, ...), custom_call_target="tpu_custom_call" | custom-call | bytes 2359296 | tf_op jit(solution)/shard_map/pallas_call | solution.py:83
  (36 shorter events, 9.0 us)
Async XLA Ops:
  2.8 8.1 %copy-start.4 = (s32[6,16]{1,0:T(8,128)S(1)}, s32[6,16]{1,0:T(8,128)}, u32[]{:S(2)}) copy-start(s32[6,16]{1,0:T(8,128)} %param.9) | copy-start | bytes 1156
  2.8 8.8 %copy-start.2 = (bf16[96,3072]{1,0:T(8,128)(2,1)S(1)}, bf16[96,3072]{1,0:T(8,128)(2,1)}, u32[]{:S(2)}) copy-start(bf16[96,3072]{1,0:T(8,128)(2,1)} %first.2) | copy-start | bytes 1769476
  2.8 8.8 %copy-start.3 = (bf16[96,3072]{1,0:T(8,128)(2,1)S(1)}, bf16[96,3072]{1,0:T(8,128)(2,1)}, u32[]{:S(2)}) copy-start(bf16[96,3072]{1,0:T(8,128)(2,1)} %second.3) | copy-start | bytes 1769476
  3.0 11.9 %collective-permute-start = (bf16[2,96,768]{2,1,0:T(8,128)(2,1)S(1)}, bf16[2,96,768]{2,1,0:T(8,128)(2,1)S(1)}, u32[]{:S(2)}, u32[]{:S(2)}) collective-permute-start(bf16[2,96,768]{2,1,0:T(8,128)(2,1)S(1)} %get-tuple-element.50), channel_id=1, source_target_pairs={{0,6},{1,2},{2,4},{3,0},{4,7},{5,3},{6,5},{7,1},{8,14},{9,10},{10,... | collective-permute-start | bytes 884744 | tf_op jit(solution)/shard_map/ppermute | solution.py:268
  7.0 7.9 %collective-permute-start.1 = (bf16[2,96,768]{2,1,0:T(8,128)(2,1)S(1)}, bf16[2,96,768]{2,1,0:T(8,128)(2,1)S(1)}, u32[]{:S(2)}, u32[]{:S(2)}) collective-permute-start(bf16[2,96,768]{2,1,0:T(8,128)(2,1)S(1)} %get-tuple-element.51), channel_id=1, source_target_pairs={{0,0},{1,4},{2,2},{3,6},{4,1},{5,5},{6,3},{7,7},{8,8},{9,12},{10,1... | collective-permute-start | bytes 884744 | tf_op jit(solution)/shard_map/ppermute | solution.py:268
  7.7 10.2 %collective-permute-start.2 = (bf16[2,96,768]{2,1,0:T(8,128)(2,1)S(1)}, bf16[2,96,768]{2,1,0:T(8,128)(2,1)S(1)}, u32[]{:S(2)}, u32[]{:S(2)}) collective-permute-start(bf16[2,96,768]{2,1,0:T(8,128)(2,1)S(1)} %get-tuple-element.52), channel_id=1, source_target_pairs={{0,2},{1,6},{2,0},{3,4},{4,3},{5,7},{6,1},{7,5},{8,10},{9,14},{10,... | collective-permute-start | bytes 884744 | tf_op jit(solution)/shard_map/ppermute | solution.py:268
  8.2 11.2 %collective-permute-start.3 = (bf16[2,96,768]{2,1,0:T(8,128)(2,1)S(1)}, bf16[2,96,768]{2,1,0:T(8,128)(2,1)S(1)}, u32[]{:S(2)}, u32[]{:S(2)}) collective-permute-start(bf16[2,96,768]{2,1,0:T(8,128)(2,1)S(1)} %get-tuple-element.53), channel_id=1, source_target_pairs={{0,4},{1,0},{2,6},{3,2},{4,5},{5,1},{6,7},{7,3},{8,12},{9,8},{10,1... | collective-permute-start | bytes 884744 | tf_op jit(solution)/shard_map/ppermute | solution.py:268
  10.9 1.0 %collective-permute-start.4 = (s32[6,16]{1,0:T(8,128)S(1)}, s32[6,16]{1,0:T(8,128)S(1)}, u32[]{:S(2)}, u32[]{:S(2)}) collective-permute-start(s32[6,16]{1,0:T(8,128)S(1)} %copy-done.4), channel_id=1, source_target_pairs={{0,0},{1,4},{2,2},{3,6},{4,1},{5,5},{6,3},{7,7},{8,8},{9,12},{10,1... | collective-permute-start | bytes 1160 | tf_op jit(solution)/shard_map/ppermute | solution.py:232
  19.7 7.0 %collective-permute-start.8 = (bf16[4,2,96,768]{3,2,1,0:T(8,128)(2,1)S(1)}, bf16[4,2,96,768]{3,2,1,0:T(8,128)(2,1)S(1)}, u32[]{:S(2)}, u32[]{:S(2)}) collective-permute-start(bf16[4,2,96,768]{3,2,1,0:T(8,128)(2,1)S(1)} %shard_map.87.refs_4_), channel_id=1, source_target_pairs={{0,1},{1,0},{2,3},{3,2},{4,5},{5,4},{6,7},{7,6},{8,9},{9,8},{10,11... | collective-permute-start | bytes 3538952 | tf_op jit(solution)/shard_map/ppermute | solution.py:276
  21.3 15.0 %collective-permute-start.10 = (bf16[4,2,96,768]{3,2,1,0:T(8,128)(2,1)S(1)}, bf16[4,2,96,768]{3,2,1,0:T(8,128)(2,1)S(1)}, u32[]{:S(2)}, u32[]{:S(2)}) collective-permute-start(bf16[4,2,96,768]{3,2,1,0:T(8,128)(2,1)S(1)} %shard_map.87.refs_4_), channel_id=1, source_target_pairs={{0,0},{1,8},{2,2},{3,10},{4,4},{5,12},{6,6},{7,14},{8,1},{9,16},{1... | collective-permute-start | bytes 3538952 | tf_op jit(solution)/shard_map/ppermute | solution.py:279
  22.0 12.0 %collective-permute-start.5 = (bf16[2,96,768]{2,1,0:T(8,128)(2,1)S(1)}, bf16[2,96,768]{2,1,0:T(8,128)(2,1)S(1)}, u32[]{:S(2)}, u32[]{:S(2)}) collective-permute-start(bf16[2,96,768]{2,1,0:T(8,128)(2,1)S(1)} %get-tuple-element.57), channel_id=1, source_target_pairs={{0,6},{1,2},{2,4},{3,0},{4,7},{5,3},{6,5},{7,1},{8,14},{9,10},{10,... | collective-permute-start | bytes 884744 | tf_op jit(solution)/shard_map/ppermute | solution.py:268
  25.3 8.7 %collective-permute-start.6 = (bf16[2,96,768]{2,1,0:T(8,128)(2,1)S(1)}, bf16[2,96,768]{2,1,0:T(8,128)(2,1)S(1)}, u32[]{:S(2)}, u32[]{:S(2)}) collective-permute-start(bf16[2,96,768]{2,1,0:T(8,128)(2,1)S(1)} %get-tuple-element.65), channel_id=1, source_target_pairs={{0,0},{1,4},{2,2},{3,6},{4,1},{5,5},{6,3},{7,7},{8,8},{9,12},{10,1... | collective-permute-start | bytes 884744 | tf_op jit(solution)/shard_map/ppermute | solution.py:268
  26.0 10.3 %collective-permute-start.7 = (bf16[2,96,768]{2,1,0:T(8,128)(2,1)S(1)}, bf16[2,96,768]{2,1,0:T(8,128)(2,1)S(1)}, u32[]{:S(2)}, u32[]{:S(2)}) collective-permute-start(bf16[2,96,768]{2,1,0:T(8,128)(2,1)S(1)} %get-tuple-element.66), channel_id=1, source_target_pairs={{0,2},{1,6},{2,0},{3,4},{4,3},{5,7},{6,1},{7,5},{8,10},{9,14},{10,... | collective-permute-start | bytes 884744 | tf_op jit(solution)/shard_map/ppermute | solution.py:268
  26.7 12.9 %collective-permute-start.9 = (bf16[2,96,768]{2,1,0:T(8,128)(2,1)S(1)}, bf16[2,96,768]{2,1,0:T(8,128)(2,1)S(1)}, u32[]{:S(2)}, u32[]{:S(2)}) collective-permute-start(bf16[2,96,768]{2,1,0:T(8,128)(2,1)S(1)} %get-tuple-element.69), channel_id=1, source_target_pairs={{0,4},{1,0},{2,6},{3,2},{4,5},{5,1},{6,7},{7,3},{8,12},{9,8},{10,1... | collective-permute-start | bytes 884744 | tf_op jit(solution)/shard_map/ppermute | solution.py:268
  50.1 8.0 %collective-permute-start.14 = (bf16[4,2,96,768]{3,2,1,0:T(8,128)(2,1)S(1)}, bf16[4,2,96,768]{3,2,1,0:T(8,128)(2,1)S(1)}, u32[]{:S(2)}, u32[]{:S(2)}) collective-permute-start(bf16[4,2,96,768]{3,2,1,0:T(8,128)(2,1)S(1)} %get-tuple-element.74), channel_id=1, source_target_pairs={{0,1},{1,0},{2,3},{3,2},{4,5},{5,4},{6,7},{7,6},{8,9},{9,8},{10,11... | collective-permute-start | bytes 3538952 | tf_op jit(solution)/shard_map/ppermute | solution.py:276
  52.1 9.8 %collective-permute-start.16 = (bf16[4,2,96,768]{3,2,1,0:T(8,128)(2,1)S(1)}, bf16[4,2,96,768]{3,2,1,0:T(8,128)(2,1)S(1)}, u32[]{:S(2)}, u32[]{:S(2)}) collective-permute-start(bf16[4,2,96,768]{3,2,1,0:T(8,128)(2,1)S(1)} %get-tuple-element.81), channel_id=1, source_target_pairs={{0,0},{1,8},{2,2},{3,10},{4,4},{5,12},{6,6},{7,14},{8,1},{9,16},{1... | collective-permute-start | bytes 3538952 | tf_op jit(solution)/shard_map/ppermute | solution.py:279
  52.8 18.2 %collective-permute-start.11 = (bf16[2,96,768]{2,1,0:T(8,128)(2,1)S(1)}, bf16[2,96,768]{2,1,0:T(8,128)(2,1)S(1)}, u32[]{:S(2)}, u32[]{:S(2)}) collective-permute-start(bf16[2,96,768]{2,1,0:T(8,128)(2,1)S(1)} %get-tuple-element.71), channel_id=1, source_target_pairs={{6,0},{2,1},{4,2},{0,3},{7,4},{3,5},{5,6},{1,7},{14,8},{10,9},{12,... | collective-permute-start | bytes 884744 | tf_op jit(solution)/shard_map/ppermute | solution.py:272
  56.4 15.3 %collective-permute-start.12 = (bf16[2,96,768]{2,1,0:T(8,128)(2,1)S(1)}, bf16[2,96,768]{2,1,0:T(8,128)(2,1)S(1)}, u32[]{:S(2)}, u32[]{:S(2)}) collective-permute-start(bf16[2,96,768]{2,1,0:T(8,128)(2,1)S(1)} %get-tuple-element.72), channel_id=1, source_target_pairs={{0,0},{4,1},{2,2},{6,3},{1,4},{5,5},{3,6},{7,7},{8,8},{12,9},{10,1... | collective-permute-start | bytes 884744 | tf_op jit(solution)/shard_map/ppermute | solution.py:272
  57.0 15.8 %collective-permute-start.13 = (bf16[2,96,768]{2,1,0:T(8,128)(2,1)S(1)}, bf16[2,96,768]{2,1,0:T(8,128)(2,1)S(1)}, u32[]{:S(2)}, u32[]{:S(2)}) collective-permute-start(bf16[2,96,768]{2,1,0:T(8,128)(2,1)S(1)} %get-tuple-element.73), channel_id=1, source_target_pairs={{2,0},{6,1},{0,2},{4,3},{3,4},{7,5},{1,6},{5,7},{10,8},{14,9},{8,1... | collective-permute-start | bytes 884744 | tf_op jit(solution)/shard_map/ppermute | solution.py:272
  58.1 18.1 %collective-permute-start.15 = (bf16[2,96,768]{2,1,0:T(8,128)(2,1)S(1)}, bf16[2,96,768]{2,1,0:T(8,128)(2,1)S(1)}, u32[]{:S(2)}, u32[]{:S(2)}) collective-permute-start(bf16[2,96,768]{2,1,0:T(8,128)(2,1)S(1)} %get-tuple-element.76), channel_id=1, source_target_pairs={{4,0},{0,1},{6,2},{2,3},{5,4},{1,5},{7,6},{3,7},{12,8},{8,9},{14,1... | collective-permute-start | bytes 884744 | tf_op jit(solution)/shard_map/ppermute | solution.py:272
  62.4 15.6 %collective-permute-start.17 = (bf16[2,96,768]{2,1,0:T(8,128)(2,1)S(1)}, bf16[2,96,768]{2,1,0:T(8,128)(2,1)S(1)}, u32[]{:S(2)}, u32[]{:S(2)}) collective-permute-start(bf16[2,96,768]{2,1,0:T(8,128)(2,1)S(1)} %get-tuple-element.82), channel_id=1, source_target_pairs={{6,0},{2,1},{4,2},{0,3},{7,4},{3,5},{5,6},{1,7},{14,8},{10,9},{12,... | collective-permute-start | bytes 884744 | tf_op jit(solution)/shard_map/ppermute | solution.py:272
  71.0 6.9 %collective-permute-start.18 = (bf16[2,96,768]{2,1,0:T(8,128)(2,1)S(1)}, bf16[2,96,768]{2,1,0:T(8,128)(2,1)S(1)}, u32[]{:S(2)}, u32[]{:S(2)}) collective-permute-start(bf16[2,96,768]{2,1,0:T(8,128)(2,1)S(1)} %get-tuple-element.83), channel_id=1, source_target_pairs={{0,0},{4,1},{2,2},{6,3},{1,4},{5,5},{3,6},{7,7},{8,8},{12,9},{10,1... | collective-permute-start | bytes 884744 | tf_op jit(solution)/shard_map/ppermute | solution.py:272
  71.7 13.7 %collective-permute-start.19 = (bf16[2,96,768]{2,1,0:T(8,128)(2,1)S(1)}, bf16[2,96,768]{2,1,0:T(8,128)(2,1)S(1)}, u32[]{:S(2)}, u32[]{:S(2)}) collective-permute-start(bf16[2,96,768]{2,1,0:T(8,128)(2,1)S(1)} %get-tuple-element.84), channel_id=1, source_target_pairs={{2,0},{6,1},{0,2},{4,3},{3,4},{7,5},{1,6},{5,7},{10,8},{14,9},{8,1... | collective-permute-start | bytes 884744 | tf_op jit(solution)/shard_map/ppermute | solution.py:272
  72.8 14.2 %collective-permute-start.20 = (bf16[2,96,768]{2,1,0:T(8,128)(2,1)S(1)}, bf16[2,96,768]{2,1,0:T(8,128)(2,1)S(1)}, u32[]{:S(2)}, u32[]{:S(2)}) collective-permute-start(bf16[2,96,768]{2,1,0:T(8,128)(2,1)S(1)} %get-tuple-element.85), channel_id=1, source_target_pairs={{4,0},{0,1},{6,2},{2,3},{5,4},{1,5},{7,6},{3,7},{12,8},{8,9},{14,1... | collective-permute-start | bytes 884744 | tf_op jit(solution)/shard_map/ppermute | solution.py:272
  (2 other events, 2.1 us)

commit v6 on v5

--- a/solution.py
+++ b/solution.py
@@ -11,8 +11,8 @@
 
 HD = 128
 TILE = 64
+BACK = (3, 2, 0, 1)
 EARLY = 1
-ABREAST = 2
 MASKED = -1e30
 AXES = ("group", "pair", "row", "core")
 PLANE = ("pair", "row", "core")
@@ -67,28 +67,28 @@
     )(first, second)
 
 
-def unpack_kernel(*refs):
+def unpack_kernel(order, *refs):
     messages, arrays, sem = refs[:4], refs[4:6], refs[6]
     width = messages[0].shape[2]
     copies = []
     for i, message in enumerate(messages):
-        columns = pl.ds(pl.multiple_of(head_group(SHIFTS[i]) * width, HD), width)
+        columns = pl.ds(pl.multiple_of(head_group(SHIFTS[order[i]]) * width, HD), width)
         for j, array in enumerate(arrays):
             copies.append(pltpu.make_async_copy(message.at[j], array.at[:, columns], sem.at[i, j]))
     run_copies(copies)
 
 
-def unpack(messages, full_width):
+def unpack(messages, full_width, order=(0, 1, 2, 3)):
     _, rows, width = messages[0].shape
     return pl.pallas_call(
-        unpack_kernel,
+        functools.partial(unpack_kernel, order),
         in_specs=[NEAR] * 4,
         out_specs=[ANY] * 2,
         out_shape=[jax.ShapeDtypeStruct((rows, full_width), BF16)] * 2,
         scratch_shapes=[pltpu.SemaphoreType.DMA((4, 2))],
         compiler_params=limit(8),
         cost_estimate=pl.CostEstimate(flops=0, bytes_accessed=8 * rows * full_width, transcendentals=0),
-    )(*messages)
+    )(*(messages[i] for i in order))
 
 
 def join_kernel(*refs):
@@ -113,53 +113,61 @@
     oq_refs, grad_refs = refs[7:11], refs[11:14]
     scale = 1.0 / math.sqrt(HD)
     log2_scale = scale * math.log2(math.e)
-    rows = queries[0].shape[1]
+    rows, width = queries[0].shape[1:]
     slab = 4 * rows
-    count = queries[0].shape[2] // HD
-    for first in range(0, count, ABREAST):
-        heads = [slice(h * HD, (h + 1) * HD) for h in range(first, first + ABREAST)]
-        attend_heads(heads, bias_ref, queries, windows, oq_refs, grad_refs, rows, slab, scale, log2_scale)
-
-
-def attend_heads(heads, bias_ref, queries, windows, oq_refs, grad_refs, rows, slab, scale, log2_scale):
-
-    def window(which, head):
-        return jnp.concatenate([ref[:, which, :, head].reshape(slab, HD) for ref in windows], axis=0)
-
-    def tokens(which, head):
-        return jnp.concatenate([m[which, :, head] for m in queries], axis=0)
-
-    def each(function, *lists):
-        return [function(*one) for one in zip(*lists)]
-
     nt = (((1,), (1,)), ((), ()))
     nn = (((1,), (0,)), ((), ()))
     tn = (((0,), (0,)), ((), ()))
     dot = functools.partial(lax.dot_general, preferred_element_type=jnp.float32)
-    keys, vals = [window(0, h) for h in heads], [window(1, h) for h in heads]
-    query, grad = [tokens(0, h) for h in heads], [tokens(1, h) for h in heads]
-    scores = each(lambda q, k: dot(q, k, nt) + bias_ref[...], query, keys)
-    dweights = each(lambda g, v: dot(g, v, nt), grad, vals)
-    peak = each(lambda s: jnp.max(s, axis=1, keepdims=True), scores)
-    weights = each(lambda s, m: jnp.exp2((s - m) * log2_scale), scores, peak)
-    weights = each(lambda w: w * (1.0 / jnp.sum(w, axis=1, keepdims=True)), weights)
-    weights_low = each(lambda w: w.astype(BF16), weights)
-    out = each(lambda w, v: dot(w, v, nn).astype(BF16), weights_low, vals)
-    out_dot = each(
-        lambda g, o: jnp.sum(g.astype(jnp.float32) * o.astype(jnp.float32), axis=1, keepdims=True), grad, out
-    )
-    dscores = each(lambda w, d, o: (w * (d - o)).astype(BF16), weights, dweights, out_dot)
-    for h, head in enumerate(heads):
-        dquery = (dot(dscores[h], keys[h], nn) * scale).astype(BF16)
+
+    def window(which, head):
+        return jnp.concatenate([ref[:, which, :, head].reshape(slab, HD) for ref in windows], axis=0)
+
+    def tokens(which, head):
+        return jnp.concatenate([m[which, :, head] for m in queries], axis=0)
+
+    def products(head):
+        scores = dot(tokens(0, head), window(0, head), nt) + bias_ref[...]
+        return scores, dot(tokens(1, head), window(1, head), nt)
+
+    def softmax(scores):
+        peak = jnp.max(scores, axis=1, keepdims=True)
+        weights = jnp.exp2((scores - peak) * log2_scale)
+        return weights * (1.0 / jnp.sum(weights, axis=1, keepdims=True))
+
+    def attended(head, weights_low):
+        out = dot(weights_low, window(1, head), nn).astype(BF16)
         for i, ref in enumerate(oq_refs):
-            ref[0, :, head] = out[h][i * rows : (i + 1) * rows]
+            ref[0, :, head] = out[i * rows : (i + 1) * rows]
+        grad = tokens(1, head).astype(jnp.float32)
+        return jnp.sum(grad * out.astype(jnp.float32), axis=1, keepdims=True)
+
+    def store(which, head, value):
+        for third, ref in enumerate(grad_refs):
+            piece = value[third * slab : (third + 1) * slab]
+            ref[:, which, :, head] = piece.reshape(4, rows, HD).astype(BF16)
+
+    def value_grad(head, weights_low):
+        store(1, head, dot(weights_low, tokens(1, head), tn))
+
+    def other_grads(head, dscores):
+        dquery = (dot(dscores, window(0, head), nn) * scale).astype(BF16)
+        for i, ref in enumerate(oq_refs):
             ref[1, :, head] = dquery[i * rows : (i + 1) * rows]
-        grads = (dot(dscores[h], query[h], tn) * scale, dot(weights_low[h], grad[h], tn))
-        for which, value in enumerate(grads):
-            for third, ref in enumerate(grad_refs):
-                piece = value[third * slab : (third + 1) * slab]
-                ref[:, which, :, head] = piece.reshape(4, rows, HD).astype(BF16)
-
+        store(0, head, dot(dscores, tokens(0, head), tn) * scale)
+
+    heads = [slice(h, h + HD) for h in range(0, width, HD)]
+    for i in range(0, len(heads), 2):
+        pair = heads[i : i + 2]
+        ready = [products(h) for h in pair]
+        weights = [softmax(s) for s, _ in ready]
+        low = [w.astype(BF16) for w in weights]
+        out_dot = [attended(h, l) for h, l in zip(pair, low)]
+        for h, l in zip(pair, low):
+            value_grad(h, l)
+        dscores = [(w * (r[1] - o)).astype(BF16) for w, r, o in zip(weights, ready, out_dot)]
+        for h, d in zip(pair, dscores):
+            other_grads(h, d)
 
 def attend(bias, queries, own, other, halo):
     _, _, rows, width = own.shape
@@ -267,10 +275,11 @@
     def send(messages):
         return [lax.ppermute(m, AXES, spread_pairs(s)) for m, s in zip(messages, SHIFTS)]
 
-    def send_back(messages):
-        return [
-            lax.ppermute(m, AXES, [(d, s) for s, d in spread_pairs(shift)]) for m, shift in zip(messages, SHIFTS)
-        ]
+    def send_back(messages, order=(0, 1, 2, 3)):
+        back = dict.fromkeys(range(4))
+        for i in order:
+            back[i] = lax.ppermute(messages[i], AXES, [(d, s) for s, d in spread_pairs(SHIFTS[i])])
+        return list(back.values())
 
     def across(x):
         return lax.ppermute(x, "core", [(0, 1), (1, 0)])
@@ -293,8 +302,8 @@
     other_part = across(other_part)
     other_part, oq[3] = lax.optimization_barrier((other_part, oq[3]))
     grads = total(own_part, other_part, halo(far_part))
-    forward = unpack(send_back(oq), full_width)
-    return *forward, *unpack(send_back(grads), full_width)
+    forward = unpack(send_back(oq, BACK), full_width, BACK)
+    return *forward, *unpack(send_back(grads, BACK), full_width, BACK)
 
 
 def solution(mesh):

time: 88.4 us -> 87.1 us (0.985); the launches traced: 88.1 us -> 85.9 us
  starting transfers between devices: 46.5 us -> 43.7 us
  waiting for transfers between devices: 22.9 us -> 23.9 us
    ppermute x8, starting transfers between devices: 22.9 us -> 20.1 us  [send_back(): lax.ppermute(messages[i], AXES, [(d, s) for s, d in spread_pairs(SHIFTS[i...]
    ppermute x8, waiting for transfers between devices: 9.7 us -> 10.6 us  [send_back(): lax.ppermute(messages[i], AXES, [(d, s) for s, d in spread_pairs(SHIFTS[i...]
where the time goes in v6:
time: 87.1 us; the launch traced here: 85.9 us
  starting transfers between devices  43.7 us (50%)
  waiting for transfers between devices  23.9 us (27%)
  Pallas kernels  15.4 us (18%)
  local copies, waits for them, and re-layouts  2.13 us (2%)
    ppermute x8, starting transfers between devices, send_back(): lax.ppermute(messages[i], AXES, [(d, s) for s, d in spread_pairs(SHIFTS[i...  20.1 us
    ppermute x8, starting transfers between devices, send(): lax.ppermute(m, AXES, spread_pairs(s))  17.9 us
    ppermute x8, waiting for transfers between devices, send(): lax.ppermute(m, AXES, spread_pairs(s))  13.2 us
    ppermute x8, waiting for transfers between devices, send_back(): lax.ppermute(messages[i], AXES, [(d, s) for s, d in spread_pairs(SHIFTS[i...  10.6 us
    pallas_call x1, Pallas kernels, attend(): pl.pallas_call(attend_kernel, in_specs=[NEAR] * 8, out_specs=[NEAR] * 7,...  10.2 us
    ppermute x2, starting transfers between devices, across(): return lax.ppermute(x, 'core', [(0, 1), (1, 0)])  3.58 us
    pallas_call x2, Pallas kernels, unpack(): pl.pallas_call(functools.partial(unpack_kernel, order), in_specs=[NEAR] *...  2.16 us
    unnamed x10, local copies, waits for them, and re-layouts  2.13 us
  transfers between devices with their start and end apart: 21, of which 8 were waited for; matrix products, arithmetic and copies ran while one was open for 0% of the time, Pallas kernels for 4%

profile of v6, /device:TPU:0, one launch (start us, length us, event | category | flops | bytes accessed | tf_op | source)
XLA Modules:
  0.0 85.9 jit_solution(1912676025781161009)
XLA Ops:
  0.6 1.1 %copy-done = bf16[96,3072]{1,0:T(8,128)(2,1)S(1)} copy-done((bf16[96,3072]{1,0:T(8,128)(2,1)S(1)}, bf16[96,3072]{1,0:T(8,128)(2,1)}, u32[]{:S(2)}) %copy-start) | copy-done | bytes 589848
  1.7 1.1 %copy-done.1 = bf16[96,3072]{1,0:T(8,128)(2,1)S(1)} copy-done((bf16[96,3072]{1,0:T(8,128)(2,1)S(1)}, bf16[96,3072]{1,0:T(8,128)(2,1)}, u32[]{:S(2)}) %copy-start.1) | copy-done | bytes 589848
  3.0 4.0 %collective-permute-start = (bf16[2,96,768]{2,1,0:T(8,128)(2,1)S(1)}, bf16[2,96,768]{2,1,0:T(8,128)(2,1)S(1)}, u32[]{:S(2)}, u32[]{:S(2)}) collective-permute-start(bf16[2,96,768]{2,1,0:T(8,128)(2,1)S(1)} %get-tuple-element.50), channel_id=1, source_target_pairs={{0,6},{1,2},{2,4},{3,0},{4,7},{5,3},{6,5},{7,1},{8,14},{9,10},{10,... | collective-permute-start | bytes 884744 | tf_op jit(solution)/shard_map/ppermute | solution.py:276
  8.2 2.6 %collective-permute-start.3 = (bf16[2,96,768]{2,1,0:T(8,128)(2,1)S(1)}, bf16[2,96,768]{2,1,0:T(8,128)(2,1)S(1)}, u32[]{:S(2)}, u32[]{:S(2)}) collective-permute-start(bf16[2,96,768]{2,1,0:T(8,128)(2,1)S(1)} %get-tuple-element.53), channel_id=1, source_target_pairs={{0,4},{1,0},{2,6},{3,2},{4,5},{5,1},{6,7},{7,3},{8,12},{9,8},{10,1... | collective-permute-start | bytes 884744 | tf_op jit(solution)/shard_map/ppermute | solution.py:276
  11.8 3.1 %collective-permute-done.refs_0_ = bf16[2,96,768]{2,1,0:T(8,128)(2,1)S(1)} collective-permute-done((bf16[2,96,768]{2,1,0:T(8,128)(2,1)S(1)}, bf16[2,96,768]{2,1,0:T(8,128)(2,1)S(1)}, u32[]{:S(2)}, u32[]{:S(2)}) %collective-permute-start) | collective-permute-done | bytes 294944 | tf_op jit(solution)/shard_map/ppermute | solution.py:276
  14.9 2.9 %collective-permute-done.2.refs_2_ = bf16[2,96,768]{2,1,0:T(8,128)(2,1)S(1)} collective-permute-done((bf16[2,96,768]{2,1,0:T(8,128)(2,1)S(1)}, bf16[2,96,768]{2,1,0:T(8,128)(2,1)S(1)}, u32[]{:S(2)}, u32[]{:S(2)}) %collective-permute-start.2) | collective-permute-done | bytes 294944 | tf_op jit(solution)/shard_map/ppermute | solution.py:276
  17.8 1.6 %collective-permute-done.3.refs_3_ = bf16[2,96,768]{2,1,0:T(8,128)(2,1)S(1)} collective-permute-done((bf16[2,96,768]{2,1,0:T(8,128)(2,1)S(1)}, bf16[2,96,768]{2,1,0:T(8,128)(2,1)S(1)}, u32[]{:S(2)}, u32[]{:S(2)}) %collective-permute-start.3) | collective-permute-done | bytes 294944 | tf_op jit(solution)/shard_map/ppermute | solution.py:276
  19.7 1.6 %collective-permute-start.8 = (bf16[4,2,96,768]{3,2,1,0:T(8,128)(2,1)S(1)}, bf16[4,2,96,768]{3,2,1,0:T(8,128)(2,1)S(1)}, u32[]{:S(2)}, u32[]{:S(2)}) collective-permute-start(bf16[4,2,96,768]{3,2,1,0:T(8,128)(2,1)S(1)} %shard_map.87.refs_4_), channel_id=1, source_target_pairs={{0,1},{1,0},{2,3},{3,2},{4,5},{5,4},{6,7},{7,6},{8,9},{9,8},{10,11... | collective-permute-start | bytes 3538952 | tf_op jit(solution)/shard_map/ppermute | solution.py:285
  22.0 3.3 %collective-permute-start.5 = (bf16[2,96,768]{2,1,0:T(8,128)(2,1)S(1)}, bf16[2,96,768]{2,1,0:T(8,128)(2,1)S(1)}, u32[]{:S(2)}, u32[]{:S(2)}) collective-permute-start(bf16[2,96,768]{2,1,0:T(8,128)(2,1)S(1)} %get-tuple-element.57), channel_id=1, source_target_pairs={{0,6},{1,2},{2,4},{3,0},{4,7},{5,3},{6,5},{7,1},{8,14},{9,10},{10,... | collective-permute-start | bytes 884744 | tf_op jit(solution)/shard_map/ppermute | solution.py:276
  26.7 5.4 %collective-permute-start.9 = (bf16[2,96,768]{2,1,0:T(8,128)(2,1)S(1)}, bf16[2,96,768]{2,1,0:T(8,128)(2,1)S(1)}, u32[]{:S(2)}, u32[]{:S(2)}) collective-permute-start(bf16[2,96,768]{2,1,0:T(8,128)(2,1)S(1)} %get-tuple-element.69), channel_id=1, source_target_pairs={{0,4},{1,0},{2,6},{3,2},{4,5},{5,1},{6,7},{7,3},{8,12},{9,8},{10,1... | collective-permute-start | bytes 884744 | tf_op jit(solution)/shard_map/ppermute | solution.py:276
  32.1 1.8 %shard_map.85.bias_ref = f32[384,1152]{1,0:T(8,128)S(1)} custom-call(s32[6,16]{1,0:T(8,128)S(1)} %collective-permute-done.4.ids_ref), custom_call_target="tpu_custom_call" | custom-call | flops 2949120 | bytes 1769472 | tf_op jit(solution)/shard_map/pallas_call | solution.py:245
  34.0 2.3 %collective-permute-done.7.refs_2_ = bf16[2,96,768]{2,1,0:T(8,128)(2,1)S(1)} collective-permute-done((bf16[2,96,768]{2,1,0:T(8,128)(2,1)S(1)}, bf16[2,96,768]{2,1,0:T(8,128)(2,1)S(1)}, u32[]{:S(2)}, u32[]{:S(2)}) %collective-permute-start.7) | collective-permute-done | bytes 294944 | tf_op jit(solution)/shard_map/ppermute | solution.py:276
  36.3 3.3 %collective-permute-done.9.refs_3_ = bf16[2,96,768]{2,1,0:T(8,128)(2,1)S(1)} collective-permute-done((bf16[2,96,768]{2,1,0:T(8,128)(2,1)S(1)}, bf16[2,96,768]{2,1,0:T(8,128)(2,1)S(1)}, u32[]{:S(2)}, u32[]{:S(2)}) %collective-permute-start.9) | collective-permute-done | bytes 294944 | tf_op jit(solution)/shard_map/ppermute | solution.py:276
  39.6 10.2 %shard_map.88 = (bf16[2,96,768]{2,1,0:T(8,128)(2,1)S(1)}, bf16[2,96,768]{2,1,0:T(8,128)(2,1)S(1)}, bf16[2,96,768]{2,1,0:T(8,128)(2,1)S(1)}, bf16[2,96,768]{2,1,0...) custom-call(f32[384,1152]{1,0:T(8,128)S(1)} %shard_map.85.bias_ref, ...), custom_call_target="tpu_custom_call" | custom-call | flops 4076863488 | bytes 16777216 | tf_op jit(solution)/shard_map/pallas_call | solution.py:178
  49.8 2.0 %collective-permute-start.11 = (bf16[4,2,96,768]{3,2,1,0:T(8,128)(2,1)S(1)}, bf16[4,2,96,768]{3,2,1,0:T(8,128)(2,1)S(1)}, u32[]{:S(2)}, u32[]{:S(2)}) collective-permute-start(bf16[4,2,96,768]{3,2,1,0:T(8,128)(2,1)S(1)} %get-tuple-element.71), channel_id=1, source_target_pairs={{0,1},{1,0},{2,3},{3,2},{4,5},{5,4},{6,7},{7,6},{8,9},{9,8},{10,11... | collective-permute-start | bytes 3538952 | tf_op jit(solution)/shard_map/ppermute | solution.py:285
  52.5 1.1 %collective-permute-start.13 = (bf16[2,96,768]{2,1,0:T(8,128)(2,1)S(1)}, bf16[2,96,768]{2,1,0:T(8,128)(2,1)S(1)}, u32[]{:S(2)}, u32[]{:S(2)}) collective-permute-start(bf16[2,96,768]{2,1,0:T(8,128)(2,1)S(1)} %get-tuple-element.74), channel_id=1, source_target_pairs={{2,0},{6,1},{0,2},{4,3},{3,4},{7,5},{1,6},{5,7},{10,8},{14,9},{8,1... | collective-permute-start | bytes 884744 | tf_op jit(solution)/shard_map/ppermute | solution.py:281
  53.6 2.5 %collective-permute-start.14 = (bf16[2,96,768]{2,1,0:T(8,128)(2,1)S(1)}, bf16[2,96,768]{2,1,0:T(8,128)(2,1)S(1)}, u32[]{:S(2)}, u32[]{:S(2)}) collective-permute-start(bf16[2,96,768]{2,1,0:T(8,128)(2,1)S(1)} %get-tuple-element.75), channel_id=1, source_target_pairs={{6,0},{2,1},{4,2},{0,3},{7,4},{3,5},{5,6},{1,7},{14,8},{10,9},{12,... | collective-permute-start | bytes 884744 | tf_op jit(solution)/shard_map/ppermute | solution.py:281
  56.8 3.3 %collective-permute-start.12 = (bf16[2,96,768]{2,1,0:T(8,128)(2,1)S(1)}, bf16[2,96,768]{2,1,0:T(8,128)(2,1)S(1)}, u32[]{:S(2)}, u32[]{:S(2)}) collective-permute-start(bf16[2,96,768]{2,1,0:T(8,128)(2,1)S(1)} %get-tuple-element.73), channel_id=1, source_target_pairs={{4,0},{0,1},{6,2},{2,3},{5,4},{1,5},{7,6},{3,7},{12,8},{8,9},{14,1... | collective-permute-start | bytes 884744 | tf_op jit(solution)/shard_map/ppermute | solution.py:281
  60.6 9.5 %collective-permute-start.17 = (bf16[2,96,768]{2,1,0:T(8,128)(2,1)S(1)}, bf16[2,96,768]{2,1,0:T(8,128)(2,1)S(1)}, u32[]{:S(2)}, u32[]{:S(2)}) collective-permute-start(bf16[2,96,768]{2,1,0:T(8,128)(2,1)S(1)} %get-tuple-element.82), channel_id=1, source_target_pairs={{4,0},{0,1},{6,2},{2,3},{5,4},{1,5},{7,6},{3,7},{12,8},{8,9},{14,1... | collective-permute-start | bytes 884744 | tf_op jit(solution)/shard_map/ppermute | solution.py:281
  71.1 1.3 %collective-permute-start.19 = (bf16[2,96,768]{2,1,0:T(8,128)(2,1)S(1)}, bf16[2,96,768]{2,1,0:T(8,128)(2,1)S(1)}, u32[]{:S(2)}, u32[]{:S(2)}) collective-permute-start(bf16[2,96,768]{2,1,0:T(8,128)(2,1)S(1)} %get-tuple-element.84), channel_id=1, source_target_pairs={{6,0},{2,1},{4,2},{0,3},{7,4},{3,5},{5,6},{1,7},{14,8},{10,9},{12,... | collective-permute-start | bytes 884744 | tf_op jit(solution)/shard_map/ppermute | solution.py:281
  73.1 1.1 %shard_map.89 = (bf16[96,3072]{1,0:T(8,128)(2,1)}, bf16[96,3072]{1,0:T(8,128)(2,1)}) custom-call(bf16[2,96,768]{2,1,0:T(8,128)(2,1)S(1)} %collective-permute-done.12.refs_0_, bf16[2,96,768]{2,1,0:T(8,128)(2,1)S(1)} %collective-permute-done.13.refs_1_, bf16[2,96,768]{2,1,0:T(8,128)(2,1)S(1)} %collective-permute-done.14.refs_2_, ...), custom_call_target="tpu_custom_call" | custom-call | bytes 2359296 | tf_op jit(solution)/shard_map/pallas_call | solution.py:83
  74.9 8.2 %collective-permute-done.18.refs_1_ = bf16[2,96,768]{2,1,0:T(8,128)(2,1)S(1)} collective-permute-done((bf16[2,96,768]{2,1,0:T(8,128)(2,1)S(1)}, bf16[2,96,768]{2,1,0:T(8,128)(2,1)S(1)}, u32[]{:S(2)}, u32[]{:S(2)}) %collective-permute-start.18) | collective-permute-done | bytes 294944 | tf_op jit(solution)/shard_map/ppermute | solution.py:281
  83.1 1.7 %collective-permute-done.19.refs_2_ = bf16[2,96,768]{2,1,0:T(8,128)(2,1)S(1)} collective-permute-done((bf16[2,96,768]{2,1,0:T(8,128)(2,1)S(1)}, bf16[2,96,768]{2,1,0:T(8,128)(2,1)S(1)}, u32[]{:S(2)}, u32[]{:S(2)}) %collective-permute-start.19) | collective-permute-done | bytes 294944 | tf_op jit(solution)/shard_map/ppermute | solution.py:281
  84.8 1.1 %shard_map.91 = (bf16[96,3072]{1,0:T(8,128)(2,1)}, bf16[96,3072]{1,0:T(8,128)(2,1)}) custom-call(bf16[2,96,768]{2,1,0:T(8,128)(2,1)S(1)} %collective-permute-done.17.refs_0_, bf16[2,96,768]{2,1,0:T(8,128)(2,1)S(1)} %collective-permute-done.18.refs_1_, bf16[2,96,768]{2,1,0:T(8,128)(2,1)S(1)} %collective-permute-done.19.refs_2_, ...), custom_call_target="tpu_custom_call" | custom-call | bytes 2359296 | tf_op jit(solution)/shard_map/pallas_call | solution.py:83
  (36 shorter events, 9.1 us)
Async XLA Ops:
  2.8 8.1 %copy-start.4 = (s32[6,16]{1,0:T(8,128)S(1)}, s32[6,16]{1,0:T(8,128)}, u32[]{:S(2)}) copy-start(s32[6,16]{1,0:T(8,128)} %param.9) | copy-start | bytes 1156
  2.8 8.8 %copy-start.2 = (bf16[96,3072]{1,0:T(8,128)(2,1)S(1)}, bf16[96,3072]{1,0:T(8,128)(2,1)}, u32[]{:S(2)}) copy-start(bf16[96,3072]{1,0:T(8,128)(2,1)} %first.2) | copy-start | bytes 1769476
  2.8 8.8 %copy-start.3 = (bf16[96,3072]{1,0:T(8,128)(2,1)S(1)}, bf16[96,3072]{1,0:T(8,128)(2,1)}, u32[]{:S(2)}) copy-start(bf16[96,3072]{1,0:T(8,128)(2,1)} %second.3) | copy-start | bytes 1769476
  3.0 11.9 %collective-permute-start = (bf16[2,96,768]{2,1,0:T(8,128)(2,1)S(1)}, bf16[2,96,768]{2,1,0:T(8,128)(2,1)S(1)}, u32[]{:S(2)}, u32[]{:S(2)}) collective-permute-start(bf16[2,96,768]{2,1,0:T(8,128)(2,1)S(1)} %get-tuple-element.50), channel_id=1, source_target_pairs={{0,6},{1,2},{2,4},{3,0},{4,7},{5,3},{6,5},{7,1},{8,14},{9,10},{10,... | collective-permute-start | bytes 884744 | tf_op jit(solution)/shard_map/ppermute | solution.py:276
  7.0 7.9 %collective-permute-start.1 = (bf16[2,96,768]{2,1,0:T(8,128)(2,1)S(1)}, bf16[2,96,768]{2,1,0:T(8,128)(2,1)S(1)}, u32[]{:S(2)}, u32[]{:S(2)}) collective-permute-start(bf16[2,96,768]{2,1,0:T(8,128)(2,1)S(1)} %get-tuple-element.51), channel_id=1, source_target_pairs={{0,0},{1,4},{2,2},{3,6},{4,1},{5,5},{6,3},{7,7},{8,8},{9,12},{10,1... | collective-permute-start | bytes 884744 | tf_op jit(solution)/shard_map/ppermute | solution.py:276
  7.7 10.2 %collective-permute-start.2 = (bf16[2,96,768]{2,1,0:T(8,128)(2,1)S(1)}, bf16[2,96,768]{2,1,0:T(8,128)(2,1)S(1)}, u32[]{:S(2)}, u32[]{:S(2)}) collective-permute-start(bf16[2,96,768]{2,1,0:T(8,128)(2,1)S(1)} %get-tuple-element.52), channel_id=1, source_target_pairs={{0,2},{1,6},{2,0},{3,4},{4,3},{5,7},{6,1},{7,5},{8,10},{9,14},{10,... | collective-permute-start | bytes 884744 | tf_op jit(solution)/shard_map/ppermute | solution.py:276
  8.2 11.2 %collective-permute-start.3 = (bf16[2,96,768]{2,1,0:T(8,128)(2,1)S(1)}, bf16[2,96,768]{2,1,0:T(8,128)(2,1)S(1)}, u32[]{:S(2)}, u32[]{:S(2)}) collective-permute-start(bf16[2,96,768]{2,1,0:T(8,128)(2,1)S(1)} %get-tuple-element.53), channel_id=1, source_target_pairs={{0,4},{1,0},{2,6},{3,2},{4,5},{5,1},{6,7},{7,3},{8,12},{9,8},{10,1... | collective-permute-start | bytes 884744 | tf_op jit(solution)/shard_map/ppermute | solution.py:276
  10.9 1.0 %collective-permute-start.4 = (s32[6,16]{1,0:T(8,128)S(1)}, s32[6,16]{1,0:T(8,128)S(1)}, u32[]{:S(2)}, u32[]{:S(2)}) collective-permute-start(s32[6,16]{1,0:T(8,128)S(1)} %copy-done.4), channel_id=1, source_target_pairs={{0,0},{1,4},{2,2},{3,6},{4,1},{5,5},{6,3},{7,7},{8,8},{9,12},{10,1... | collective-permute-start | bytes 1160 | tf_op jit(solution)/shard_map/ppermute | solution.py:240
  19.7 7.0 %collective-permute-start.8 = (bf16[4,2,96,768]{3,2,1,0:T(8,128)(2,1)S(1)}, bf16[4,2,96,768]{3,2,1,0:T(8,128)(2,1)S(1)}, u32[]{:S(2)}, u32[]{:S(2)}) collective-permute-start(bf16[4,2,96,768]{3,2,1,0:T(8,128)(2,1)S(1)} %shard_map.87.refs_4_), channel_id=1, source_target_pairs={{0,1},{1,0},{2,3},{3,2},{4,5},{5,4},{6,7},{7,6},{8,9},{9,8},{10,11... | collective-permute-start | bytes 3538952 | tf_op jit(solution)/shard_map/ppermute | solution.py:285
  21.3 15.0 %collective-permute-start.10 = (bf16[4,2,96,768]{3,2,1,0:T(8,128)(2,1)S(1)}, bf16[4,2,96,768]{3,2,1,0:T(8,128)(2,1)S(1)}, u32[]{:S(2)}, u32[]{:S(2)}) collective-permute-start(bf16[4,2,96,768]{3,2,1,0:T(8,128)(2,1)S(1)} %shard_map.87.refs_4_), channel_id=1, source_target_pairs={{0,0},{1,8},{2,2},{3,10},{4,4},{5,12},{6,6},{7,14},{8,1},{9,16},{1... | collective-permute-start | bytes 3538952 | tf_op jit(solution)/shard_map/ppermute | solution.py:288
  22.0 12.0 %collective-permute-start.5 = (bf16[2,96,768]{2,1,0:T(8,128)(2,1)S(1)}, bf16[2,96,768]{2,1,0:T(8,128)(2,1)S(1)}, u32[]{:S(2)}, u32[]{:S(2)}) collective-permute-start(bf16[2,96,768]{2,1,0:T(8,128)(2,1)S(1)} %get-tuple-element.57), channel_id=1, source_target_pairs={{0,6},{1,2},{2,4},{3,0},{4,7},{5,3},{6,5},{7,1},{8,14},{9,10},{10,... | collective-permute-start | bytes 884744 | tf_op jit(solution)/shard_map/ppermute | solution.py:276
  25.3 8.7 %collective-permute-start.6 = (bf16[2,96,768]{2,1,0:T(8,128)(2,1)S(1)}, bf16[2,96,768]{2,1,0:T(8,128)(2,1)S(1)}, u32[]{:S(2)}, u32[]{:S(2)}) collective-permute-start(bf16[2,96,768]{2,1,0:T(8,128)(2,1)S(1)} %get-tuple-element.65), channel_id=1, source_target_pairs={{0,0},{1,4},{2,2},{3,6},{4,1},{5,5},{6,3},{7,7},{8,8},{9,12},{10,1... | collective-permute-start | bytes 884744 | tf_op jit(solution)/shard_map/ppermute | solution.py:276
  26.0 10.3 %collective-permute-start.7 = (bf16[2,96,768]{2,1,0:T(8,128)(2,1)S(1)}, bf16[2,96,768]{2,1,0:T(8,128)(2,1)S(1)}, u32[]{:S(2)}, u32[]{:S(2)}) collective-permute-start(bf16[2,96,768]{2,1,0:T(8,128)(2,1)S(1)} %get-tuple-element.66), channel_id=1, source_target_pairs={{0,2},{1,6},{2,0},{3,4},{4,3},{5,7},{6,1},{7,5},{8,10},{9,14},{10,... | collective-permute-start | bytes 884744 | tf_op jit(solution)/shard_map/ppermute | solution.py:276
  26.7 12.9 %collective-permute-start.9 = (bf16[2,96,768]{2,1,0:T(8,128)(2,1)S(1)}, bf16[2,96,768]{2,1,0:T(8,128)(2,1)S(1)}, u32[]{:S(2)}, u32[]{:S(2)}) collective-permute-start(bf16[2,96,768]{2,1,0:T(8,128)(2,1)S(1)} %get-tuple-element.69), channel_id=1, source_target_pairs={{0,4},{1,0},{2,6},{3,2},{4,5},{5,1},{6,7},{7,3},{8,12},{9,8},{10,1... | collective-permute-start | bytes 884744 | tf_op jit(solution)/shard_map/ppermute | solution.py:276
  49.8 7.0 %collective-permute-start.11 = (bf16[4,2,96,768]{3,2,1,0:T(8,128)(2,1)S(1)}, bf16[4,2,96,768]{3,2,1,0:T(8,128)(2,1)S(1)}, u32[]{:S(2)}, u32[]{:S(2)}) collective-permute-start(bf16[4,2,96,768]{3,2,1,0:T(8,128)(2,1)S(1)} %get-tuple-element.71), channel_id=1, source_target_pairs={{0,1},{1,0},{2,3},{3,2},{4,5},{5,4},{6,7},{7,6},{8,9},{9,8},{10,11... | collective-permute-start | bytes 3538952 | tf_op jit(solution)/shard_map/ppermute | solution.py:285
  51.8 8.3 %collective-permute-start.16 = (bf16[4,2,96,768]{3,2,1,0:T(8,128)(2,1)S(1)}, bf16[4,2,96,768]{3,2,1,0:T(8,128)(2,1)S(1)}, u32[]{:S(2)}, u32[]{:S(2)}) collective-permute-start(bf16[4,2,96,768]{3,2,1,0:T(8,128)(2,1)S(1)} %get-tuple-element.81), channel_id=1, source_target_pairs={{0,0},{1,8},{2,2},{3,10},{4,4},{5,12},{6,6},{7,14},{8,1},{9,16},{1... | collective-permute-start | bytes 3538952 | tf_op jit(solution)/shard_map/ppermute | solution.py:288
  52.5 17.5 %collective-permute-start.13 = (bf16[2,96,768]{2,1,0:T(8,128)(2,1)S(1)}, bf16[2,96,768]{2,1,0:T(8,128)(2,1)S(1)}, u32[]{:S(2)}, u32[]{:S(2)}) collective-permute-start(bf16[2,96,768]{2,1,0:T(8,128)(2,1)S(1)} %get-tuple-element.74), channel_id=1, source_target_pairs={{2,0},{6,1},{0,2},{4,3},{3,4},{7,5},{1,6},{5,7},{10,8},{14,9},{8,1... | collective-permute-start | bytes 884744 | tf_op jit(solution)/shard_map/ppermute | solution.py:281
  53.6 17.5 %collective-permute-start.14 = (bf16[2,96,768]{2,1,0:T(8,128)(2,1)S(1)}, bf16[2,96,768]{2,1,0:T(8,128)(2,1)S(1)}, u32[]{:S(2)}, u32[]{:S(2)}) collective-permute-start(bf16[2,96,768]{2,1,0:T(8,128)(2,1)S(1)} %get-tuple-element.75), channel_id=1, source_target_pairs={{6,0},{2,1},{4,2},{0,3},{7,4},{3,5},{5,6},{1,7},{14,8},{10,9},{12,... | collective-permute-start | bytes 884744 | tf_op jit(solution)/shard_map/ppermute | solution.py:281
  56.1 16.3 %collective-permute-start.15 = (bf16[2,96,768]{2,1,0:T(8,128)(2,1)S(1)}, bf16[2,96,768]{2,1,0:T(8,128)(2,1)S(1)}, u32[]{:S(2)}, u32[]{:S(2)}) collective-permute-start(bf16[2,96,768]{2,1,0:T(8,128)(2,1)S(1)} %get-tuple-element.76), channel_id=1, source_target_pairs={{0,0},{4,1},{2,2},{6,3},{1,4},{5,5},{3,6},{7,7},{8,8},{12,9},{10,1... | collective-permute-start | bytes 884744 | tf_op jit(solution)/shard_map/ppermute | solution.py:281
  56.8 16.3 %collective-permute-start.12 = (bf16[2,96,768]{2,1,0:T(8,128)(2,1)S(1)}, bf16[2,96,768]{2,1,0:T(8,128)(2,1)S(1)}, u32[]{:S(2)}, u32[]{:S(2)}) collective-permute-start(bf16[2,96,768]{2,1,0:T(8,128)(2,1)S(1)} %get-tuple-element.73), channel_id=1, source_target_pairs={{4,0},{0,1},{6,2},{2,3},{5,4},{1,5},{7,6},{3,7},{12,8},{8,9},{14,1... | collective-permute-start | bytes 884744 | tf_op jit(solution)/shard_map/ppermute | solution.py:281
  60.6 14.3 %collective-permute-start.17 = (bf16[2,96,768]{2,1,0:T(8,128)(2,1)S(1)}, bf16[2,96,768]{2,1,0:T(8,128)(2,1)S(1)}, u32[]{:S(2)}, u32[]{:S(2)}) collective-permute-start(bf16[2,96,768]{2,1,0:T(8,128)(2,1)S(1)} %get-tuple-element.82), channel_id=1, source_target_pairs={{4,0},{0,1},{6,2},{2,3},{5,4},{1,5},{7,6},{3,7},{12,8},{8,9},{14,1... | collective-permute-start | bytes 884744 | tf_op jit(solution)/shard_map/ppermute | solution.py:281
  70.1 13.0 %collective-permute-start.18 = (bf16[2,96,768]{2,1,0:T(8,128)(2,1)S(1)}, bf16[2,96,768]{2,1,0:T(8,128)(2,1)S(1)}, u32[]{:S(2)}, u32[]{:S(2)}) collective-permute-start(bf16[2,96,768]{2,1,0:T(8,128)(2,1)S(1)} %get-tuple-element.83), channel_id=1, source_target_pairs={{2,0},{6,1},{0,2},{4,3},{3,4},{7,5},{1,6},{5,7},{10,8},{14,9},{8,1... | collective-permute-start | bytes 884744 | tf_op jit(solution)/shard_map/ppermute | solution.py:281
  71.1 13.7 %collective-permute-start.19 = (bf16[2,96,768]{2,1,0:T(8,128)(2,1)S(1)}, bf16[2,96,768]{2,1,0:T(8,128)(2,1)S(1)}, u32[]{:S(2)}, u32[]{:S(2)}) collective-permute-start(bf16[2,96,768]{2,1,0:T(8,128)(2,1)S(1)} %get-tuple-element.84), channel_id=1, source_target_pairs={{6,0},{2,1},{4,2},{0,3},{7,4},{3,5},{5,6},{1,7},{14,8},{10,9},{12,... | collective-permute-start | bytes 884744 | tf_op jit(solution)/shard_map/ppermute | solution.py:281
  72.4 12.4 %collective-permute-start.20 = (bf16[2,96,768]{2,1,0:T(8,128)(2,1)S(1)}, bf16[2,96,768]{2,1,0:T(8,128)(2,1)S(1)}, u32[]{:S(2)}, u32[]{:S(2)}) collective-permute-start(bf16[2,96,768]{2,1,0:T(8,128)(2,1)S(1)} %get-tuple-element.85), channel_id=1, source_target_pairs={{0,0},{4,1},{2,2},{6,3},{1,4},{5,5},{3,6},{7,7},{8,8},{12,9},{10,1... | collective-permute-start | bytes 884744 | tf_op jit(solution)/shard_map/ppermute | solution.py:281
  (2 other events, 2.1 us)

commit v7 on v6

--- a/solution.py
+++ b/solution.py
@@ -11,12 +11,12 @@
 
 HD = 128
 TILE = 64
-BACK = (3, 2, 0, 1)
+BACK = (2, 1, 0, 3)
 EARLY = 1
 MASKED = -1e30
 AXES = ("group", "pair", "row", "core")
 PLANE = ("pair", "row", "core")
-SHIFTS = ((1, 1), (0, 0), (0, 1), (1, 0))
+SHIFTS = ((1, 1), (0, 1), (1, 0), (0, 0))
 BF16 = jnp.bfloat16
 ANY = pl.BlockSpec(memory_space=pl.ANY)
 FAR = pl.BlockSpec(memory_space=pltpu.HBM)

time: 87.1 us -> 85.5 us (0.982)
  starting transfers between devices: 43.7 us -> 35.3 us
  waiting for transfers between devices: 23.9 us -> 30.5 us
    ppermute x8, waiting for transfers between devices: 13.2 us -> 20.4 us  [send(): lax.ppermute(m, AXES, spread_pairs(s))]
    ppermute x8, starting transfers between devices: 17.9 us -> 11.7 us  [send(): lax.ppermute(m, AXES, spread_pairs(s))]
    ppermute x2, starting transfers between devices: 3.58 us -> 1.34 us  [across(): return lax.ppermute(x, 'core', [(0, 1), (1, 0)])]
  transfers between devices with their start and end apart: 21 -> 21, of which waited for: 8 -> 7; matrix products, arithmetic and copies ran while one was open for 0% -> 0% of each run, Pallas kernels for 4% -> 4%
where the time goes in v7:
time: 85.5 us; the launch traced here: 84.2 us
  starting transfers between devices  35.3 us (41%)
  waiting for transfers between devices  30.5 us (36%)
  Pallas kernels  15.4 us (18%)
  local copies, waits for them, and re-layouts  2.13 us (2%)
    ppermute x8, waiting for transfers between devices, send(): lax.ppermute(m, AXES, spread_pairs(s))  20.4 us
    ppermute x8, starting transfers between devices, send_back(): lax.ppermute(messages[i], AXES, [(d, s) for s, d in spread_pairs(SHIFTS[i...  20.2 us
    ppermute x8, starting transfers between devices, send(): lax.ppermute(m, AXES, spread_pairs(s))  11.7 us
    pallas_call x1, Pallas kernels, attend(): pl.pallas_call(attend_kernel, in_specs=[NEAR] * 8, out_specs=[NEAR] * 7,...  10.2 us
    ppermute x8, waiting for transfers between devices, send_back(): lax.ppermute(messages[i], AXES, [(d, s) for s, d in spread_pairs(SHIFTS[i...  10.1 us
    pallas_call x2, Pallas kernels, unpack(): pl.pallas_call(functools.partial(unpack_kernel, order), in_specs=[NEAR] *...  2.16 us
    unnamed x10, local copies, waits for them, and re-layouts  2.13 us
    pallas_call x1, Pallas kernels, window_bias(): pl.pallas_call(functools.partial(bias_kernel, rows), in_specs=[pl.BlockSp...  1.83 us
  transfers between devices with their start and end apart: 21, of which 7 were waited for; matrix products, arithmetic and copies ran while one was open for 0% of the time, Pallas kernels for 4%

profile of v7, /device:TPU:0, one launch (start us, length us, event | category | flops | bytes accessed | tf_op | source)
XLA Modules:
  0.0 84.2 jit_solution(980678435939422748)
XLA Ops:
  0.6 1.1 %copy-done = bf16[96,3072]{1,0:T(8,128)(2,1)S(1)} copy-done((bf16[96,3072]{1,0:T(8,128)(2,1)S(1)}, bf16[96,3072]{1,0:T(8,128)(2,1)}, u32[]{:S(2)}) %copy-start) | copy-done | bytes 589848
  1.7 1.1 %copy-done.1 = bf16[96,3072]{1,0:T(8,128)(2,1)S(1)} copy-done((bf16[96,3072]{1,0:T(8,128)(2,1)S(1)}, bf16[96,3072]{1,0:T(8,128)(2,1)}, u32[]{:S(2)}) %copy-start.1) | copy-done | bytes 589848
  3.0 4.0 %collective-permute-start = (bf16[2,96,768]{2,1,0:T(8,128)(2,1)S(1)}, bf16[2,96,768]{2,1,0:T(8,128)(2,1)S(1)}, u32[]{:S(2)}, u32[]{:S(2)}) collective-permute-start(bf16[2,96,768]{2,1,0:T(8,128)(2,1)S(1)} %get-tuple-element.50), channel_id=1, source_target_pairs={{0,6},{1,2},{2,4},{3,0},{4,7},{5,3},{6,5},{7,1},{8,14},{9,10},{10,... | collective-permute-start | bytes 884744 | tf_op jit(solution)/shard_map/ppermute | solution.py:276
  9.2 9.1 %collective-permute-done.refs_0_ = bf16[2,96,768]{2,1,0:T(8,128)(2,1)S(1)} collective-permute-done((bf16[2,96,768]{2,1,0:T(8,128)(2,1)S(1)}, bf16[2,96,768]{2,1,0:T(8,128)(2,1)S(1)}, u32[]{:S(2)}, u32[]{:S(2)}) %collective-permute-start) | collective-permute-done | bytes 294944 | tf_op jit(solution)/shard_map/ppermute | solution.py:276
  18.3 1.1 %collective-permute-done.1.refs_1_ = bf16[2,96,768]{2,1,0:T(8,128)(2,1)S(1)} collective-permute-done((bf16[2,96,768]{2,1,0:T(8,128)(2,1)S(1)}, bf16[2,96,768]{2,1,0:T(8,128)(2,1)S(1)}, u32[]{:S(2)}, u32[]{:S(2)}) %collective-permute-start.1) | collective-permute-done | bytes 294944 | tf_op jit(solution)/shard_map/ppermute | solution.py:276
  19.4 0.9 %collective-permute-done.2.refs_2_ = bf16[2,96,768]{2,1,0:T(8,128)(2,1)S(1)} collective-permute-done((bf16[2,96,768]{2,1,0:T(8,128)(2,1)S(1)}, bf16[2,96,768]{2,1,0:T(8,128)(2,1)S(1)}, u32[]{:S(2)}, u32[]{:S(2)}) %collective-permute-start.2) | collective-permute-done | bytes 294944 | tf_op jit(solution)/shard_map/ppermute | solution.py:276
  21.6 2.8 %collective-permute-start.5 = (bf16[2,96,768]{2,1,0:T(8,128)(2,1)S(1)}, bf16[2,96,768]{2,1,0:T(8,128)(2,1)S(1)}, u32[]{:S(2)}, u32[]{:S(2)}) collective-permute-start(bf16[2,96,768]{2,1,0:T(8,128)(2,1)S(1)} %get-tuple-element.57), channel_id=1, source_target_pairs={{0,6},{1,2},{2,4},{3,0},{4,7},{5,3},{6,5},{7,1},{8,14},{9,10},{10,... | collective-permute-start | bytes 884744 | tf_op jit(solution)/shard_map/ppermute | solution.py:276
  24.4 1.0 %collective-permute-start.6 = (bf16[2,96,768]{2,1,0:T(8,128)(2,1)S(1)}, bf16[2,96,768]{2,1,0:T(8,128)(2,1)S(1)}, u32[]{:S(2)}, u32[]{:S(2)}) collective-permute-start(bf16[2,96,768]{2,1,0:T(8,128)(2,1)S(1)} %get-tuple-element.65), channel_id=1, source_target_pairs={{0,2},{1,6},{2,0},{3,4},{4,3},{5,7},{6,1},{7,5},{8,10},{9,14},{10,... | collective-permute-start | bytes 884744 | tf_op jit(solution)/shard_map/ppermute | solution.py:276
  25.4 2.0 %collective-permute-start.7 = (bf16[2,96,768]{2,1,0:T(8,128)(2,1)S(1)}, bf16[2,96,768]{2,1,0:T(8,128)(2,1)S(1)}, u32[]{:S(2)}, u32[]{:S(2)}) collective-permute-start(bf16[2,96,768]{2,1,0:T(8,128)(2,1)S(1)} %get-tuple-element.66), channel_id=1, source_target_pairs={{0,4},{1,0},{2,6},{3,2},{4,5},{5,1},{6,7},{7,3},{8,12},{9,8},{10,1... | collective-permute-start | bytes 884744 | tf_op jit(solution)/shard_map/ppermute | solution.py:276
  28.1 1.8 %shard_map.85.bias_ref = f32[384,1152]{1,0:T(8,128)S(1)} custom-call(s32[6,16]{1,0:T(8,128)S(1)} %collective-permute-done.4.ids_ref), custom_call_target="tpu_custom_call" | custom-call | flops 2949120 | bytes 1769472 | tf_op jit(solution)/shard_map/pallas_call | solution.py:245
  30.0 7.8 %collective-permute-done.5.refs_0_ = bf16[2,96,768]{2,1,0:T(8,128)(2,1)S(1)} collective-permute-done((bf16[2,96,768]{2,1,0:T(8,128)(2,1)S(1)}, bf16[2,96,768]{2,1,0:T(8,128)(2,1)S(1)}, u32[]{:S(2)}, u32[]{:S(2)}) %collective-permute-start.5) | collective-permute-done | bytes 294944 | tf_op jit(solution)/shard_map/ppermute | solution.py:276
  37.8 1.5 %collective-permute-done.6.refs_1_ = bf16[2,96,768]{2,1,0:T(8,128)(2,1)S(1)} collective-permute-done((bf16[2,96,768]{2,1,0:T(8,128)(2,1)S(1)}, bf16[2,96,768]{2,1,0:T(8,128)(2,1)S(1)}, u32[]{:S(2)}, u32[]{:S(2)}) %collective-permute-start.6) | collective-permute-done | bytes 294944 | tf_op jit(solution)/shard_map/ppermute | solution.py:276
  39.2 10.2 %shard_map.88 = (bf16[2,96,768]{2,1,0:T(8,128)(2,1)S(1)}, bf16[2,96,768]{2,1,0:T(8,128)(2,1)S(1)}, bf16[2,96,768]{2,1,0:T(8,128)(2,1)S(1)}, bf16[2,96,768]{2,1,0...) custom-call(f32[384,1152]{1,0:T(8,128)S(1)} %shard_map.85.bias_ref, ...), custom_call_target="tpu_custom_call" | custom-call | flops 4076863488 | bytes 16777216 | tf_op jit(solution)/shard_map/pallas_call | solution.py:178
  49.4 1.1 %collective-permute-start.14 = (bf16[4,2,96,768]{3,2,1,0:T(8,128)(2,1)S(1)}, bf16[4,2,96,768]{3,2,1,0:T(8,128)(2,1)S(1)}, u32[]{:S(2)}, u32[]{:S(2)}) collective-permute-start(bf16[4,2,96,768]{3,2,1,0:T(8,128)(2,1)S(1)} %get-tuple-element.74), channel_id=1, source_target_pairs={{0,1},{1,0},{2,3},{3,2},{4,5},{5,4},{6,7},{7,6},{8,9},{9,8},{10,11... | collective-permute-start | bytes 3538952 | tf_op jit(solution)/shard_map/ppermute | solution.py:285
  51.3 2.9 %collective-permute-start.11 = (bf16[2,96,768]{2,1,0:T(8,128)(2,1)S(1)}, bf16[2,96,768]{2,1,0:T(8,128)(2,1)S(1)}, u32[]{:S(2)}, u32[]{:S(2)}) collective-permute-start(bf16[2,96,768]{2,1,0:T(8,128)(2,1)S(1)} %get-tuple-element.71), channel_id=1, source_target_pairs={{4,0},{0,1},{6,2},{2,3},{5,4},{1,5},{7,6},{3,7},{12,8},{8,9},{14,1... | collective-permute-start | bytes 884744 | tf_op jit(solution)/shard_map/ppermute | solution.py:281
  54.1 0.9 %collective-permute-start.12 = (bf16[2,96,768]{2,1,0:T(8,128)(2,1)S(1)}, bf16[2,96,768]{2,1,0:T(8,128)(2,1)S(1)}, u32[]{:S(2)}, u32[]{:S(2)}) collective-permute-start(bf16[2,96,768]{2,1,0:T(8,128)(2,1)S(1)} %get-tuple-element.72), channel_id=1, source_target_pairs={{2,0},{6,1},{0,2},{4,3},{3,4},{7,5},{1,6},{5,7},{10,8},{14,9},{8,1... | collective-permute-start | bytes 884744 | tf_op jit(solution)/shard_map/ppermute | solution.py:281
  55.1 1.5 %collective-permute-start.13 = (bf16[2,96,768]{2,1,0:T(8,128)(2,1)S(1)}, bf16[2,96,768]{2,1,0:T(8,128)(2,1)S(1)}, u32[]{:S(2)}, u32[]{:S(2)}) collective-permute-start(bf16[2,96,768]{2,1,0:T(8,128)(2,1)S(1)} %get-tuple-element.73), channel_id=1, source_target_pairs={{6,0},{2,1},{4,2},{0,3},{7,4},{3,5},{5,6},{1,7},{14,8},{10,9},{12,... | collective-permute-start | bytes 884744 | tf_op jit(solution)/shard_map/ppermute | solution.py:281
  57.7 10.8 %collective-permute-start.17 = (bf16[2,96,768]{2,1,0:T(8,128)(2,1)S(1)}, bf16[2,96,768]{2,1,0:T(8,128)(2,1)S(1)}, u32[]{:S(2)}, u32[]{:S(2)}) collective-permute-start(bf16[2,96,768]{2,1,0:T(8,128)(2,1)S(1)} %get-tuple-element.82), channel_id=1, source_target_pairs={{4,0},{0,1},{6,2},{2,3},{5,4},{1,5},{7,6},{3,7},{12,8},{8,9},{14,1... | collective-permute-start | bytes 884744 | tf_op jit(solution)/shard_map/ppermute | solution.py:281
  68.5 0.9 %collective-permute-start.18 = (bf16[2,96,768]{2,1,0:T(8,128)(2,1)S(1)}, bf16[2,96,768]{2,1,0:T(8,128)(2,1)S(1)}, u32[]{:S(2)}, u32[]{:S(2)}) collective-permute-start(bf16[2,96,768]{2,1,0:T(8,128)(2,1)S(1)} %get-tuple-element.83), channel_id=1, source_target_pairs={{2,0},{6,1},{0,2},{4,3},{3,4},{7,5},{1,6},{5,7},{10,8},{14,9},{8,1... | collective-permute-start | bytes 884744 | tf_op jit(solution)/shard_map/ppermute | solution.py:281
  69.4 1.8 %collective-permute-start.19 = (bf16[2,96,768]{2,1,0:T(8,128)(2,1)S(1)}, bf16[2,96,768]{2,1,0:T(8,128)(2,1)S(1)}, u32[]{:S(2)}, u32[]{:S(2)}) collective-permute-start(bf16[2,96,768]{2,1,0:T(8,128)(2,1)S(1)} %get-tuple-element.84), channel_id=1, source_target_pairs={{6,0},{2,1},{4,2},{0,3},{7,4},{3,5},{5,6},{1,7},{14,8},{10,9},{12,... | collective-permute-start | bytes 884744 | tf_op jit(solution)/shard_map/ppermute | solution.py:281
  72.0 1.1 %shard_map.89 = (bf16[96,3072]{1,0:T(8,128)(2,1)}, bf16[96,3072]{1,0:T(8,128)(2,1)}) custom-call(bf16[2,96,768]{2,1,0:T(8,128)(2,1)S(1)} %collective-permute-done.11.refs_0_, bf16[2,96,768]{2,1,0:T(8,128)(2,1)S(1)} %collective-permute-done.12.refs_1_, bf16[2,96,768]{2,1,0:T(8,128)(2,1)S(1)} %collective-permute-done.13.refs_2_, ...), custom_call_target="tpu_custom_call" | custom-call | bytes 2359296 | tf_op jit(solution)/shard_map/pallas_call | solution.py:83
  73.1 8.5 %collective-permute-done.18.refs_1_ = bf16[2,96,768]{2,1,0:T(8,128)(2,1)S(1)} collective-permute-done((bf16[2,96,768]{2,1,0:T(8,128)(2,1)S(1)}, bf16[2,96,768]{2,1,0:T(8,128)(2,1)S(1)}, u32[]{:S(2)}, u32[]{:S(2)}) %collective-permute-start.18) | collective-permute-done | bytes 294944 | tf_op jit(solution)/shard_map/ppermute | solution.py:281
  81.5 1.6 %collective-permute-done.19.refs_2_ = bf16[2,96,768]{2,1,0:T(8,128)(2,1)S(1)} collective-permute-done((bf16[2,96,768]{2,1,0:T(8,128)(2,1)S(1)}, bf16[2,96,768]{2,1,0:T(8,128)(2,1)S(1)}, u32[]{:S(2)}, u32[]{:S(2)}) %collective-permute-start.19) | collective-permute-done | bytes 294944 | tf_op jit(solution)/shard_map/ppermute | solution.py:281
  83.2 1.1 %shard_map.91 = (bf16[96,3072]{1,0:T(8,128)(2,1)}, bf16[96,3072]{1,0:T(8,128)(2,1)}) custom-call(bf16[2,96,768]{2,1,0:T(8,128)(2,1)S(1)} %collective-permute-done.17.refs_0_, bf16[2,96,768]{2,1,0:T(8,128)(2,1)S(1)} %collective-permute-done.18.refs_1_, bf16[2,96,768]{2,1,0:T(8,128)(2,1)S(1)} %collective-permute-done.19.refs_2_, ...), custom_call_target="tpu_custom_call" | custom-call | bytes 2359296 | tf_op jit(solution)/shard_map/pallas_call | solution.py:83
  (36 shorter events, 6.8 us)
Async XLA Ops:
  2.8 5.4 %copy-start.4 = (s32[6,16]{1,0:T(8,128)S(1)}, s32[6,16]{1,0:T(8,128)}, u32[]{:S(2)}) copy-start(s32[6,16]{1,0:T(8,128)} %param.9) | copy-start | bytes 1156
  2.8 6.1 %copy-start.2 = (bf16[96,3072]{1,0:T(8,128)(2,1)S(1)}, bf16[96,3072]{1,0:T(8,128)(2,1)}, u32[]{:S(2)}) copy-start(bf16[96,3072]{1,0:T(8,128)(2,1)} %first.2) | copy-start | bytes 1769476
  2.8 6.1 %copy-start.3 = (bf16[96,3072]{1,0:T(8,128)(2,1)S(1)}, bf16[96,3072]{1,0:T(8,128)(2,1)}, u32[]{:S(2)}) copy-start(bf16[96,3072]{1,0:T(8,128)(2,1)} %second.3) | copy-start | bytes 1769476
  3.0 15.3 %collective-permute-start = (bf16[2,96,768]{2,1,0:T(8,128)(2,1)S(1)}, bf16[2,96,768]{2,1,0:T(8,128)(2,1)S(1)}, u32[]{:S(2)}, u32[]{:S(2)}) collective-permute-start(bf16[2,96,768]{2,1,0:T(8,128)(2,1)S(1)} %get-tuple-element.50), channel_id=1, source_target_pairs={{0,6},{1,2},{2,4},{3,0},{4,7},{5,3},{6,5},{7,1},{8,14},{9,10},{10,... | collective-permute-start | bytes 884744 | tf_op jit(solution)/shard_map/ppermute | solution.py:276
  7.0 12.4 %collective-permute-start.1 = (bf16[2,96,768]{2,1,0:T(8,128)(2,1)S(1)}, bf16[2,96,768]{2,1,0:T(8,128)(2,1)S(1)}, u32[]{:S(2)}, u32[]{:S(2)}) collective-permute-start(bf16[2,96,768]{2,1,0:T(8,128)(2,1)S(1)} %get-tuple-element.51), channel_id=1, source_target_pairs={{0,2},{1,6},{2,0},{3,4},{4,3},{5,7},{6,1},{7,5},{8,10},{9,14},{10,... | collective-permute-start | bytes 884744 | tf_op jit(solution)/shard_map/ppermute | solution.py:276
  7.5 12.8 %collective-permute-start.2 = (bf16[2,96,768]{2,1,0:T(8,128)(2,1)S(1)}, bf16[2,96,768]{2,1,0:T(8,128)(2,1)S(1)}, u32[]{:S(2)}, u32[]{:S(2)}) collective-permute-start(bf16[2,96,768]{2,1,0:T(8,128)(2,1)S(1)} %get-tuple-element.52), channel_id=1, source_target_pairs={{0,4},{1,0},{2,6},{3,2},{4,5},{5,1},{6,7},{7,3},{8,12},{9,8},{10,1... | collective-permute-start | bytes 884744 | tf_op jit(solution)/shard_map/ppermute | solution.py:276
  7.5 12.8 %collective-permute-start.3 = (bf16[2,96,768]{2,1,0:T(8,128)(2,1)S(1)}, bf16[2,96,768]{2,1,0:T(8,128)(2,1)S(1)}, u32[]{:S(2)}, u32[]{:S(2)}) collective-permute-start(bf16[2,96,768]{2,1,0:T(8,128)(2,1)S(1)} %get-tuple-element.53), channel_id=1, source_target_pairs={{0,0},{1,4},{2,2},{3,6},{4,1},{5,5},{6,3},{7,7},{8,8},{9,12},{10,1... | collective-permute-start | bytes 884744 | tf_op jit(solution)/shard_map/ppermute | solution.py:276
  8.2 1.0 %collective-permute-start.4 = (s32[6,16]{1,0:T(8,128)S(1)}, s32[6,16]{1,0:T(8,128)S(1)}, u32[]{:S(2)}, u32[]{:S(2)}) collective-permute-start(s32[6,16]{1,0:T(8,128)S(1)} %copy-done.4), channel_id=1, source_target_pairs={{0,0},{1,4},{2,2},{3,6},{4,1},{5,5},{6,3},{7,7},{8,8},{9,12},{10,1... | collective-permute-start | bytes 1160 | tf_op jit(solution)/shard_map/ppermute | solution.py:240
  20.6 6.9 %collective-permute-start.8 = (bf16[4,2,96,768]{3,2,1,0:T(8,128)(2,1)S(1)}, bf16[4,2,96,768]{3,2,1,0:T(8,128)(2,1)S(1)}, u32[]{:S(2)}, u32[]{:S(2)}) collective-permute-start(bf16[4,2,96,768]{3,2,1,0:T(8,128)(2,1)S(1)} %shard_map.87.refs_4_), channel_id=1, source_target_pairs={{0,1},{1,0},{2,3},{3,2},{4,5},{5,4},{6,7},{7,6},{8,9},{9,8},{10,11... | collective-permute-start | bytes 3538952 | tf_op jit(solution)/shard_map/ppermute | solution.py:285
  20.9 18.4 %collective-permute-start.10 = (bf16[4,2,96,768]{3,2,1,0:T(8,128)(2,1)S(1)}, bf16[4,2,96,768]{3,2,1,0:T(8,128)(2,1)S(1)}, u32[]{:S(2)}, u32[]{:S(2)}) collective-permute-start(bf16[4,2,96,768]{3,2,1,0:T(8,128)(2,1)S(1)} %shard_map.87.refs_4_), channel_id=1, source_target_pairs={{0,0},{1,8},{2,2},{3,10},{4,4},{5,12},{6,6},{7,14},{8,1},{9,16},{1... | collective-permute-start | bytes 3538952 | tf_op jit(solution)/shard_map/ppermute | solution.py:288
  21.6 16.2 %collective-permute-start.5 = (bf16[2,96,768]{2,1,0:T(8,128)(2,1)S(1)}, bf16[2,96,768]{2,1,0:T(8,128)(2,1)S(1)}, u32[]{:S(2)}, u32[]{:S(2)}) collective-permute-start(bf16[2,96,768]{2,1,0:T(8,128)(2,1)S(1)} %get-tuple-element.57), channel_id=1, source_target_pairs={{0,6},{1,2},{2,4},{3,0},{4,7},{5,3},{6,5},{7,1},{8,14},{9,10},{10,... | collective-permute-start | bytes 884744 | tf_op jit(solution)/shard_map/ppermute | solution.py:276
  24.4 14.8 %collective-permute-start.6 = (bf16[2,96,768]{2,1,0:T(8,128)(2,1)S(1)}, bf16[2,96,768]{2,1,0:T(8,128)(2,1)S(1)}, u32[]{:S(2)}, u32[]{:S(2)}) collective-permute-start(bf16[2,96,768]{2,1,0:T(8,128)(2,1)S(1)} %get-tuple-element.65), channel_id=1, source_target_pairs={{0,2},{1,6},{2,0},{3,4},{4,3},{5,7},{6,1},{7,5},{8,10},{9,14},{10,... | collective-permute-start | bytes 884744 | tf_op jit(solution)/shard_map/ppermute | solution.py:276
  25.4 13.8 %collective-permute-start.7 = (bf16[2,96,768]{2,1,0:T(8,128)(2,1)S(1)}, bf16[2,96,768]{2,1,0:T(8,128)(2,1)S(1)}, u32[]{:S(2)}, u32[]{:S(2)}) collective-permute-start(bf16[2,96,768]{2,1,0:T(8,128)(2,1)S(1)} %get-tuple-element.66), channel_id=1, source_target_pairs={{0,4},{1,0},{2,6},{3,2},{4,5},{5,1},{6,7},{7,3},{8,12},{9,8},{10,1... | collective-permute-start | bytes 884744 | tf_op jit(solution)/shard_map/ppermute | solution.py:276
  27.5 11.8 %collective-permute-start.9 = (bf16[2,96,768]{2,1,0:T(8,128)(2,1)S(1)}, bf16[2,96,768]{2,1,0:T(8,128)(2,1)S(1)}, u32[]{:S(2)}, u32[]{:S(2)}) collective-permute-start(bf16[2,96,768]{2,1,0:T(8,128)(2,1)S(1)} %get-tuple-element.69), channel_id=1, source_target_pairs={{0,0},{1,4},{2,2},{3,6},{4,1},{5,5},{6,3},{7,7},{8,8},{9,12},{10,1... | collective-permute-start | bytes 884744 | tf_op jit(solution)/shard_map/ppermute | solution.py:276
  49.4 7.2 %collective-permute-start.14 = (bf16[4,2,96,768]{3,2,1,0:T(8,128)(2,1)S(1)}, bf16[4,2,96,768]{3,2,1,0:T(8,128)(2,1)S(1)}, u32[]{:S(2)}, u32[]{:S(2)}) collective-permute-start(bf16[4,2,96,768]{3,2,1,0:T(8,128)(2,1)S(1)} %get-tuple-element.74), channel_id=1, source_target_pairs={{0,1},{1,0},{2,3},{3,2},{4,5},{5,4},{6,7},{7,6},{8,9},{9,8},{10,11... | collective-permute-start | bytes 3538952 | tf_op jit(solution)/shard_map/ppermute | solution.py:285
  50.5 6.8 %collective-permute-start.16 = (bf16[4,2,96,768]{3,2,1,0:T(8,128)(2,1)S(1)}, bf16[4,2,96,768]{3,2,1,0:T(8,128)(2,1)S(1)}, u32[]{:S(2)}, u32[]{:S(2)}) collective-permute-start(bf16[4,2,96,768]{3,2,1,0:T(8,128)(2,1)S(1)} %get-tuple-element.81), channel_id=1, source_target_pairs={{0,0},{1,8},{2,2},{3,10},{4,4},{5,12},{6,6},{7,14},{8,1},{9,16},{1... | collective-permute-start | bytes 3538952 | tf_op jit(solution)/shard_map/ppermute | solution.py:288
  51.3 17.2 %collective-permute-start.11 = (bf16[2,96,768]{2,1,0:T(8,128)(2,1)S(1)}, bf16[2,96,768]{2,1,0:T(8,128)(2,1)S(1)}, u32[]{:S(2)}, u32[]{:S(2)}) collective-permute-start(bf16[2,96,768]{2,1,0:T(8,128)(2,1)S(1)} %get-tuple-element.71), channel_id=1, source_target_pairs={{4,0},{0,1},{6,2},{2,3},{5,4},{1,5},{7,6},{3,7},{12,8},{8,9},{14,1... | collective-permute-start | bytes 884744 | tf_op jit(solution)/shard_map/ppermute | solution.py:281
  54.1 15.3 %collective-permute-start.12 = (bf16[2,96,768]{2,1,0:T(8,128)(2,1)S(1)}, bf16[2,96,768]{2,1,0:T(8,128)(2,1)S(1)}, u32[]{:S(2)}, u32[]{:S(2)}) collective-permute-start(bf16[2,96,768]{2,1,0:T(8,128)(2,1)S(1)} %get-tuple-element.72), channel_id=1, source_target_pairs={{2,0},{6,1},{0,2},{4,3},{3,4},{7,5},{1,6},{5,7},{10,8},{14,9},{8,1... | collective-permute-start | bytes 884744 | tf_op jit(solution)/shard_map/ppermute | solution.py:281
  55.1 16.2 %collective-permute-start.13 = (bf16[2,96,768]{2,1,0:T(8,128)(2,1)S(1)}, bf16[2,96,768]{2,1,0:T(8,128)(2,1)S(1)}, u32[]{:S(2)}, u32[]{:S(2)}) collective-permute-start(bf16[2,96,768]{2,1,0:T(8,128)(2,1)S(1)} %get-tuple-element.73), channel_id=1, source_target_pairs={{6,0},{2,1},{4,2},{0,3},{7,4},{3,5},{5,6},{1,7},{14,8},{10,9},{12,... | collective-permute-start | bytes 884744 | tf_op jit(solution)/shard_map/ppermute | solution.py:281
  56.6 15.3 %collective-permute-start.15 = (bf16[2,96,768]{2,1,0:T(8,128)(2,1)S(1)}, bf16[2,96,768]{2,1,0:T(8,128)(2,1)S(1)}, u32[]{:S(2)}, u32[]{:S(2)}) collective-permute-start(bf16[2,96,768]{2,1,0:T(8,128)(2,1)S(1)} %get-tuple-element.76), channel_id=1, source_target_pairs={{0,0},{4,1},{2,2},{6,3},{1,4},{5,5},{3,6},{7,7},{8,8},{12,9},{10,1... | collective-permute-start | bytes 884744 | tf_op jit(solution)/shard_map/ppermute | solution.py:281
  57.7 15.3 %collective-permute-start.17 = (bf16[2,96,768]{2,1,0:T(8,128)(2,1)S(1)}, bf16[2,96,768]{2,1,0:T(8,128)(2,1)S(1)}, u32[]{:S(2)}, u32[]{:S(2)}) collective-permute-start(bf16[2,96,768]{2,1,0:T(8,128)(2,1)S(1)} %get-tuple-element.82), channel_id=1, source_target_pairs={{4,0},{0,1},{6,2},{2,3},{5,4},{1,5},{7,6},{3,7},{12,8},{8,9},{14,1... | collective-permute-start | bytes 884744 | tf_op jit(solution)/shard_map/ppermute | solution.py:281
  68.5 13.0 %collective-permute-start.18 = (bf16[2,96,768]{2,1,0:T(8,128)(2,1)S(1)}, bf16[2,96,768]{2,1,0:T(8,128)(2,1)S(1)}, u32[]{:S(2)}, u32[]{:S(2)}) collective-permute-start(bf16[2,96,768]{2,1,0:T(8,128)(2,1)S(1)} %get-tuple-element.83), channel_id=1, source_target_pairs={{2,0},{6,1},{0,2},{4,3},{3,4},{7,5},{1,6},{5,7},{10,8},{14,9},{8,1... | collective-permute-start | bytes 884744 | tf_op jit(solution)/shard_map/ppermute | solution.py:281
  69.4 13.7 %collective-permute-start.19 = (bf16[2,96,768]{2,1,0:T(8,128)(2,1)S(1)}, bf16[2,96,768]{2,1,0:T(8,128)(2,1)S(1)}, u32[]{:S(2)}, u32[]{:S(2)}) collective-permute-start(bf16[2,96,768]{2,1,0:T(8,128)(2,1)S(1)} %get-tuple-element.84), channel_id=1, source_target_pairs={{6,0},{2,1},{4,2},{0,3},{7,4},{3,5},{5,6},{1,7},{14,8},{10,9},{12,... | collective-permute-start | bytes 884744 | tf_op jit(solution)/shard_map/ppermute | solution.py:281
  71.3 11.9 %collective-permute-start.20 = (bf16[2,96,768]{2,1,0:T(8,128)(2,1)S(1)}, bf16[2,96,768]{2,1,0:T(8,128)(2,1)S(1)}, u32[]{:S(2)}, u32[]{:S(2)}) collective-permute-start(bf16[2,96,768]{2,1,0:T(8,128)(2,1)S(1)} %get-tuple-element.85), channel_id=1, source_target_pairs={{0,0},{4,1},{2,2},{6,3},{1,4},{5,5},{3,6},{7,7},{8,8},{12,9},{10,1... | collective-permute-start | bytes 884744 | tf_op jit(solution)/shard_map/ppermute | solution.py:281
  (2 other events, 2.1 us)
